TPU v7x, 32 devices: a whole 2x2x4 slice. The times are simulated.
32 devices in a mesh: head: 4 (over y, x), blk: 8 (over z, core).
Axes of the slice: x: 2, y: 2, z: 4, core: 2. Of those that a mesh axis runs over, the one named last changes fastest.
Arguments:
- query: bfloat16 [4096, 2048], P(('blk', 'head')), may hold values from -8 to 8
- key_in: bfloat16 [4096, 2048], P(('blk', 'head')), may hold values from -8 to 8
- value: bfloat16 [4096, 2048], P(('blk', 'head')), may hold values from -6 to 6
- grad_out: bfloat16 [4096, 2048], P(('blk', 'head')), may hold values from -96 to 96
Outputs:
- grad_query: bfloat16 [4096, 2048], P(('blk', 'head'))
- grad_key: bfloat16 [4096, 2048], P(('blk', 'head'))
- grad_value: bfloat16 [4096, 2048], P(('blk', 'head'))
All inputs are finite; a program needn't handle non-finite values.
Results may differ from a plain program's by a relative error of at most 0.0052.
Values may be sent and summed in bfloat16 or wider, within the bound.
No kernel may reach another device: no remote copies, remote signals or barrier semaphores. Data moves between devices by JAX's collectives and lax.ppermute only.
A program may use at most 64 MiB of HBM per device.

v0:
```python
import jax
import jax.numpy as jnp
from jax import lax
from jax.sharding import PartitionSpec as P

HEADS = 16
HEAD_DIM = 128
HALF = 512
TILE = 512


def with_halo(cells, sides, width):
    for axis, dim in sides:
        count = lax.axis_size(axis)
        ends = count - 1
        head = lax.slice_in_dim(cells, 0, width, axis=dim)
        tail = lax.slice_in_dim(cells, cells.shape[dim] - width, cells.shape[dim], axis=dim)
        cells = jnp.concatenate(
            [
                lax.ppermute(tail, axis, [(i, (i + 1) % count) for i in range(ends)]),
                cells,
                lax.ppermute(head, axis, [((i + 1) % count, i) for i in range(ends)]),
            ],
            axis=dim,
        )
    return cells


def from_behind(array, axis, by):
    devices = lax.axis_size(axis)
    pairs = [(i, i + by) for i in range(devices) if 0 <= i + by < devices]
    return lax.ppermute(array, axis, pairs)


def masked_scores(query_part, key_part, query_first, key_first, seq_total, score_scale):
    raw = (
        jnp.einsum("qhd,khd->hqk", query_part, key_part, preferred_element_type=jnp.float32)
        * score_scale
    )
    query_pos = query_first + jnp.arange(query_part.shape[0], dtype=jnp.int32)
    key_pos = key_first + jnp.arange(key_part.shape[0], dtype=jnp.int32)
    within = jnp.abs(query_pos[:, None] - key_pos[None, :]) <= HALF
    query_ok = (query_pos >= 0) & (query_pos < seq_total)
    key_ok = (key_pos >= 0) & (key_pos < seq_total)
    allowed = within & query_ok[:, None] & key_ok[None, :]
    return jnp.where(allowed[None], raw, -1e30)


def forward_stats(scores, grad_part, value_part):
    row_max = jnp.max(scores, axis=-1)
    shifted = jnp.exp(scores - row_max[..., None])
    denominator = jnp.sum(shifted, axis=-1)
    weighted = jnp.einsum(
        "hqk,khd->hqd", shifted.astype(jnp.bfloat16), value_part, preferred_element_type=jnp.float32
    )
    output_rows = weighted / denominator[..., None]
    log_total = row_max + jnp.log(denominator)
    grad_float = jnp.transpose(grad_part.astype(jnp.float32), (1, 0, 2))
    row_delta = jnp.sum(grad_float * output_rows, axis=-1)
    return (log_total, row_delta)


def grad_parts(scores, log_total, row_delta, grad_part, value_part):
    weights = jnp.exp(scores - log_total[..., None])
    grad_weights = jnp.einsum(
        "qhd,khd->hqk", grad_part, value_part, preferred_element_type=jnp.float32
    )
    grad_scores = weights * (grad_weights - row_delta[..., None])
    return (weights.astype(jnp.bfloat16), grad_scores.astype(jnp.bfloat16))


def shards(query, key_in, value, grad_out):
    heads_dev = HEADS // lax.axis_size("head")
    score_scale = HEAD_DIM ** (-0.5)
    query_t, key_t, value_t, grad_t = (
        lax.all_to_all(query, "head", split_axis=1, concat_axis=0, tiled=True),
        lax.all_to_all(key_in, "head", split_axis=1, concat_axis=0, tiled=True),
        lax.all_to_all(value, "head", split_axis=1, concat_axis=0, tiled=True),
        lax.all_to_all(grad_out, "head", split_axis=1, concat_axis=0, tiled=True),
    )
    row_count = query_t.shape[0]
    feat_width = heads_dev * HEAD_DIM
    seq_total = row_count * lax.axis_size("blk")
    block_base = lax.axis_index("blk") * row_count
    key_span = TILE + 2 * HALF
    tile_count = row_count // TILE
    tile_ids = jnp.arange(tile_count, dtype=jnp.int32)

    def split_heads(matrix):
        return matrix.reshape(matrix.shape[0], heads_dev, HEAD_DIM)

    query_h = split_heads(query_t)
    grad_h = split_heads(grad_t)
    key_pair = jnp.concatenate([key_t, value_t], axis=1)
    pair_ext = with_halo(key_pair, (("blk", 0),), HALF)
    key_ext = split_heads(pair_ext[:, :feat_width])
    value_ext = split_heads(pair_ext[:, feat_width:])

    def tile_step(running, tile_index):
        key_acc, value_acc = running
        offset = tile_index * TILE
        query_part = lax.dynamic_slice_in_dim(query_h, offset, TILE, 0)
        grad_part = lax.dynamic_slice_in_dim(grad_h, offset, TILE, 0)
        key_part = lax.dynamic_slice_in_dim(key_ext, offset, key_span, 0)
        value_part = lax.dynamic_slice_in_dim(value_ext, offset, key_span, 0)
        scores = masked_scores(
            query_part,
            key_part,
            block_base + offset,
            block_base - HALF + offset,
            seq_total,
            score_scale,
        )
        log_total, row_delta = forward_stats(scores, grad_part, value_part)
        weights_low, scores_low = grad_parts(scores, log_total, row_delta, grad_part, value_part)
        add_value = jnp.einsum(
            "hqk,qhd->khd", weights_low, grad_part, preferred_element_type=jnp.float32
        )
        add_key = (
            jnp.einsum("hqk,qhd->khd", scores_low, query_part, preferred_element_type=jnp.float32)
            * score_scale
        )
        add_query = (
            jnp.einsum("hqk,khd->qhd", scores_low, key_part, preferred_element_type=jnp.float32)
            * score_scale
        )
        old_key = lax.dynamic_slice_in_dim(key_acc, offset, key_span, 0)
        old_value = lax.dynamic_slice_in_dim(value_acc, offset, key_span, 0)
        key_acc = lax.dynamic_update_slice_in_dim(key_acc, old_key + add_key, offset, 0)
        value_acc = lax.dynamic_update_slice_in_dim(value_acc, old_value + add_value, offset, 0)
        return ((key_acc, value_acc), (add_query, log_total, row_delta))

    zeros_ext = jnp.zeros((row_count + 2 * HALF, heads_dev, HEAD_DIM), jnp.float32)
    (key_acc, value_acc), (query_tiles, total_tiles, delta_tiles) = lax.scan(
        tile_step, (zeros_ext, zeros_ext), tile_ids
    )
    query_sum = query_tiles.reshape(row_count, heads_dev, HEAD_DIM)
    key_sum = key_acc[HALF : HALF + row_count]
    value_sum = value_acc[HALF : HALF + row_count]
    down_key, down_value = from_behind((key_acc[:HALF], value_acc[:HALF]), "blk", -1)
    up_key, up_value = from_behind(
        (key_acc[HALF + row_count :], value_acc[HALF + row_count :]), "blk", 1
    )
    key_sum = key_sum.at[row_count - HALF :].add(down_key).at[:HALF].add(up_key)
    value_sum = value_sum.at[row_count - HALF :].add(down_value).at[:HALF].add(up_value)

    def merge_heads(stacked):
        return stacked.reshape(row_count, feat_width).astype(jnp.bfloat16)

    grad_query, grad_key, grad_value = (
        lax.all_to_all(merge_heads(query_sum), "head", split_axis=0, concat_axis=1, tiled=True),
        lax.all_to_all(merge_heads(key_sum), "head", split_axis=0, concat_axis=1, tiled=True),
        lax.all_to_all(merge_heads(value_sum), "head", split_axis=0, concat_axis=1, tiled=True),
    )
    return (grad_query, grad_key, grad_value)


def solution(mesh):
    placed = (
        P(("blk", "head"), None),
        P(("blk", "head"), None),
        P(("blk", "head"), None),
        P(("blk", "head"), None),
    )
    return jax.shard_map(
        shards,
        mesh=mesh,
        in_specs=placed,
        out_specs=(P(("blk", "head"), None), P(("blk", "head"), None), P(("blk", "head"), None)),
        check_vma=False,
    )
```

profile of v0, /device:TPU:0, one launch (start us, length us, event | category | flops | bytes accessed | tf_op | source)
XLA Modules:
  0.0 146.8 jit_solution(15438371323978473748)
XLA Ops:
  0.6 2.1 %copy.55 = bf16[128,2048]{0,1:T(8,128)(2,1)} copy(bf16[128,2048]{1,0:T(8,128)(2,1)} %param.22) | data formatting | bytes 1048576 | tf_op args[2]
  2.7 5.2 %all-to-all-start.1 = ((bf16[128,4,512]{0,2,1:T(8,128)(2,1)}), bf16[128,4,512]{0,2,1:T(8,128)(2,1)S(1)}, u32[]{:S(2)}, u32[]{:S(2)}) async-start(bf16[128,4,512]{0,2,1:T(8,128)(2,1)} %bitcast.3), calls=%async_computation.1 | async-start | bytes 1048576 | tf_op jit(solution)/shard_map/all_to_all | solution.py:78
  7.9 2.0 %copy.53 = bf16[128,2048]{0,1:T(8,128)(2,1)} copy(bf16[128,2048]{1,0:T(8,128)(2,1)} %param.21) | data formatting | bytes 1048576 | tf_op args[1]
  9.9 6.0 %all-to-all-done.1 = bf16[128,4,512]{0,2,1:T(8,128)(2,1)S(1)} async-done(((bf16[128,4,512]{0,2,1:T(8,128)(2,1)}), bf16[128,4,512]{0,2,1:T(8,128)(2,1)S(1)}, u32[]{:S(2)}, u32[]{:S(2)}) %all-to-all-start.1) | async-done | bytes 524320 | tf_op jit(solution)/shard_map/all_to_all | solution.py:78
  15.9 3.5 %all-to-all-start = ((bf16[128,4,512]{0,2,1:T(8,128)(2,1)}), bf16[128,4,512]{0,2,1:T(8,128)(2,1)S(1)}, u32[]{:S(2)}, u32[]{:S(2)}) async-start(bf16[128,4,512]{0,2,1:T(8,128)(2,1)} %bitcast), calls=%async_computation | async-start | bytes 1048576 | tf_op jit(solution)/shard_map/all_to_all | solution.py:77
  19.4 0.2 copy.56
  19.6 6.9 %all-to-all-done = bf16[128,4,512]{0,2,1:T(8,128)(2,1)S(1)} async-done(((bf16[128,4,512]{0,2,1:T(8,128)(2,1)}), bf16[128,4,512]{0,2,1:T(8,128)(2,1)S(1)}, u32[]{:S(2)}, u32[]{:S(2)}) %all-to-all-start) | async-done | bytes 524320 | tf_op jit(solution)/shard_map/all_to_all | solution.py:77
  26.5 0.2 copy.54
  26.7 0.1 pad_maximum_fusion.1
  26.9 1.3 collective-permute-start.1
  28.2 4.0 %collective-permute-start = (bf16[512,1024]{1,0:T(8,128)(2,1)S(1)}, bf16[512,1024]{1,0:T(8,128)(2,1)}, u32[]{:S(2)}, u32[]{:S(2)}) collective-permute-start(bf16[512,1024]{1,0:T(8,128)(2,1)S(1)} %pad_maximum_fusion.1), channel_id=1, source_target_pairs={{0,1},{1,2},{2,3},{3,4},{4,5},{5,6},{6,7},{8,9},{9,10},{10,11},{11... | collective-permute-start | bytes 3145736 | tf_op jit(solution)/shard_map/ppermute | solution.py:20
  32.2 0.8 copy.93
  33.0 3.5 %all-to-all-start.2 = ((bf16[128,4,512]{2,0,1:T(8,128)(2,1)}), bf16[128,4,512]{2,0,1:T(8,128)(2,1)S(1)}, u32[]{:S(2)}, u32[]{:S(2)}) async-start(bf16[128,4,512]{2,0,1:T(8,128)(2,1)} %bitcast.48), calls=%async_computation.2 | async-start | bytes 1048576 | tf_op jit(solution)/shard_map/all_to_all | solution.py:76
  36.5 1.9 %copy.92 = bf16[16,4,8,512]{3,2,0,1:T(8,128)(2,1)} copy(bf16[16,4,8,512]{3,2,1,0:T(8,128)(2,1)} %bitcast.66) | data formatting | bytes 1048576 | tf_op jit(solution)/shard_map/all_to_all | solution.py:79
  38.5 6.7 %all-to-all-done.2 = bf16[128,4,512]{2,0,1:T(8,128)(2,1)S(1)} async-done(((bf16[128,4,512]{2,0,1:T(8,128)(2,1)}), bf16[128,4,512]{2,0,1:T(8,128)(2,1)S(1)}, u32[]{:S(2)}, u32[]{:S(2)}) %all-to-all-start.2) | async-done | bytes 524320 | tf_op jit(solution)/shard_map/all_to_all | solution.py:76
  45.2 3.5 %all-to-all-start.3 = ((bf16[128,4,512]{2,0,1:T(8,128)(2,1)}), bf16[128,4,512]{2,0,1:T(8,128)(2,1)S(1)}, u32[]{:S(2)}, u32[]{:S(2)}) async-start(bf16[128,4,512]{2,0,1:T(8,128)(2,1)} %bitcast.47), calls=%async_computation.3 | async-start | bytes 1048576 | tf_op jit(solution)/shard_map/all_to_all | solution.py:79
  48.7 2.1 %fusion.15 = pred[512,1536]{0,1:T(8,128)(4,1)} fusion(s32[1536]{0:T(1024)S(1)} %iota_add_fusion, s32[512]{0:T(512)S(1)} %iota_add_fusion.1, pred[1536]{0:T(1024)(128)(4,1)S(1)} %compare_and_fusion, pred[512]{0:T(512)(128)(4,1)S(1)} %compare_and_fusion.1), kind=kLoop, calls=%fused_computation.18 | loop fusion | flops 3932160 | bytes 796672 | tf_op jit(solution)/shard_map/while/body/eval_jaxpr/and | solution.py:45
  50.8 0.9 reshape.263
  51.7 4.8 %all-to-all-done.3 = bf16[128,4,512]{2,0,1:T(8,128)(2,1)S(1)} async-done(((bf16[128,4,512]{2,0,1:T(8,128)(2,1)}), bf16[128,4,512]{2,0,1:T(8,128)(2,1)S(1)}, u32[]{:S(2)}, u32[]{:S(2)}) %all-to-all-start.3) | async-done | bytes 524320 | tf_op jit(solution)/shard_map/all_to_all | solution.py:79
  56.5 0.1 reshape.265
  56.7 1.1 copy.65
  57.8 0.0 collective-permute-done.1
  57.8 0.0 collective-permute-done
  57.8 1.8 %pad_maximum_fusion = bf16[1536,1024]{1,0:T(8,128)(2,1)S(1)} fusion(bf16[512,1024]{1,0:T(8,128)(2,1)} %collective-permute-done.1, bf16[512,512]{1,0:T(8,128)(2,1)S(1)} %bitcast.54, bf16[512,512]{1,0:T(8,128)(2,1)S(1)} %bitcast.56, bf16[512,1024]{1,0:T(8,128)(2,1)} %collective-permute-done), kind=kLoop, calls=%fused_computation.15 | loop fusion | flops 12582912 | bytes 6291456 | tf_op jit(solution)/shard_map/concatenate | solution.py:18
  59.6 1.4 fusion.35
  61.0 0.7 copy.57
  61.7 2.3 %copy.61 = bf16[1536,512]{0,1:T(8,128)(2,1)S(1)} copy(bf16[1536,512]{1,0:T(8,128)(2,1)} %get-tuple-element.120) | data formatting | bytes 3145728 | tf_op jit(solution)/shard_map/slice | solution.py:97
  64.0 4.5 %fusion.36 = (f32[4,512]{1,0:T(4,128)S(1)}, f32[4,512,1536]{1,2,0:T(8,128)S(1)}) fusion(bf16[1536,4,128]{0,2,1:T(8,128)(2,1)S(1)} %bitcast.49, bf16[512,4,128]{2,1,0:T(4,128)(2,1)} %reshape.263, pred[512,1536]{0,1:T(8,128)(4,1)} %fusion.15), kind=kOutput, calls=%fused_computation.44 | convolution fusion | flops 814741504 | bytes 15474688 | tf_op jit(solution)/shard_map/while/body/eval_jaxpr/qhd,khd->hqk/dot_general | solution.py:37
  68.5 0.0 copy-start.3
  68.5 1.7 %fusion.2 = f32[4,512]{1,0:T(4,128)S(1)} fusion(f32[4,512,1536]{1,2,0:T(8,128)S(1)} %get-tuple-element.123, f32[4,512]{1,0:T(4,128)S(1)} %get-tuple-element.122), kind=kLoop, calls=%fused_computation.6 | loop fusion | flops 6289408 | bytes 12599296 | tf_op jit(solution)/shard_map/while/body/eval_jaxpr/reduce_sum | solution.py:52
  70.2 2.4 %fusion.24 = f32[4,512]{1,0:T(4,128)S(1)} fusion(bf16[1536,4,128]{0,2,1:T(8,128)(2,1)S(1)} %bitcast.51, f32[4,512,1536]{1,2,0:T(8,128)S(1)} %get-tuple-element.123, f32[4,512]{1,0:T(4,128)S(1)} %get-tuple-element.122, bf16[512,4,128]{0,2,1:T(8,128)(2,1)S(1)} %copy-done.3, f32[4,512]{1,0:T(4,128)S(1)} %fusion.2), kind=kOutput, calls=%fused_computation.24 | convolution fusion | flops 812644352 | bytes 14704640 | tf_op jit(solution)/shard_map/while/body/eval_jaxpr/hqk,khd->hqd/dot_general | solution.py:53
  72.6 0.0 copy-start.4
  72.6 4.9 %fusion = bf16[4,512,1536]{1,2,0:T(8,128)(2,1)} fusion(f32[4,512,1536]{1,2,0:T(8,128)S(1)} %get-tuple-element.123, bf16[1536,4,128]{0,2,1:T(8,128)(2,1)S(1)} %bitcast.52, bf16[512,4,128]{0,2,1:T(8,128)(2,1)S(1)} %copy-done.3, f32[4,512]{1,0:T(4,128)S(1)} %fusion.24, f32[4,512]{1,0:T(4,128)S(1)} %log_add_fusion), kind=kOutput, calls=%fused_computation.1 | convolution fusion | flops 817889280 | bytes 20987904 | tf_op jit(solution)/shard_map/while/body/eval_jaxpr/qhd,khd->hqk/dot_general | solution.py:65
  77.5 4.6 %fusion.10 = f32[1536,4,128]{2,0,1:T(8,128)S(1)} fusion(bf16[4,512,1536]{1,2,0:T(8,128)(2,1)} %fusion, bf16[512,4,128]{2,1,0:T(4,128)(2,1)S(1)} %copy-done.4), kind=kOutput, calls=%fused_computation.13 | convolution fusion | flops 806092800 | bytes 9961472 | tf_op jit(solution)/shard_map/while/body/eval_jaxpr/hqk,qhd->khd/dot_general | solution.py:120
  82.1 1.6 %fusion.34 = (f32[512,4,128]{2,0,1:T(8,128)}, f32[512,4,128]{2,0,1:T(8,128)}) fusion(f32[1536,4,128]{2,0,1:T(8,128)S(1)} %fusion.10), kind=kLoop, calls=%fused_computation.42 | loop fusion | bytes 4194304 | tf_op jit(solution)/shard_map/slice | solution.py:140
  83.7 2.3 %collective-permute-start.3 = (f32[512,4,128]{2,0,1:T(8,128)}, f32[512,4,128]{2,0,1:T(8,128)}, u32[]{:S(2)}, u32[]{:S(2)}) collective-permute-start(f32[512,4,128]{2,0,1:T(8,128)} %get-tuple-element.119), channel_id=1, source_target_pairs={{0,1},{1,2},{2,3},{3,4},{4,5},{5,6},{6,7},{8,9},{9,10},{10,11},{11... | collective-permute-start | bytes 3145736 | tf_op jit(solution)/shard_map/ppermute | solution.py:32
  85.9 1.6 %collective-permute-start.2 = (f32[512,4,128]{2,0,1:T(8,128)}, f32[512,4,128]{2,0,1:T(8,128)}, u32[]{:S(2)}, u32[]{:S(2)}) collective-permute-start(f32[512,4,128]{2,0,1:T(8,128)} %get-tuple-element.118), channel_id=1, source_target_pairs={{1,0},{2,1},{3,2},{4,3},{5,4},{6,5},{7,6},{9,8},{10,9},{11,10},{12... | collective-permute-start | bytes 3145736 | tf_op jit(solution)/shard_map/ppermute | solution.py:32
  87.5 3.0 %fusion.11 = f32[1536,4,128]{2,0,1:T(8,128)S(1)} fusion(bf16[512,4,128]{0,2,1:T(8,128)(2,1)} %copy.65, f32[4,512,1536]{1,2,0:T(8,128)S(1)} %get-tuple-element.123, f32[4,512]{1,0:T(4,128)S(1)} %log_add_fusion), kind=kOutput, calls=%fused_computation.14 | convolution fusion | flops 811597824 | bytes 16261120 | tf_op jit(solution)/shard_map/while/body/eval_jaxpr/hqk,qhd->khd/dot_general | solution.py:116
  90.5 1.7 %copy-done.2 = f32[1536,4,128]{2,0,1:T(8,128)} copy-done((f32[1536,4,128]{2,0,1:T(8,128)}, f32[1536,4,128]{2,0,1:T(8,128)S(1)}, u32[]{:S(2)}) %copy-start.2) | copy-done | bytes 3145752
  92.2 1.5 %fusion.33 = (f32[512,4,128]{2,0,1:T(8,128)}, f32[512,4,128]{2,0,1:T(8,128)}) fusion(f32[1536,4,128]{2,0,1:T(8,128)S(1)} %fusion.11), kind=kLoop, calls=%fused_computation.41 | loop fusion | bytes 4194304 | tf_op jit(solution)/shard_map/slice | solution.py:140
  93.7 5.4 %collective-permute-start.5 = (f32[512,4,128]{2,0,1:T(8,128)}, f32[512,4,128]{2,0,1:T(8,128)}, u32[]{:S(2)}, u32[]{:S(2)}) collective-permute-start(f32[512,4,128]{2,0,1:T(8,128)} %get-tuple-element.117), channel_id=1, source_target_pairs={{0,1},{1,2},{2,3},{3,4},{4,5},{5,6},{6,7},{8,9},{9,10},{10,11},{11... | collective-permute-start | bytes 3145736 | tf_op jit(solution)/shard_map/ppermute | solution.py:32
  99.2 1.3 collective-permute-start.4
  100.5 4.6 %fusion.17 = bf16[512,4,128]{0,2,1:T(8,128)(2,1)} fusion(bf16[1536,4,128]{0,2,1:T(8,128)(2,1)S(1)} %bitcast.50, bf16[4,512,1536]{1,2,0:T(8,128)(2,1)} %fusion), kind=kOutput, calls=%fused_computation.21 | convolution fusion | flops 805830656 | bytes 8388608 | tf_op jit(solution)/shard_map/while/body/eval_jaxpr/hqk,khd->qhd/dot_general | solution.py:124
  105.0 2.0 %convert_element_type.42 = bf16[4,128,512]{1,0,2:T(4,128)(2,1)} reshape(bf16[512,4,128]{0,2,1:T(8,128)(2,1)} %fusion.17) | data formatting | bytes 1048576 | tf_op jit(solution)/shard_map/convert_element_type | solution.py:148
  107.0 1.9 %copy.68 = bf16[4,128,512]{1,2,0:T(8,128)(2,1)} copy(bf16[4,128,512]{1,0,2:T(4,128)(2,1)} %convert_element_type.42) | data formatting | bytes 1048576 | tf_op jit(solution)/shard_map/convert_element_type | solution.py:148
  108.9 4.1 %all-to-all-start.4 = ((bf16[4,128,512]{1,2,0:T(8,128)(2,1)}), bf16[4,128,512]{1,2,0:T(8,128)(2,1)}, u32[]{:S(2)}, u32[]{:S(2)}) async-start(bf16[4,128,512]{1,2,0:T(8,128)(2,1)} %copy.68), calls=%async_computation.4 | async-start | bytes 1048576 | tf_op jit(solution)/shard_map/all_to_all | solution.py:151
  113.1 0.0 collective-permute-done.3
  113.1 0.0 collective-permute-done.2
  113.1 1.7 %fusion.30 = bf16[512,4,128]{2,0,1:T(8,128)(2,1)S(1)} fusion(f32[512,4,128]{2,0,1:T(8,128)} %collective-permute-done.3, f32[512,4,128]{2,0,1:T(8,128)} %collective-permute-done.2, f32[1536,4,128]{2,0,1:T(8,128)S(1)} %fusion.10), kind=kLoop, calls=%fused_computation.30 | loop fusion | flops 786432 | bytes 3670016 | tf_op jit(solution)/shard_map/convert_element_type | solution.py:148
  114.8 0.4 copy.70
  115.2 1.0 convert_element_type.44
  116.2 6.0 %all-to-all-done.4 = bf16[4,128,512]{1,2,0:T(8,128)(2,1)} async-done(((bf16[4,128,512]{1,2,0:T(8,128)(2,1)}), bf16[4,128,512]{1,2,0:T(8,128)(2,1)}, u32[]{:S(2)}, u32[]{:S(2)}) %all-to-all-start.4) | async-done | bytes 524320 | tf_op jit(solution)/shard_map/all_to_all | solution.py:151
  122.2 3.5 %all-to-all-start.5 = ((bf16[4,128,512]{2,1,0:T(8,128)(2,1)}), bf16[4,128,512]{2,1,0:T(8,128)(2,1)S(1)}, u32[]{:S(2)}, u32[]{:S(2)}) async-start(bf16[4,128,512]{2,1,0:T(8,128)(2,1)} %convert_element_type.44), calls=%async_computation.5 | async-start | bytes 1048576 | tf_op jit(solution)/shard_map/all_to_all | solution.py:152
  125.7 2.0 %fusion.28 = bf16[512,4,128]{2,0,1:T(8,128)(2,1)S(1)} fusion(f32[512,4,128]{2,0,1:T(8,128)} %collective-permute-done.5, f32[512,4,128]{2,0,1:T(8,128)} %collective-permute-done.4, f32[1536,4,128]{2,0,1:T(8,128)} %copy-done.2), kind=kLoop, calls=%fused_computation.27 | loop fusion | flops 786432 | bytes 3670016 | tf_op jit(solution)/shard_map/convert_element_type | solution.py:148
  127.7 0.4 copy.73
  128.1 1.0 convert_element_type.47
  129.1 5.2 %all-to-all-done.5 = bf16[4,128,512]{2,1,0:T(8,128)(2,1)S(1)} async-done(((bf16[4,128,512]{2,1,0:T(8,128)(2,1)}), bf16[4,128,512]{2,1,0:T(8,128)(2,1)S(1)}, u32[]{:S(2)}, u32[]{:S(2)}) %all-to-all-start.5) | async-done | bytes 524320 | tf_op jit(solution)/shard_map/all_to_all | solution.py:152
  134.3 3.5 %all-to-all-start.6 = ((bf16[4,128,512]{2,1,0:T(8,128)(2,1)}), bf16[4,128,512]{2,1,0:T(8,128)(2,1)S(1)}, u32[]{:S(2)}, u32[]{:S(2)}) async-start(bf16[4,128,512]{2,1,0:T(8,128)(2,1)} %convert_element_type.47), calls=%async_computation.6 | async-start | bytes 1048576 | tf_op jit(solution)/shard_map/all_to_all | solution.py:153
  137.8 2.0 %copy.75 = bf16[128,2048]{1,0:T(8,128)(2,1)} copy(bf16[128,2048]{0,1:T(8,128)(2,1)} %bitcast.15) | data formatting | bytes 1048576
  139.8 0.3 copy.71
  140.1 1.0 copy.76
  141.1 4.4 %all-to-all-done.6 = bf16[4,128,512]{2,1,0:T(8,128)(2,1)S(1)} async-done(((bf16[4,128,512]{2,1,0:T(8,128)(2,1)}), bf16[4,128,512]{2,1,0:T(8,128)(2,1)S(1)}, u32[]{:S(2)}, u32[]{:S(2)}) %all-to-all-start.6) | async-done | bytes 524320 | tf_op jit(solution)/shard_map/all_to_all | solution.py:153
  145.5 0.3 copy.74
  145.8 1.0 copy.77
  (16 shorter events, 0.1 us)
Async XLA Ops:
  0.6 31.6 %copy-start.5 = (bf16[128,2048]{1,0:T(8,128)(2,1)S(1)}, bf16[128,2048]{1,0:T(8,128)(2,1)}, u32[]{:S(2)}) copy-start(bf16[128,2048]{1,0:T(8,128)(2,1)} %param.20) | copy-start | bytes 1572868
  2.7 13.2 %all-to-all-start.1 = ((bf16[128,4,512]{0,2,1:T(8,128)(2,1)}), bf16[128,4,512]{0,2,1:T(8,128)(2,1)S(1)}, u32[]{:S(2)}, u32[]{:S(2)}) async-start(bf16[128,4,512]{0,2,1:T(8,128)(2,1)} %bitcast.3), calls=%async_computation.1 | async-start | bytes 1048576 | tf_op jit(solution)/shard_map/all_to_all | solution.py:78
  15.9 10.6 %all-to-all-start = ((bf16[128,4,512]{0,2,1:T(8,128)(2,1)}), bf16[128,4,512]{0,2,1:T(8,128)(2,1)S(1)}, u32[]{:S(2)}, u32[]{:S(2)}) async-start(bf16[128,4,512]{0,2,1:T(8,128)(2,1)} %bitcast), calls=%async_computation | async-start | bytes 1048576 | tf_op jit(solution)/shard_map/all_to_all | solution.py:77
  26.9 30.9 %collective-permute-start.1 = (bf16[512,1024]{1,0:T(8,128)(2,1)S(1)}, bf16[512,1024]{1,0:T(8,128)(2,1)}, u32[]{:S(2)}, u32[]{:S(2)}) collective-permute-start(bf16[512,1024]{1,0:T(8,128)(2,1)S(1)} %pad_maximum_fusion.1), channel_id=1, source_target_pairs={{1,0},{2,1},{3,2},{4,3},{5,4},{6,5},{7,6},{9,8},{10,9},{11,10},{12... | collective-permute-start | bytes 3145736 | tf_op jit(solution)/shard_map/ppermute | solution.py:22
  28.2 29.6 %collective-permute-start = (bf16[512,1024]{1,0:T(8,128)(2,1)S(1)}, bf16[512,1024]{1,0:T(8,128)(2,1)}, u32[]{:S(2)}, u32[]{:S(2)}) collective-permute-start(bf16[512,1024]{1,0:T(8,128)(2,1)S(1)} %pad_maximum_fusion.1), channel_id=1, source_target_pairs={{0,1},{1,2},{2,3},{3,4},{4,5},{5,6},{6,7},{8,9},{9,10},{10,11},{11... | collective-permute-start | bytes 3145736 | tf_op jit(solution)/shard_map/ppermute | solution.py:20
  33.0 12.2 %all-to-all-start.2 = ((bf16[128,4,512]{2,0,1:T(8,128)(2,1)}), bf16[128,4,512]{2,0,1:T(8,128)(2,1)S(1)}, u32[]{:S(2)}, u32[]{:S(2)}) async-start(bf16[128,4,512]{2,0,1:T(8,128)(2,1)} %bitcast.48), calls=%async_computation.2 | async-start | bytes 1048576 | tf_op jit(solution)/shard_map/all_to_all | solution.py:76
  45.2 11.3 %all-to-all-start.3 = ((bf16[128,4,512]{2,0,1:T(8,128)(2,1)}), bf16[128,4,512]{2,0,1:T(8,128)(2,1)S(1)}, u32[]{:S(2)}, u32[]{:S(2)}) async-start(bf16[128,4,512]{2,0,1:T(8,128)(2,1)} %bitcast.47), calls=%async_computation.3 | async-start | bytes 1048576 | tf_op jit(solution)/shard_map/all_to_all | solution.py:79
  61.7 6.8 %copy-start = (bf16[1536,512]{0,1:T(8,128)(2,1)}, bf16[1536,512]{0,1:T(8,128)(2,1)S(1)}, u32[]{:S(2)}) copy-start(bf16[1536,512]{0,1:T(8,128)(2,1)S(1)} %copy.57) | copy-start | bytes 4718596
  68.5 1.7 %copy-start.3 = (bf16[512,4,128]{0,2,1:T(8,128)(2,1)S(1)}, bf16[512,4,128]{0,2,1:T(8,128)(2,1)}, u32[]{:S(2)}) copy-start(bf16[512,4,128]{0,2,1:T(8,128)(2,1)} %copy.65) | copy-start | bytes 1572868
  72.6 4.9 %copy-start.4 = (bf16[512,4,128]{2,1,0:T(4,128)(2,1)S(1)}, bf16[512,4,128]{2,1,0:T(4,128)(2,1)}, u32[]{:S(2)}) copy-start(bf16[512,4,128]{2,1,0:T(4,128)(2,1)} %reshape.263) | copy-start | bytes 1572868
  83.7 29.4 %collective-permute-start.3 = (f32[512,4,128]{2,0,1:T(8,128)}, f32[512,4,128]{2,0,1:T(8,128)}, u32[]{:S(2)}, u32[]{:S(2)}) collective-permute-start(f32[512,4,128]{2,0,1:T(8,128)} %get-tuple-element.119), channel_id=1, source_target_pairs={{0,1},{1,2},{2,3},{3,4},{4,5},{5,6},{6,7},{8,9},{9,10},{10,11},{11... | collective-permute-start | bytes 3145736 | tf_op jit(solution)/shard_map/ppermute | solution.py:32
  85.9 14.5 %copy-start.1 = (bf16[1536,512]{0,1:T(8,128)(2,1)S(1)}, bf16[1536,512]{0,1:T(8,128)(2,1)}, u32[]{:S(2)}) copy-start(bf16[1536,512]{0,1:T(8,128)(2,1)} %copy-done) | copy-start | bytes 4718596
  85.9 27.1 %collective-permute-start.2 = (f32[512,4,128]{2,0,1:T(8,128)}, f32[512,4,128]{2,0,1:T(8,128)}, u32[]{:S(2)}, u32[]{:S(2)}) collective-permute-start(f32[512,4,128]{2,0,1:T(8,128)} %get-tuple-element.118), channel_id=1, source_target_pairs={{1,0},{2,1},{3,2},{4,3},{5,4},{6,5},{7,6},{9,8},{10,9},{11,10},{12... | collective-permute-start | bytes 3145736 | tf_op jit(solution)/shard_map/ppermute | solution.py:32
  90.5 1.7 %copy-start.2 = (f32[1536,4,128]{2,0,1:T(8,128)}, f32[1536,4,128]{2,0,1:T(8,128)S(1)}, u32[]{:S(2)}) copy-start(f32[1536,4,128]{2,0,1:T(8,128)S(1)} %fusion.11) | copy-start | bytes 9437188
  93.7 32.0 %collective-permute-start.5 = (f32[512,4,128]{2,0,1:T(8,128)}, f32[512,4,128]{2,0,1:T(8,128)}, u32[]{:S(2)}, u32[]{:S(2)}) collective-permute-start(f32[512,4,128]{2,0,1:T(8,128)} %get-tuple-element.117), channel_id=1, source_target_pairs={{0,1},{1,2},{2,3},{3,4},{4,5},{5,6},{6,7},{8,9},{9,10},{10,11},{11... | collective-permute-start | bytes 3145736 | tf_op jit(solution)/shard_map/ppermute | solution.py:32
  99.2 26.5 %collective-permute-start.4 = (f32[512,4,128]{2,0,1:T(8,128)}, f32[512,4,128]{2,0,1:T(8,128)}, u32[]{:S(2)}, u32[]{:S(2)}) collective-permute-start(f32[512,4,128]{2,0,1:T(8,128)} %get-tuple-element.116), channel_id=1, source_target_pairs={{1,0},{2,1},{3,2},{4,3},{5,4},{6,5},{7,6},{9,8},{10,9},{11,10},{12... | collective-permute-start | bytes 3145736 | tf_op jit(solution)/shard_map/ppermute | solution.py:32
  108.9 13.3 %all-to-all-start.4 = ((bf16[4,128,512]{1,2,0:T(8,128)(2,1)}), bf16[4,128,512]{1,2,0:T(8,128)(2,1)}, u32[]{:S(2)}, u32[]{:S(2)}) async-start(bf16[4,128,512]{1,2,0:T(8,128)(2,1)} %copy.68), calls=%async_computation.4 | async-start | bytes 1048576 | tf_op jit(solution)/shard_map/all_to_all | solution.py:151
  122.2 12.1 %all-to-all-start.5 = ((bf16[4,128,512]{2,1,0:T(8,128)(2,1)}), bf16[4,128,512]{2,1,0:T(8,128)(2,1)S(1)}, u32[]{:S(2)}, u32[]{:S(2)}) async-start(bf16[4,128,512]{2,1,0:T(8,128)(2,1)} %convert_element_type.44), calls=%async_computation.5 | async-start | bytes 1048576 | tf_op jit(solution)/shard_map/all_to_all | solution.py:152
  134.3 11.2 %all-to-all-start.6 = ((bf16[4,128,512]{2,1,0:T(8,128)(2,1)}), bf16[4,128,512]{2,1,0:T(8,128)(2,1)S(1)}, u32[]{:S(2)}, u32[]{:S(2)}) async-start(bf16[4,128,512]{2,1,0:T(8,128)(2,1)} %convert_element_type.47), calls=%async_computation.6 | async-start | bytes 1048576 | tf_op jit(solution)/shard_map/all_to_all | solution.py:153
where the time goes:
time: 148 us; the launch traced here: 147 us
  starting transfers between devices  42.5 us (29%)
  waiting for transfers between devices  40.1 us (27%)
  local copies, waits for them, and re-layouts  29.9 us (20%)
  matrix products  23.9 us (16%)
  other arithmetic  9.46 us (6%)
    ppermute x4, starting transfers between devices, from_behind(): return lax.ppermute(array, axis, pairs)  10.6 us
    unnamed x17, local copies, waits for them, and re-layouts  9.94 us
    all_to_all x1, waiting for transfers between devices, shards(): lax.all_to_all(key_in, 'head', split_axis=1, concat_axis=0, tiled=True)  6.9 us
    all_to_all x1, waiting for transfers between devices, shards(): lax.all_to_all(query, 'head', split_axis=1, concat_axis=0, tiled=True)  6.74 us
    convert_element_type x6, local copies, waits for them, and re-layouts, merge_heads(): return stacked.reshape(row_count, feat_width).astype(jnp.bfloat16)  6.66 us
    all_to_all x1, waiting for transfers between devices, shards(): lax.all_to_all(merge_heads(query_sum), 'head', split_axis=0, concat_axis=...  6.02 us
    all_to_all x1, waiting for transfers between devices, shards(): lax.all_to_all(value, 'head', split_axis=1, concat_axis=0, tiled=True)  5.98 us
    all_to_all x1, starting transfers between devices, shards(): lax.all_to_all(value, 'head', split_axis=1, concat_axis=0, tiled=True)  5.16 us
  transfers between devices with their start and end apart: 13, of which 7 were waited for; matrix products, arithmetic and copies ran while one was open for 22% of the time, Pallas kernels for 0%

commit v1 on v0

v1 whole, which is shorter than its diff:
```python
import functools
import math

import jax
import jax.numpy as jnp
from jax import lax
from jax.experimental import pallas as pl
from jax.experimental.pallas import tpu as pltpu
from jax.sharding import PartitionSpec as P

HEADS = 16
HEAD_DIM = 128
HALF = 512
TILE = 512
SUB = 256
SPAN = SUB + 2 * HALF
CHUNKS = SPAN // SUB
NEG = -1e30


def dot(a, b, contract):
    return lax.dot_general(
        a, b, ((contract[:1], contract[1:]), ((), ())), preferred_element_type=jnp.float32
    )


def attention_kernel(
    edge_ref, qd_ref, kv_ref, prev_ref, next_ref,
    dq_ref, own_ref, dprev_ref, dnext_ref,
    k_ext, v_ext, dk_ext, dv_ext, s_buf, p_buf,
):
    tile, tiles = pl.program_id(1), pl.num_programs(1)
    rows = kv_ref.shape[0] * kv_ref.shape[2]
    scale = HEAD_DIM ** -0.5
    rate = scale * math.log2(math.e)
    has_prev = jnp.logical_or(edge_ref[0] > 0, tile > 0)
    has_next = jnp.logical_or(edge_ref[1] > 0, tile < tiles - 1)

    @pl.when(tile == 0)
    def _():
        for which, ext in ((0, k_ext), (1, v_ext)):
            ext[:HALF] = prev_ref[:, which].reshape(HALF, HEAD_DIM)
            ext[HALF:HALF + rows] = kv_ref[:, which].reshape(rows, HEAD_DIM)
            ext[HALF + rows:] = next_ref[:, which].reshape(HALF, HEAD_DIM)
        dk_ext[...] = jnp.zeros_like(dk_ext)
        dv_ext[...] = jnp.zeros_like(dv_ext)

    query_all = qd_ref[:, 0].reshape(TILE, HEAD_DIM)
    grad_all = qd_ref[:, 1].reshape(TILE, HEAD_DIM)
    key_id = lax.broadcasted_iota(jnp.int32, (SUB, SUB), 0)
    query_id = lax.broadcasted_iota(jnp.int32, (SUB, SUB), 1)
    for sub in range(TILE // SUB):
        query = query_all[sub * SUB:(sub + 1) * SUB]
        grad = grad_all[sub * SUB:(sub + 1) * SUB]

        def ext_rows(c):
            start = tile * TILE + (sub + c) * SUB
            return pl.ds(pl.multiple_of(start, SUB), SUB)

        top = jnp.full((1, SUB), NEG, jnp.float32)
        for c in range(CHUNKS):
            s = dot(k_ext[ext_rows(c)], query, (1, 1)) * rate
            keep = None
            if c == 0:
                keep = key_id >= query_id
            if c == CHUNKS - 1:
                keep = key_id <= query_id
            if sub + c < HALF // SUB:
                keep = has_prev if keep is None else jnp.logical_and(keep, has_prev)
            if sub + c >= (HALF + TILE) // SUB:
                keep = has_next if keep is None else jnp.logical_and(keep, has_next)
            if keep is not None:
                s = jnp.where(keep, s, NEG)
            s_buf[c * SUB:(c + 1) * SUB] = s
            top = jnp.maximum(top, jnp.max(s, axis=0, keepdims=True))
        total = jnp.zeros((1, SUB), jnp.float32)
        delta = jnp.zeros((1, SUB), jnp.float32)
        for c in range(CHUNKS):
            at = slice(c * SUB, (c + 1) * SUB)
            e = jnp.exp2(s_buf[at] - top)
            dp = dot(v_ext[ext_rows(c)], grad, (1, 1))
            s_buf[at] = e
            p_buf[at] = dp
            total += jnp.sum(e, axis=0, keepdims=True)
            delta += jnp.sum(e * dp, axis=0, keepdims=True)
        inverse = 1.0 / total
        delta = delta * inverse
        dq = jnp.zeros((SUB, HEAD_DIM), jnp.float32)
        for c in range(CHUNKS):
            at = slice(c * SUB, (c + 1) * SUB)
            w = s_buf[at] * inverse
            ds = (w * (p_buf[at] - delta)).astype(jnp.bfloat16)
            dv_ext[ext_rows(c)] += dot(w.astype(jnp.bfloat16), grad, (1, 0))
            dk_ext[ext_rows(c)] += dot(ds, query, (1, 0))
            dq += dot(ds, k_ext[ext_rows(c)], (0, 0))
        per = SUB // dq_ref.shape[1]
        dq_ref[sub * per:(sub + 1) * per] = (
            (dq * scale).astype(jnp.bfloat16).reshape(per, dq_ref.shape[1], HEAD_DIM)
        )

    @pl.when(tile == tiles - 1)
    def _():
        for which, ext, factor in ((0, dk_ext, scale), (1, dv_ext, 1.0)):
            dprev_ref[:, which] = (
                (ext[:HALF] * factor).astype(jnp.bfloat16).reshape(dprev_ref[:, which].shape)
            )
            own_ref[:, which] = (ext[HALF:HALF + rows] * factor).reshape(own_ref[:, which].shape)
            dnext_ref[:, which] = (
                (ext[HALF + rows:] * factor).astype(jnp.bfloat16).reshape(dnext_ref[:, which].shape)
            )


def attention(edge, qd, kv, prev, nxt):
    n, _, r, width = kv.shape
    rows = n * r
    heads, tiles = width // HEAD_DIM, rows // TILE
    whole = pl.BlockSpec((n, 2, r, HEAD_DIM), lambda h, t, e: (0, 0, 0, h))
    halo = pl.BlockSpec((HALF // r, 2, r, HEAD_DIM), lambda h, t, e: (0, 0, 0, h))
    return pl.pallas_call(
        attention_kernel,
        grid_spec=pltpu.PrefetchScalarGridSpec(
            num_scalar_prefetch=1,
            grid=(heads, tiles),
            in_specs=[
                pl.BlockSpec((TILE // r, 2, r, HEAD_DIM), lambda h, t, e: (t, 0, 0, h)),
                whole, halo, halo,
            ],
            out_specs=[
                pl.BlockSpec((TILE // r, r, HEAD_DIM), lambda h, t, e: (t, 0, h)),
                whole, halo, halo,
            ],
            scratch_shapes=[
                pltpu.VMEM((rows + 2 * HALF, HEAD_DIM), jnp.bfloat16),
                pltpu.VMEM((rows + 2 * HALF, HEAD_DIM), jnp.bfloat16),
                pltpu.VMEM((rows + 2 * HALF, HEAD_DIM), jnp.float32),
                pltpu.VMEM((rows + 2 * HALF, HEAD_DIM), jnp.float32),
                pltpu.VMEM((SPAN, SUB), jnp.float32),
                pltpu.VMEM((SPAN, SUB), jnp.float32),
            ],
        ),
        out_shape=[
            jax.ShapeDtypeStruct((n, r, width), jnp.bfloat16),
            jax.ShapeDtypeStruct(kv.shape, jnp.float32),
            jax.ShapeDtypeStruct(prev.shape, jnp.bfloat16),
            jax.ShapeDtypeStruct(prev.shape, jnp.bfloat16),
        ],
        compiler_params=pltpu.CompilerParams(vmem_limit_bytes=40 * 1024 * 1024),
        name="attention",
    )(edge, qd, kv, prev, nxt)


def moved(array, by):
    count = lax.axis_size("blk")
    return lax.ppermute(array, "blk", [(i, i + by) for i in range(count) if 0 <= i + by < count])


def shards(query, key_in, value, grad_out):
    n = lax.axis_size("head")
    r = query.shape[0]
    width = query.shape[1] // n
    blocks = HALF // r

    def packed(a, b):
        return jnp.stack(
            [
                jnp.stack([x[:, i * width:(i + 1) * width] for x in (a, b)])
                for i in range(n)
            ]
        )

    def swapped(array):
        return lax.all_to_all(array, "head", split_axis=0, concat_axis=0, tiled=True)

    kv = swapped(packed(key_in, value))
    prev = moved(kv[n - blocks:], 1)
    nxt = moved(kv[:blocks], -1)
    qd = swapped(packed(query, grad_out))
    index = lax.axis_index("blk")
    edge = jnp.stack([index, lax.axis_size("blk") - 1 - index]).astype(jnp.int32)
    dq, own, dprev, dnext = attention(edge, qd, kv, prev, nxt)
    down = moved(dprev, -1).astype(jnp.float32)
    up = moved(dnext, 1).astype(jnp.float32)
    if n == blocks:
        total = own + down + up
    else:
        total = own.at[n - blocks:].add(down).at[:blocks].add(up)
    dkv = swapped(total.astype(jnp.bfloat16))
    dq = swapped(dq)

    def merged(x):
        return jnp.concatenate([x[i] for i in range(n)], axis=1)

    return merged(dq), merged(dkv[:, 0]), merged(dkv[:, 1])


def solution(mesh):
    spec = P(("blk", "head"), None)
    return jax.shard_map(
        shards, mesh=mesh, in_specs=(spec,) * 4, out_specs=(spec,) * 3, check_vma=False
    )
```

time: 148 us -> 102 us (0.69)
  the two profiles are of different devices: /device:TPU:0 before, /device:TPU:16 now
where the time goes in v1:
time: 102 us
  waiting for transfers between devices  51.3 us (50%)
  starting transfers between devices  22.9 us (22%)
  Pallas kernels  14 us (14%)
  other arithmetic  8.08 us (8%)
  local copies, waits for them, and re-layouts  4.62 us (5%)
    all_to_all x4, waiting for transfers between devices, swapped(): lax.all_to_all(array, 'head', split_axis=0, concat_axis=0, tiled=True)  40.7 us
    all_to_all x4, starting transfers between devices, swapped(): lax.all_to_all(array, 'head', split_axis=0, concat_axis=0, tiled=True)  14.2 us
    pallas_call x1, Pallas kernels, attention(): pl.pallas_call(attention_kernel, grid_spec=pltpu.PrefetchScalarGridSpec(n...  14 us
    ppermute x4, waiting for transfers between devices, moved(): lax.ppermute(array, 'blk', [(i, i + by) for i in range(count) if 0 <= i +...  10.6 us
    ppermute x4, starting transfers between devices, moved(): lax.ppermute(array, 'blk', [(i, i + by) for i in range(count) if 0 <= i +...  8.63 us
    convert_element_type x1, other arithmetic, shards(): dkv = swapped(total.astype(jnp.bfloat16))  3.01 us
    concatenate x3, other arithmetic, merged(): return jnp.concatenate([x[i] for i in range(n)], axis=1)  2.55 us
    another operation x6, other arithmetic, packed(): jnp.stack([jnp.stack([x[:, i * width:(i + 1) * width] for x in (a, b)]) f...  2.44 us
  transfers between devices with their start and end apart: 8, of which 5 were waited for; matrix products, arithmetic and copies ran while one was open for 5% of the time, Pallas kernels for 0%

profile of v1, /device:TPU:16, one launch (start us, length us, event | category | flops | bytes accessed | tf_op | source)
XLA Modules:
  0.0 101.6 jit_solution(7448487603190903073)
XLA Ops:
  0.6 1.1 %slice_bitcast_fusion.19 = (bf16[1,128,512]{2,1,0:T(8,128)(2,1)S(1)}, bf16[1,128,512]{2,1,0:T(8,128)(2,1)S(1)}, bf16[1,128,512]{2,1,0:T(8,128)(2,1)S(1)}, bf16[1,128,512]{2,1,0:T(8,128)(2,1)S(1)}) fusion(bf16[128,2048]{1,0:T(8,128)(2,1)} %param.5), kind=kLoop, calls=%fused_computation.33 | loop fusion | bytes 1048576 | tf_op jit(solution)/shard_map/stack | solution.py:166
  1.8 1.1 %slice_bitcast_fusion.18 = (bf16[1,128,512]{2,1,0:T(8,128)(2,1)S(1)}, bf16[1,128,512]{2,1,0:T(8,128)(2,1)S(1)}, bf16[1,128,512]{2,1,0:T(8,128)(2,1)S(1)}, bf16[1,128,512]{2,1,0:T(8,128)(2,1)S(1)}) fusion(bf16[128,2048]{1,0:T(8,128)(2,1)} %param.6), kind=kLoop, calls=%fused_computation.32 | loop fusion | bytes 1048576 | tf_op jit(solution)/shard_map/stack | solution.py:166
  3.0 0.0 copy-start.2
  3.0 0.0 copy-start.3
  3.0 1.2 %pad_maximum_fusion.1 = bf16[4,2,128,512]{3,2,1,0:T(8,128)(2,1)} fusion(bf16[1,2,128,512]{3,2,1,0:T(8,128)(2,1)S(1)} %get-tuple-element.46, bf16[1,2,128,512]{3,2,1,0:T(8,128)(2,1)S(1)} %get-tuple-element.45, bf16[1,2,128,512]{3,2,1,0:T(8,128)(2,1)S(1)} %get-tuple-element.44, bf16[1,2,128,512]{3,2,1,0:T(8,128)(2,1)S(1)} %get-tuple-element.43), kind=kLoop, calls=%fused_computation.2 | loop fusion | flops 1572864 | bytes 2097152 | tf_op jit(solution)/shard_map/stack | solution.py:164
  4.2 3.7 %all-to-all-start.1 = ((bf16[4,2,128,512]{3,2,1,0:T(8,128)(2,1)}), bf16[4,2,128,512]{3,2,1,0:T(8,128)(2,1)S(1)}, u32[]{:S(2)}, u32[]{:S(2)}) async-start(bf16[4,2,128,512]{3,2,1,0:T(8,128)(2,1)} %pad_maximum_fusion.1), calls=%async_computation.1 | async-start | bytes 2097152 | tf_op jit(solution)/shard_map/all_to_all | solution.py:172
  7.9 0.0 copy-done.2
  8.0 0.0 copy-done.3
  8.1 13.5 %all-to-all-done.1.kv_ref = bf16[4,2,128,512]{3,2,1,0:T(8,128)(2,1)S(1)} async-done(((bf16[4,2,128,512]{3,2,1,0:T(8,128)(2,1)}), bf16[4,2,128,512]{3,2,1,0:T(8,128)(2,1)S(1)}, u32[]{:S(2)}, u32[]{:S(2)}) %all-to-all-start.1) | async-done | bytes 1048608 | tf_op jit(solution)/shard_map/all_to_all | solution.py:172
  21.6 1.9 %collective-permute-start.1 = (bf16[4,2,128,512]{3,2,1,0:T(8,128)(2,1)S(1)}, bf16[4,2,128,512]{3,2,1,0:T(8,128)(2,1)S(1)}, u32[]{:S(2)}, u32[]{:S(2)}) collective-permute-start(bf16[4,2,128,512]{3,2,1,0:T(8,128)(2,1)S(1)} %all-to-all-done.1.kv_ref), channel_id=1, source_target_pairs={{1,0},{2,1},{3,2},{4,3},{5,4},{6,5},{7,6},{9,8},{10,9},{11,10},{12... | collective-permute-start | bytes 3145736 | tf_op jit(solution)/shard_map/ppermute | solution.py:154
  23.5 2.4 %collective-permute-start = (bf16[4,2,128,512]{3,2,1,0:T(8,128)(2,1)S(1)}, bf16[4,2,128,512]{3,2,1,0:T(8,128)(2,1)}, u32[]{:S(2)}, u32[]{:S(2)}) collective-permute-start(bf16[4,2,128,512]{3,2,1,0:T(8,128)(2,1)S(1)} %all-to-all-done.1.kv_ref), channel_id=1, source_target_pairs={{0,1},{1,2},{2,3},{3,4},{4,5},{5,6},{6,7},{8,9},{9,10},{10,11},{11... | collective-permute-start | bytes 3145736 | tf_op jit(solution)/shard_map/ppermute | solution.py:154
  26.0 1.1 %pad_maximum_fusion = bf16[4,2,128,512]{3,2,1,0:T(8,128)(2,1)} fusion(bf16[1,2,128,512]{3,2,1,0:T(8,128)(2,1)S(1)} %get-tuple-element.42, bf16[1,2,128,512]{3,2,1,0:T(8,128)(2,1)S(1)} %get-tuple-element.41, bf16[1,2,128,512]{3,2,1,0:T(8,128)(2,1)S(1)} %get-tuple-element.40, bf16[1,2,128,512]{3,2,1,0:T(8,128)(2,1)S(1)} %get-tuple-element.39), kind=kLoop, calls=%fused_computation.1 | loop fusion | flops 1572864 | bytes 2097152 | tf_op jit(solution)/shard_map/stack | solution.py:164
  27.1 3.5 %all-to-all-start = ((bf16[4,2,128,512]{3,2,1,0:T(8,128)(2,1)}), bf16[4,2,128,512]{3,2,1,0:T(8,128)(2,1)S(1)}, u32[]{:S(2)}, u32[]{:S(2)}) async-start(bf16[4,2,128,512]{3,2,1,0:T(8,128)(2,1)} %pad_maximum_fusion), calls=%async_computation | async-start | bytes 2097152 | tf_op jit(solution)/shard_map/all_to_all | solution.py:172
  30.6 0.1 pad_add_fusion.edge_ref
  30.7 14.7 %all-to-all-done.qd_ref = bf16[4,2,128,512]{3,2,1,0:T(8,128)(2,1)S(1)} async-done(((bf16[4,2,128,512]{3,2,1,0:T(8,128)(2,1)}), bf16[4,2,128,512]{3,2,1,0:T(8,128)(2,1)S(1)}, u32[]{:S(2)}, u32[]{:S(2)}) %all-to-all-start) | async-done | bytes 1048608 | tf_op jit(solution)/shard_map/all_to_all | solution.py:172
  45.4 0.0 collective-permute-done.1.next_ref
  45.4 0.0 collective-permute-done.prev_ref
  45.4 14.0 %attention.1 = (bf16[4,128,512]{2,1,0:T(8,128)(2,1)S(1)}, f32[4,2,128,512]{3,2,1,0:T(8,128)S(1)}, bf16[4,2,128,512]{3,2,1,0:T(8,128)(2,1)}, bf16[4,2,128,512]{3,2,1,0:T(8,128)(2,1)}) custom-call(s32[2]{0:T(128)S(1)} %pad_add_fusion.edge_ref, bf16[4,2,128,512]{3,2,1,0:T(8,128)(2,1)S(1)} %all-to-all-done.qd_ref, ...), custom_call_target="tpu_custom_call" | custom-call | tf_op jit(solution)/shard_map/attention/pallas_call | solution.py:119
  59.4 0.0 copy-start
  59.4 1.3 %copy-done = f32[4,2,128,512]{3,2,1,0:T(8,128)} copy-done((f32[4,2,128,512]{3,2,1,0:T(8,128)}, f32[4,2,128,512]{3,2,1,0:T(8,128)S(1)}, u32[]{:S(2)}) %copy-start) | copy-done | bytes 2097176
  60.7 0.0 copy-start.1
  60.7 0.8 copy-done.1
  61.5 2.1 %collective-permute-start.2 = (bf16[4,2,128,512]{3,2,1,0:T(8,128)(2,1)}, bf16[4,2,128,512]{3,2,1,0:T(8,128)(2,1)S(1)}, u32[]{:S(2)}, u32[]{:S(2)}) collective-permute-start(bf16[4,2,128,512]{3,2,1,0:T(8,128)(2,1)} %get-tuple-element.9), channel_id=1, source_target_pairs={{1,0},{2,1},{3,2},{4,3},{5,4},{6,5},{7,6},{9,8},{10,9},{11,10},{12... | collective-permute-start | bytes 3145736 | tf_op jit(solution)/shard_map/ppermute | solution.py:154
  63.6 2.3 %collective-permute-start.3 = (bf16[4,2,128,512]{3,2,1,0:T(8,128)(2,1)}, bf16[4,2,128,512]{3,2,1,0:T(8,128)(2,1)S(1)}, u32[]{:S(2)}, u32[]{:S(2)}) collective-permute-start(bf16[4,2,128,512]{3,2,1,0:T(8,128)(2,1)} %get-tuple-element.10), channel_id=1, source_target_pairs={{0,1},{1,2},{2,3},{3,4},{4,5},{5,6},{6,7},{8,9},{9,10},{10,11},{11... | collective-permute-start | bytes 3145736 | tf_op jit(solution)/shard_map/ppermute | solution.py:154
  65.9 3.5 %all-to-all-start.2 = ((bf16[4,128,512]{2,1,0:T(8,128)(2,1)}), bf16[4,128,512]{2,1,0:T(8,128)(2,1)S(1)}, u32[]{:S(2)}, u32[]{:S(2)}) async-start(bf16[4,128,512]{2,1,0:T(8,128)(2,1)} %copy-done.1), calls=%async_computation.2 | async-start | bytes 1048576 | tf_op jit(solution)/shard_map/all_to_all | solution.py:172
  69.4 6.9 %collective-permute-done.2 = bf16[4,2,128,512]{3,2,1,0:T(8,128)(2,1)S(1)} collective-permute-done((bf16[4,2,128,512]{3,2,1,0:T(8,128)(2,1)}, bf16[4,2,128,512]{3,2,1,0:T(8,128)(2,1)S(1)}, u32[]{:S(2)}, u32[]{:S(2)}) %collective-permute-start.2) | collective-permute-done | bytes 1048608 | tf_op jit(solution)/shard_map/ppermute | solution.py:154
  76.2 3.7 %collective-permute-done.3 = bf16[4,2,128,512]{3,2,1,0:T(8,128)(2,1)S(1)} collective-permute-done((bf16[4,2,128,512]{3,2,1,0:T(8,128)(2,1)}, bf16[4,2,128,512]{3,2,1,0:T(8,128)(2,1)S(1)}, u32[]{:S(2)}, u32[]{:S(2)}) %collective-permute-start.3) | collective-permute-done | bytes 1048608 | tf_op jit(solution)/shard_map/ppermute | solution.py:154
  79.9 3.0 %add_convert_fusion = bf16[4,2,128,512]{3,2,1,0:T(8,128)(2,1)} fusion(bf16[4,2,128,512]{3,2,1,0:T(8,128)(2,1)S(1)} %collective-permute-done.3, f32[4,2,128,512]{3,2,1,0:T(8,128)} %copy-done, bf16[4,2,128,512]{3,2,1,0:T(8,128)(2,1)S(1)} %collective-permute-done.2), kind=kLoop, calls=%fused_computation | loop fusion | flops 2621440 | bytes 5242880 | tf_op jit(solution)/shard_map/convert_element_type | solution.py:187
  82.9 0.0 all-to-all-done.2
  83.0 3.5 %all-to-all-start.3 = ((bf16[4,2,128,512]{3,2,1,0:T(8,128)(2,1)}), bf16[4,2,128,512]{3,2,1,0:T(8,128)(2,1)S(1)}, u32[]{:S(2)}, u32[]{:S(2)}) async-start(bf16[4,2,128,512]{3,2,1,0:T(8,128)(2,1)} %add_convert_fusion), calls=%async_computation.3 | async-start | bytes 2097152 | tf_op jit(solution)/shard_map/all_to_all | solution.py:172
  86.5 0.8 pad_maximum_fusion.2
  87.4 12.5 %all-to-all-done.3 = bf16[4,2,128,512]{3,2,1,0:T(8,128)(2,1)S(1)} async-done(((bf16[4,2,128,512]{3,2,1,0:T(8,128)(2,1)}), bf16[4,2,128,512]{3,2,1,0:T(8,128)(2,1)S(1)}, u32[]{:S(2)}, u32[]{:S(2)}) %all-to-all-start.3) | async-done | bytes 1048608 | tf_op jit(solution)/shard_map/all_to_all | solution.py:172
  99.8 0.1 slice_bitcast_fusion.3
  99.9 0.9 pad_maximum_fusion.4
  100.8 0.8 pad_maximum_fusion.3
  (7 shorter events, 0.3 us)
Async XLA Ops:
  3.0 4.9 %copy-start.2 = (bf16[128,2048]{1,0:T(8,128)(2,1)S(1)}, bf16[128,2048]{1,0:T(8,128)(2,1)}, u32[]{:S(2)}) copy-start(bf16[128,2048]{1,0:T(8,128)(2,1)} %param.4) | copy-start | bytes 1572868
  3.0 4.9 %copy-start.3 = (bf16[128,2048]{1,0:T(8,128)(2,1)S(1)}, bf16[128,2048]{1,0:T(8,128)(2,1)}, u32[]{:S(2)}) copy-start(bf16[128,2048]{1,0:T(8,128)(2,1)} %param.7) | copy-start | bytes 1572868
  4.2 17.4 %all-to-all-start.1 = ((bf16[4,2,128,512]{3,2,1,0:T(8,128)(2,1)}), bf16[4,2,128,512]{3,2,1,0:T(8,128)(2,1)S(1)}, u32[]{:S(2)}, u32[]{:S(2)}) async-start(bf16[4,2,128,512]{3,2,1,0:T(8,128)(2,1)} %pad_maximum_fusion.1), calls=%async_computation.1 | async-start | bytes 2097152 | tf_op jit(solution)/shard_map/all_to_all | solution.py:172
  21.6 23.8 %collective-permute-start.1 = (bf16[4,2,128,512]{3,2,1,0:T(8,128)(2,1)S(1)}, bf16[4,2,128,512]{3,2,1,0:T(8,128)(2,1)S(1)}, u32[]{:S(2)}, u32[]{:S(2)}) collective-permute-start(bf16[4,2,128,512]{3,2,1,0:T(8,128)(2,1)S(1)} %all-to-all-done.1.kv_ref), channel_id=1, source_target_pairs={{1,0},{2,1},{3,2},{4,3},{5,4},{6,5},{7,6},{9,8},{10,9},{11,10},{12... | collective-permute-start | bytes 3145736 | tf_op jit(solution)/shard_map/ppermute | solution.py:154
  23.5 21.9 %collective-permute-start = (bf16[4,2,128,512]{3,2,1,0:T(8,128)(2,1)S(1)}, bf16[4,2,128,512]{3,2,1,0:T(8,128)(2,1)}, u32[]{:S(2)}, u32[]{:S(2)}) collective-permute-start(bf16[4,2,128,512]{3,2,1,0:T(8,128)(2,1)S(1)} %all-to-all-done.1.kv_ref), channel_id=1, source_target_pairs={{0,1},{1,2},{2,3},{3,4},{4,5},{5,6},{6,7},{8,9},{9,10},{10,11},{11... | collective-permute-start | bytes 3145736 | tf_op jit(solution)/shard_map/ppermute | solution.py:154
  27.1 18.3 %all-to-all-start = ((bf16[4,2,128,512]{3,2,1,0:T(8,128)(2,1)}), bf16[4,2,128,512]{3,2,1,0:T(8,128)(2,1)S(1)}, u32[]{:S(2)}, u32[]{:S(2)}) async-start(bf16[4,2,128,512]{3,2,1,0:T(8,128)(2,1)} %pad_maximum_fusion), calls=%async_computation | async-start | bytes 2097152 | tf_op jit(solution)/shard_map/all_to_all | solution.py:172
  59.4 1.3 %copy-start = (f32[4,2,128,512]{3,2,1,0:T(8,128)}, f32[4,2,128,512]{3,2,1,0:T(8,128)S(1)}, u32[]{:S(2)}) copy-start(f32[4,2,128,512]{3,2,1,0:T(8,128)S(1)} %get-tuple-element.8) | copy-start | bytes 6291460
  60.7 0.8 copy-start.1
  61.5 14.7 %collective-permute-start.2 = (bf16[4,2,128,512]{3,2,1,0:T(8,128)(2,1)}, bf16[4,2,128,512]{3,2,1,0:T(8,128)(2,1)S(1)}, u32[]{:S(2)}, u32[]{:S(2)}) collective-permute-start(bf16[4,2,128,512]{3,2,1,0:T(8,128)(2,1)} %get-tuple-element.9), channel_id=1, source_target_pairs={{1,0},{2,1},{3,2},{4,3},{5,4},{6,5},{7,6},{9,8},{10,9},{11,10},{12... | collective-permute-start | bytes 3145736 | tf_op jit(solution)/shard_map/ppermute | solution.py:154
  63.6 16.3 %collective-permute-start.3 = (bf16[4,2,128,512]{3,2,1,0:T(8,128)(2,1)}, bf16[4,2,128,512]{3,2,1,0:T(8,128)(2,1)S(1)}, u32[]{:S(2)}, u32[]{:S(2)}) collective-permute-start(bf16[4,2,128,512]{3,2,1,0:T(8,128)(2,1)} %get-tuple-element.10), channel_id=1, source_target_pairs={{0,1},{1,2},{2,3},{3,4},{4,5},{5,6},{6,7},{8,9},{9,10},{10,11},{11... | collective-permute-start | bytes 3145736 | tf_op jit(solution)/shard_map/ppermute | solution.py:154
  65.9 17.1 %all-to-all-start.2 = ((bf16[4,128,512]{2,1,0:T(8,128)(2,1)}), bf16[4,128,512]{2,1,0:T(8,128)(2,1)S(1)}, u32[]{:S(2)}, u32[]{:S(2)}) async-start(bf16[4,128,512]{2,1,0:T(8,128)(2,1)} %copy-done.1), calls=%async_computation.2 | async-start | bytes 1048576 | tf_op jit(solution)/shard_map/all_to_all | solution.py:172
  83.0 16.9 %all-to-all-start.3 = ((bf16[4,2,128,512]{3,2,1,0:T(8,128)(2,1)}), bf16[4,2,128,512]{3,2,1,0:T(8,128)(2,1)S(1)}, u32[]{:S(2)}, u32[]{:S(2)}) async-start(bf16[4,2,128,512]{3,2,1,0:T(8,128)(2,1)} %add_convert_fusion), calls=%async_computation.3 | async-start | bytes 2097152 | tf_op jit(solution)/shard_map/all_to_all | solution.py:172

commit v2 on v1

v2 whole, which is shorter than its diff:
```python
import math

import jax
import jax.numpy as jnp
from jax import lax
from jax.experimental import pallas as pl
from jax.experimental.pallas import tpu as pltpu
from jax.sharding import PartitionSpec as P

HEADS = 16
HEAD_DIM = 128
HALF = 512
TILE = 512
SUB = 256
SPAN = SUB + 2 * HALF
CHUNKS = SPAN // SUB
NEG = -1e30
SCALE = HEAD_DIM ** -0.5
RATE = SCALE * math.log2(math.e)


def dot(a, b, contract):
    return lax.dot_general(
        a, b, ((contract[:1], contract[1:]), ((), ())), preferred_element_type=jnp.float32
    )


def rows_at(start, size):
    return pl.ds(pl.multiple_of(start, size), size)


def pack_kernel(order_ref, first_ref, second_ref, *outs):
    width = outs[0].shape[2]
    for k, out in enumerate(outs):
        columns = pl.ds(pl.multiple_of(order_ref[k] * width, 128), width)
        out[0] = first_ref[:, columns]
        out[1] = second_ref[:, columns]


def packed(order, first, second):
    n = order.shape[0]
    r, width = first.shape[0], first.shape[1] // n
    return pl.pallas_call(
        pack_kernel,
        in_specs=[pl.BlockSpec(memory_space=pltpu.SMEM)]
        + [pl.BlockSpec(memory_space=pltpu.VMEM)] * 2,
        out_specs=[pl.BlockSpec(memory_space=pltpu.VMEM)] * n,
        out_shape=[jax.ShapeDtypeStruct((2, r, width), first.dtype)] * n,
        name="pack",
    )(order, first, second)


def merge_kernel(order_ref, *refs):
    outs, ins = refs[-3:], refs[:-3]
    n = len(ins) // 2
    width = ins[0].shape[1]
    for k in range(n):
        columns = pl.ds(pl.multiple_of(order_ref[k] * width, 128), width)
        outs[0][:, columns] = ins[k][...]
        outs[1][:, columns] = ins[n + k][0]
        outs[2][:, columns] = ins[n + k][1]


def merged(order, dq, dkv):
    n = order.shape[0]
    r, width = dq[0].shape
    return pl.pallas_call(
        merge_kernel,
        in_specs=[pl.BlockSpec(memory_space=pltpu.SMEM)]
        + [pl.BlockSpec(memory_space=pltpu.VMEM)] * (2 * n),
        out_specs=[pl.BlockSpec(memory_space=pltpu.VMEM)] * 3,
        out_shape=[jax.ShapeDtypeStruct((r, n * width), dq[0].dtype)] * 3,
        name="merge",
    )(order, *dq, *dkv)


def query_kernel(n, order_ref, halo_ref, edge_ref, *refs):
    kv_refs, refs = refs[:n], refs[n:]
    qd_refs, refs = refs[:n], refs[n:]
    prev_ref, next_ref = refs[:2]
    dq_refs, refs = refs[2:2 + n], refs[2 + n:]
    stat_ref, part_ref, k_ext, v_ext, q_all, g_all, dq_all, s_buf, p_buf = refs
    tile, tiles = pl.program_id(1), pl.num_programs(1)
    r = kv_refs[0].shape[1]
    rows = n * r
    has_prev = jnp.logical_or(edge_ref[0] > 0, tile > 0)
    has_next = jnp.logical_or(edge_ref[1] > 0, tile < tiles - 1)
    single = rows == TILE

    @pl.when(tile == 0)
    def _():
        for i in range(HALF // r):
            at = halo_ref[i] * r
            for which, ext in ((0, k_ext), (1, v_ext)):
                ext[rows_at(at, r)] = prev_ref[i, which]
                ext[rows_at(HALF + rows + at, r)] = next_ref[i, which]
        for k in range(n):
            at = order_ref[k] * r
            for which, ext in ((0, k_ext), (1, v_ext)):
                ext[rows_at(HALF + at, r)] = kv_refs[k][which]
            q_all[rows_at(at, r)] = qd_refs[k][0]
            g_all[rows_at(at, r)] = qd_refs[k][1]
        if not single:
            part_ref[...] = jnp.zeros_like(part_ref)

    key_id = lax.broadcasted_iota(jnp.int32, (SUB, SUB), 0)
    query_id = lax.broadcasted_iota(jnp.int32, (SUB, SUB), 1)
    for sub in range(TILE // SUB):
        here = rows_at(tile * TILE + sub * SUB, SUB)
        query = q_all[here]
        grad = g_all[here]

        def ext_rows(c):
            return rows_at(tile * TILE + (sub + c) * SUB, SUB)

        top = jnp.full((1, SUB), NEG, jnp.float32)
        for c in range(CHUNKS):
            s = dot(k_ext[ext_rows(c)], query, (1, 1)) * RATE
            keep = None
            if c == 0:
                keep = key_id >= query_id
            if c == CHUNKS - 1:
                keep = key_id <= query_id
            if sub + c < HALF // SUB:
                keep = has_prev if keep is None else jnp.logical_and(keep, has_prev)
            if sub + c >= (HALF + TILE) // SUB:
                keep = has_next if keep is None else jnp.logical_and(keep, has_next)
            if keep is not None:
                s = jnp.where(keep, s, NEG)
            s_buf[c * SUB:(c + 1) * SUB] = s
            top = jnp.maximum(top, jnp.max(s, axis=0, keepdims=True))
        total = jnp.zeros((1, SUB), jnp.float32)
        delta = jnp.zeros((1, SUB), jnp.float32)
        for c in range(CHUNKS):
            at = slice(c * SUB, (c + 1) * SUB)
            e = jnp.exp2(s_buf[at] - top)
            dp = dot(v_ext[ext_rows(c)], grad, (1, 1))
            s_buf[at] = e
            p_buf[at] = dp
            total += jnp.sum(e, axis=0, keepdims=True)
            delta += jnp.sum(e * dp, axis=0, keepdims=True)
        inverse = 1.0 / total
        delta = delta * inverse
        stat_ref[0, 0:1, here] = top + jnp.log2(total)
        stat_ref[0, 1:2, here] = delta
        dq = jnp.zeros((SUB, HEAD_DIM), jnp.float32)
        for c in range(CHUNKS):
            at = slice(c * SUB, (c + 1) * SUB)
            w = s_buf[at] * inverse
            ds = (w * (p_buf[at] - delta)).astype(jnp.bfloat16)
            dq += dot(ds, k_ext[ext_rows(c)], (0, 0))
            low = w.astype(jnp.bfloat16)

            def keys_add(own, fresh):
                for which, left, right in ((0, ds, query), (1, low, grad)):
                    term = dot(left, right, (1, 0))
                    if fresh:
                        part_ref[which, own] = term
                    else:
                        part_ref[which, own] += term

            if single:
                e_at = (sub + c) * SUB - HALF
                if 0 <= e_at < TILE:
                    keys_add(slice(e_at, e_at + SUB), sub == 0)
            else:
                e_at = tile * TILE + (sub + c) * SUB - HALF

                @pl.when(jnp.logical_and(e_at >= 0, e_at < rows))
                def _():
                    keys_add(rows_at(e_at, SUB), False)
        dq_all[here] = (dq * SCALE).astype(jnp.bfloat16)

    @pl.when(tile == tiles - 1)
    def _():
        for k in range(n):
            dq_refs[k][...] = dq_all[rows_at(order_ref[k] * r, r)]


def query_part(order, halo, edge, kv, qd, prev, nxt):
    n = len(kv)
    _, r, width = kv[0].shape
    rows = n * r
    heads, tiles = width // HEAD_DIM, rows // TILE
    piece = pl.BlockSpec((2, r, HEAD_DIM), lambda h, t, *_: (0, 0, h))
    side = pl.BlockSpec((HALF // r, 2, r, HEAD_DIM), lambda h, t, *_: (0, 0, 0, h))
    outs = pl.pallas_call(
        lambda *refs: query_kernel(n, *refs),
        grid_spec=pltpu.PrefetchScalarGridSpec(
            num_scalar_prefetch=3,
            grid=(heads, tiles),
            in_specs=[piece] * (2 * n) + [side] * 2,
            out_specs=[pl.BlockSpec((r, HEAD_DIM), lambda h, t, *_: (0, h))] * n
            + [
                pl.BlockSpec((1, 2, rows), lambda h, t, *_: (h, 0, 0)),
                pl.BlockSpec((2, rows, HEAD_DIM), lambda h, t, *_: (0, 0, h)),
            ],
            scratch_shapes=[pltpu.VMEM((rows + 2 * HALF, HEAD_DIM), jnp.bfloat16)] * 2
            + [pltpu.VMEM((rows, HEAD_DIM), jnp.bfloat16)] * 3
            + [pltpu.VMEM((SPAN, SUB), jnp.float32)] * 2,
        ),
        out_shape=[jax.ShapeDtypeStruct((r, width), jnp.bfloat16)] * n
        + [
            jax.ShapeDtypeStruct((heads, 2, rows), jnp.float32),
            jax.ShapeDtypeStruct((2, rows, width), jnp.float32),
        ],
        compiler_params=pltpu.CompilerParams(vmem_limit_bytes=40 * 1024 * 1024),
        cost_estimate=pl.CostEstimate(
            flops=10 * heads * rows * SPAN * HEAD_DIM,
            bytes_accessed=12 * rows * width,
            transcendentals=heads * rows * SPAN,
        ),
        name="query_part",
    )(order, halo, edge, *kv, *qd, prev, nxt)
    return outs[:n], outs[n], outs[n + 1]


def key_kernel(n, order_ref, halo_ref, *refs):
    kv_refs, refs = refs[:n], refs[n:]
    sides, stats, part_ref = refs[:2], refs[2:4], refs[4]
    out_refs, (k_all, v_all, q_all, g_all, dk_all, dv_all) = refs[5:5 + n], refs[5 + n:]
    r = kv_refs[0].shape[1]
    rows = n * r
    for k in range(n):
        at = rows_at(order_ref[k] * r, r)
        k_all[at] = kv_refs[k][0]
        v_all[at] = kv_refs[k][1]
    for i in range(HALF // r):
        for side in range(2):
            at = rows_at(side * HALF + halo_ref[i] * r, r)
            q_all[at] = sides[side][i, 0]
            g_all[at] = sides[side][i, 1]
    dk_all[...] = part_ref[0]
    dv_all[...] = part_ref[1]
    key_id = lax.broadcasted_iota(jnp.int32, (SUB, SUB), 0)
    query_id = lax.broadcasted_iota(jnp.int32, (SUB, SUB), 1)
    steps = HALF // SUB
    for side in range(2):
        for b in range(steps):
            lanes = slice(b * SUB, (b + 1) * SUB)
            here = slice(side * HALF + b * SUB, side * HALF + (b + 1) * SUB)
            query = q_all[here]
            grad = g_all[here]
            log_total = stats[side][0, 0:1, lanes]
            delta = stats[side][0, 1:2, lanes]
            for a in range(steps):
                if (side == 0 and b < a) or (side == 1 and b > a):
                    continue
                first = a * SUB + (0 if side == 0 else rows - HALF)
                at = slice(first, first + SUB)
                w = jnp.exp2(dot(k_all[at], query, (1, 1)) * RATE - log_total)
                if a == b:
                    keep = key_id <= query_id if side == 0 else key_id >= query_id
                    w = jnp.where(keep, w, 0.0)
                ds = w * (dot(v_all[at], grad, (1, 1)) - delta)
                dk_all[at] += dot(ds.astype(jnp.bfloat16), query, (1, 0))
                dv_all[at] += dot(w.astype(jnp.bfloat16), grad, (1, 0))
    for k in range(n):
        at = rows_at(order_ref[k] * r, r)
        out_refs[k][0] = (dk_all[at] * SCALE).astype(jnp.bfloat16)
        out_refs[k][1] = dv_all[at].astype(jnp.bfloat16)


def key_part(order, halo, kv, prev, nxt, stat_prev, stat_next, part):
    n = len(kv)
    _, r, width = kv[0].shape
    rows = n * r
    heads = width // HEAD_DIM
    piece = pl.BlockSpec((2, r, HEAD_DIM), lambda h, *_: (0, 0, h))
    side = pl.BlockSpec((HALF // r, 2, r, HEAD_DIM), lambda h, *_: (0, 0, 0, h))
    stat = pl.BlockSpec((1, 2, HALF), lambda h, *_: (h, 0, 0))
    return pl.pallas_call(
        lambda *refs: key_kernel(n, *refs),
        grid_spec=pltpu.PrefetchScalarGridSpec(
            num_scalar_prefetch=2,
            grid=(heads,),
            in_specs=[piece] * n + [side] * 2 + [stat] * 2
            + [pl.BlockSpec((2, rows, HEAD_DIM), lambda h, *_: (0, 0, h))],
            out_specs=[piece] * n,
            scratch_shapes=[pltpu.VMEM((rows, HEAD_DIM), jnp.bfloat16)] * 2
            + [pltpu.VMEM((2 * HALF, HEAD_DIM), jnp.bfloat16)] * 2
            + [pltpu.VMEM((rows, HEAD_DIM), jnp.float32)] * 2,
        ),
        out_shape=[jax.ShapeDtypeStruct((2, r, width), jnp.bfloat16)] * n,
        compiler_params=pltpu.CompilerParams(vmem_limit_bytes=40 * 1024 * 1024),
        cost_estimate=pl.CostEstimate(
            flops=8 * heads * HALF * (HALF + SUB) * HEAD_DIM,
            bytes_accessed=24 * rows * width,
            transcendentals=heads * HALF * (HALF + SUB),
        ),
        name="key_part",
    )(order, halo, *kv, prev, nxt, stat_prev, stat_next, part)


def moved(array, by):
    count = lax.axis_size("blk")
    return lax.ppermute(array, "blk", [(i, i + by) for i in range(count) if 0 <= i + by < count])


def exchanged(pieces):
    n = len(pieces)
    return [pieces[0]] + [
        lax.ppermute(pieces[k], "head", [(i, i ^ k) for i in range(n)]) for k in range(1, n)
    ]


def shards(query, key_in, value, grad_out):
    n = lax.axis_size("head")
    blocks = HALF // query.shape[0]
    order = lax.axis_index("head").astype(jnp.int32) ^ jnp.arange(n, dtype=jnp.int32)
    index = lax.axis_index("blk")
    edge = jnp.stack([index, lax.axis_size("blk") - 1 - index]).astype(jnp.int32)

    def sides(pieces):
        stacked = jnp.stack(pieces)
        if n == blocks:
            return moved(stacked, 1), moved(stacked, -1)
        stacked = jnp.take(stacked, order, axis=0)
        return moved(stacked[n - blocks:], 1), moved(stacked[:blocks], -1)

    halo = order if n == blocks else jnp.arange(blocks, dtype=jnp.int32)
    kv = exchanged(packed(order, key_in, value))
    qd = exchanged(packed(order, query, grad_out))
    kv_prev, kv_next = sides(kv)
    qd_prev, qd_next = sides(qd)
    dq, stat, part = query_part(order, halo, edge, kv, qd, kv_prev, kv_next)
    stat_prev = moved(stat[:, :, -HALF:], 1)
    stat_next = moved(stat[:, :, :HALF], -1)
    dkv = key_part(order, halo, kv, qd_prev, qd_next, stat_prev, stat_next, part)
    dq, dkv = lax.optimization_barrier((exchanged(dq), dkv))
    return merged(order, dq, exchanged(dkv))


def solution(mesh):
    spec = P(("blk", "head"), None)
    return jax.shard_map(
        shards, mesh=mesh, in_specs=(spec,) * 4, out_specs=(spec,) * 3, check_vma=False
    )
```

time: 102 us -> 91.9 us (0.901)
  the two profiles are of different devices: /device:TPU:16 before, /device:TPU:0 now
where the time goes in v2:
time: 91.9 us; the launch traced here: 91.5 us
  starting transfers between devices  35.5 us (39%)
  Pallas kernels  28.1 us (31%)
  waiting for transfers between devices  21.2 us (23%)
  other arithmetic  3.83 us (4%)
  local copies, waits for them, and re-layouts  2.08 us (2%)
    ppermute x12, waiting for transfers between devices, exchanged(): lax.ppermute(pieces[k], 'head', [(i, i ^ k) for i in range(n)])  21.2 us
    ppermute x12, starting transfers between devices, exchanged(): lax.ppermute(pieces[k], 'head', [(i, i ^ k) for i in range(n)])  18.1 us
    ppermute x6, starting transfers between devices, moved(): lax.ppermute(array, 'blk', [(i, i + by) for i in range(count) if 0 <= i +...  17.4 us
    pallas_call x1, Pallas kernels, query_part(): pl.pallas_call(lambda *refs: query_kernel(n, *refs), grid_spec=pltpu.Pref...  12.4 us
    pallas_call x1, Pallas kernels, key_part(): pl.pallas_call(lambda *refs: key_kernel(n, *refs), grid_spec=pltpu.Prefet...  8.46 us
    pallas_call x2, Pallas kernels, packed(): pl.pallas_call(pack_kernel, in_specs=[pl.BlockSpec(memory_space=pltpu.SME...  4.51 us
    another operation x2, other arithmetic, sides(): stacked = jnp.stack(pieces)  3.24 us
    pallas_call x1, Pallas kernels, merged(): pl.pallas_call(merge_kernel, in_specs=[pl.BlockSpec(memory_space=pltpu.SM...  2.65 us
  transfers between devices with their start and end apart: 18, of which 6 were waited for; matrix products, arithmetic and copies ran while one was open for 4% of the time, Pallas kernels for 25%

profile of v2, /device:TPU:0, one launch (start us, length us, event | category | flops | bytes accessed | tf_op | source)
XLA Modules:
  0.0 91.5 jit_solution(5384684191928220780)
XLA Ops:
  0.6 0.5 iota_xor_fusion.order_ref.refs_0_.refs_1_
  1.2 2.2 %pack.2 = (bf16[2,128,512]{2,1,0:T(8,128)(2,1)}, bf16[2,128,512]{2,1,0:T(8,128)(2,1)}, bf16[2,128,512]{2,1,0:T(8,128)(2,1)}, bf16[2,128,512]{2,1,0:T(8,128)(2,1)}) custom-call(s32[4]{0:T(128)} %iota_xor_fusion.order_ref.refs_0_.refs_1_, bf16[128,2048]{1,0:T(8,128)(2,1)} %first_ref.2, bf16[128,2048]{1,0:T(8,128)(2,1)} %second_ref.2), custom_call_target="tpu_custom_call" | custom-call | tf_op jit(solution)/shard_map/pack/pallas_call | solution.py:43
  3.4 2.9 %collective-permute-start = (bf16[2,128,512]{2,1,0:T(8,128)(2,1)}, bf16[2,128,512]{2,1,0:T(8,128)(2,1)S(1)}, u32[]{:S(2)}, u32[]{:S(2)}) collective-permute-start(bf16[2,128,512]{2,1,0:T(8,128)(2,1)} %get-tuple-element.30), channel_id=1, source_target_pairs={{0,8},{8,0},{16,24},{24,16},{1,9},{9,1},{17,25},{25,17},{2,10},{10... | collective-permute-start | bytes 786440 | tf_op jit(solution)/shard_map/ppermute | solution.py:303
  6.3 1.5 %collective-permute-start.1 = (bf16[2,128,512]{2,1,0:T(8,128)(2,1)}, bf16[2,128,512]{2,1,0:T(8,128)(2,1)S(1)}, u32[]{:S(2)}, u32[]{:S(2)}) collective-permute-start(bf16[2,128,512]{2,1,0:T(8,128)(2,1)} %get-tuple-element.31), channel_id=1, source_target_pairs={{0,16},{8,24},{16,0},{24,8},{1,17},{9,25},{17,1},{25,9},{2,18},{10... | collective-permute-start | bytes 786440 | tf_op jit(solution)/shard_map/ppermute | solution.py:303
  7.9 0.0 collective-permute-start.2
  7.9 2.3 %pack.3 = (bf16[2,128,512]{2,1,0:T(8,128)(2,1)}, bf16[2,128,512]{2,1,0:T(8,128)(2,1)}, bf16[2,128,512]{2,1,0:T(8,128)(2,1)}, bf16[2,128,512]{2,1,0:T(8,128)(2,1)}) custom-call(s32[4]{0:T(128)} %iota_xor_fusion.order_ref.refs_0_.refs_1_, bf16[128,2048]{1,0:T(8,128)(2,1)} %first_ref.3, bf16[128,2048]{1,0:T(8,128)(2,1)} %second_ref.3), custom_call_target="tpu_custom_call" | custom-call | tf_op jit(solution)/shard_map/pack/pallas_call | solution.py:43
  10.1 0.0 copy-start.2
  10.1 2.0 %collective-permute-start.3 = (bf16[2,128,512]{2,1,0:T(8,128)(2,1)}, bf16[2,128,512]{2,1,0:T(8,128)(2,1)S(1)}, u32[]{:S(2)}, u32[]{:S(2)}) collective-permute-start(bf16[2,128,512]{2,1,0:T(8,128)(2,1)} %get-tuple-element.34), channel_id=1, source_target_pairs={{0,8},{8,0},{16,24},{24,16},{1,9},{9,1},{17,25},{25,17},{2,10},{10... | collective-permute-start | bytes 786440 | tf_op jit(solution)/shard_map/ppermute | solution.py:303
  12.1 1.5 %collective-permute-start.4 = (bf16[2,128,512]{2,1,0:T(8,128)(2,1)}, bf16[2,128,512]{2,1,0:T(8,128)(2,1)S(1)}, u32[]{:S(2)}, u32[]{:S(2)}) collective-permute-start(bf16[2,128,512]{2,1,0:T(8,128)(2,1)} %get-tuple-element.35), channel_id=1, source_target_pairs={{0,16},{8,24},{16,0},{24,8},{1,17},{9,25},{17,1},{25,9},{2,18},{10... | collective-permute-start | bytes 786440 | tf_op jit(solution)/shard_map/ppermute | solution.py:303
  13.6 0.1 collective-permute-done.refs_4_.refs_3_
  13.7 3.0 %collective-permute-start.5 = (bf16[2,128,512]{2,1,0:T(8,128)(2,1)}, bf16[2,128,512]{2,1,0:T(8,128)(2,1)S(1)}, u32[]{:S(2)}, u32[]{:S(2)}) collective-permute-start(bf16[2,128,512]{2,1,0:T(8,128)(2,1)} %get-tuple-element.36), channel_id=1, source_target_pairs={{0,24},{8,16},{16,8},{24,0},{1,25},{9,17},{17,9},{25,1},{2,26},{10... | collective-permute-start | bytes 786440 | tf_op jit(solution)/shard_map/ppermute | solution.py:303
  16.7 4.2 %collective-permute-done.1.refs_5_.refs_4_ = bf16[2,128,512]{2,1,0:T(8,128)(2,1)S(1)} collective-permute-done((bf16[2,128,512]{2,1,0:T(8,128)(2,1)}, bf16[2,128,512]{2,1,0:T(8,128)(2,1)S(1)}, u32[]{:S(2)}, u32[]{:S(2)}) %collective-permute-start.1) | collective-permute-done | bytes 262176 | tf_op jit(solution)/shard_map/ppermute | solution.py:303
  20.9 0.0 collective-permute-done.2.refs_6_.refs_5_
  20.9 0.0 copy-start.1
  20.9 0.0 copy-start.4
  20.9 2.1 %pad_maximum_fusion = bf16[4,2,128,512]{3,2,1,0:T(8,128)(2,1)} fusion(bf16[1,2,128,512]{3,2,1,0:T(8,128)(2,1)S(1)} %bitcast.13, bf16[1,2,128,512]{3,2,1,0:T(8,128)(2,1)S(1)} %bitcast.12, bf16[1,2,128,512]{3,2,1,0:T(8,128)(2,1)S(1)} %bitcast.11, bf16[1,2,128,512]{3,2,1,0:T(8,128)(2,1)} %bitcast.10), kind=kLoop, calls=%fused_computation | loop fusion | flops 1572864 | bytes 2097152 | tf_op jit(solution)/shard_map/stack | solution.py:315
  23.1 2.3 %collective-permute-start.6 = (bf16[4,2,128,512]{3,2,1,0:T(8,128)(2,1)}, bf16[4,2,128,512]{3,2,1,0:T(8,128)(2,1)}, u32[]{:S(2)}, u32[]{:S(2)}) collective-permute-start(bf16[4,2,128,512]{3,2,1,0:T(8,128)(2,1)} %pad_maximum_fusion), channel_id=1, source_target_pairs={{0,1},{1,2},{2,3},{3,4},{4,5},{5,6},{6,7},{8,9},{9,10},{10,11},{11... | collective-permute-start | bytes 3145736 | tf_op jit(solution)/shard_map/ppermute | solution.py:297
  25.3 1.3 %collective-permute-start.7 = (bf16[4,2,128,512]{3,2,1,0:T(8,128)(2,1)}, bf16[4,2,128,512]{3,2,1,0:T(8,128)(2,1)}, u32[]{:S(2)}, u32[]{:S(2)}) collective-permute-start(bf16[4,2,128,512]{3,2,1,0:T(8,128)(2,1)} %pad_maximum_fusion), channel_id=1, source_target_pairs={{1,0},{2,1},{3,2},{4,3},{5,4},{6,5},{7,6},{9,8},{10,9},{11,10},{12... | collective-permute-start | bytes 3145736 | tf_op jit(solution)/shard_map/ppermute | solution.py:297
  26.6 0.0 collective-permute-done.3.refs_8_
  26.6 4.6 %collective-permute-done.4.refs_9_ = bf16[2,128,512]{2,1,0:T(8,128)(2,1)S(1)} collective-permute-done((bf16[2,128,512]{2,1,0:T(8,128)(2,1)}, bf16[2,128,512]{2,1,0:T(8,128)(2,1)S(1)}, u32[]{:S(2)}, u32[]{:S(2)}) %collective-permute-start.4) | collective-permute-done | bytes 262176 | tf_op jit(solution)/shard_map/ppermute | solution.py:303
  31.2 0.0 collective-permute-done.5.refs_10_
  31.2 0.0 copy-done.2
  31.2 1.1 %pad_maximum_fusion.1 = bf16[4,2,128,512]{3,2,1,0:T(8,128)(2,1)} fusion(bf16[1,2,128,512]{3,2,1,0:T(8,128)(2,1)S(1)} %bitcast.17, bf16[1,2,128,512]{3,2,1,0:T(8,128)(2,1)S(1)} %bitcast.16, bf16[1,2,128,512]{3,2,1,0:T(8,128)(2,1)S(1)} %bitcast.15, bf16[1,2,128,512]{3,2,1,0:T(8,128)(2,1)S(1)} %bitcast.14), kind=kLoop, calls=%fused_computation.1 | loop fusion | flops 1572864 | bytes 2097152 | tf_op jit(solution)/shard_map/stack | solution.py:315
  32.3 1.3 %collective-permute-start.11 = (bf16[4,2,128,512]{3,2,1,0:T(8,128)(2,1)}, bf16[4,2,128,512]{3,2,1,0:T(8,128)(2,1)S(1)}, u32[]{:S(2)}, u32[]{:S(2)}) collective-permute-start(bf16[4,2,128,512]{3,2,1,0:T(8,128)(2,1)} %pad_maximum_fusion.1), channel_id=1, source_target_pairs={{0,1},{1,2},{2,3},{3,4},{4,5},{5,6},{6,7},{8,9},{9,10},{10,11},{11... | collective-permute-start | bytes 3145736 | tf_op jit(solution)/shard_map/ppermute | solution.py:297
  33.6 1.3 %collective-permute-start.12 = (bf16[4,2,128,512]{3,2,1,0:T(8,128)(2,1)}, bf16[4,2,128,512]{3,2,1,0:T(8,128)(2,1)}, u32[]{:S(2)}, u32[]{:S(2)}) collective-permute-start(bf16[4,2,128,512]{3,2,1,0:T(8,128)(2,1)} %pad_maximum_fusion.1), channel_id=1, source_target_pairs={{1,0},{2,1},{3,2},{4,3},{5,4},{6,5},{7,6},{9,8},{10,9},{11,10},{12... | collective-permute-start | bytes 3145736 | tf_op jit(solution)/shard_map/ppermute | solution.py:297
  34.9 0.1 pad_add_fusion.refs_2_
  35.0 0.0 collective-permute-done.6.refs_11_
  35.0 0.0 collective-permute-done.7.refs_12_
  35.0 0.0 copy-done.1
  35.0 0.0 copy-done.4
  35.0 12.4 %query_part.1 = (bf16[128,512]{1,0:T(8,128)(2,1)S(1)}, bf16[128,512]{1,0:T(8,128)(2,1)S(1)}, bf16[128,512]{1,0:T(8,128)(2,1)S(1)}, bf16[128,512]{1,0:T(8,128)(2,...) custom-call(s32[4]{0:T(128)S(1)} %copy-done.4, s32[4]{0:T(128)S(1)} %copy-done.4, ...), custom_call_target="tpu_custom_call" | custom-call | flops 3355443200 | bytes 3145728 | tf_op jit(solution)/shard_map/query_part/pallas_call | solution.py:187
  47.5 0.0 copy-start.3
  47.5 0.6 copy-done.3
  48.1 9.9 %collective-permute-start.13 = (f32[4,2,512]{2,1,0:T(2,128)S(1)}, f32[4,2,512]{2,1,0:T(2,128)S(1)}, u32[]{:S(2)}, u32[]{:S(2)}) collective-permute-start(f32[4,2,512]{2,1,0:T(2,128)S(1)} %get-tuple-element.41), channel_id=1, source_target_pairs={{0,1},{1,2},{2,3},{3,4},{4,5},{5,6},{6,7},{8,9},{9,10},{10,11},{11... | collective-permute-start | bytes 49160 | tf_op jit(solution)/shard_map/ppermute | solution.py:297
  58.1 1.3 %collective-permute-start.14 = (f32[4,2,512]{2,1,0:T(2,128)S(1)}, f32[4,2,512]{2,1,0:T(2,128)S(1)}, u32[]{:S(2)}, u32[]{:S(2)}) collective-permute-start(f32[4,2,512]{2,1,0:T(2,128)S(1)} %get-tuple-element.41), channel_id=1, source_target_pairs={{1,0},{2,1},{3,2},{4,3},{5,4},{6,5},{7,6},{9,8},{10,9},{11,10},{12... | collective-permute-start | bytes 49160 | tf_op jit(solution)/shard_map/ppermute | solution.py:297
  59.4 1.5 %collective-permute-start.8 = (bf16[128,512]{1,0:T(8,128)(2,1)S(1)}, bf16[128,512]{1,0:T(8,128)(2,1)S(1)}, u32[]{:S(2)}, u32[]{:S(2)}) collective-permute-start(bf16[128,512]{1,0:T(8,128)(2,1)S(1)} %get-tuple-element.38), channel_id=1, source_target_pairs={{0,8},{8,0},{16,24},{24,16},{1,9},{9,1},{17,25},{25,17},{2,10},{10... | collective-permute-start | bytes 393224 | tf_op jit(solution)/shard_map/ppermute | solution.py:303
  60.9 0.0 collective-permute-done.11.refs_6_
  60.9 0.7 collective-permute-start.9
  61.5 0.0 collective-permute-done.12.refs_7_
  61.6 1.4 %collective-permute-start.10 = (bf16[128,512]{1,0:T(8,128)(2,1)S(1)}, bf16[128,512]{1,0:T(8,128)(2,1)S(1)}, u32[]{:S(2)}, u32[]{:S(2)}) collective-permute-start(bf16[128,512]{1,0:T(8,128)(2,1)S(1)} %get-tuple-element.40), channel_id=1, source_target_pairs={{0,24},{8,16},{16,8},{24,0},{1,25},{9,17},{17,9},{25,1},{2,26},{10... | collective-permute-start | bytes 393224 | tf_op jit(solution)/shard_map/ppermute | solution.py:303
  63.0 0.0 collective-permute-done.13.refs_8_
  63.0 0.0 collective-permute-done.14.refs_9_
  63.0 8.5 %key_part.1 = (bf16[2,128,512]{2,1,0:T(8,128)(2,1)S(1)}, bf16[2,128,512]{2,1,0:T(8,128)(2,1)S(1)}, bf16[2,128,512]{2,1,0:T(8,128)(2,1)S(1)}, bf16[2,128,512]{2,1,0:T(8,128)(2,1)S(1)}) custom-call(s32[4]{0:T(128)S(1)} %copy-done.4, s32[4]{0:T(128)S(1)} %copy-done.4, bf16[2,128,512]{2,1,0:T(8,128)(2,1)S(1)} %copy-done.1, ...), custom_call_target="tpu_custom_call" | custom-call | flops 1610612736 | bytes 6291456 | tf_op jit(solution)/shard_map/key_part/pallas_call | solution.py:272
  71.5 0.0 copy-start
  71.5 0.7 copy-done
  72.2 0.0 collective-permute-done.8.refs_1_
  72.2 0.0 collective-permute-done.9.refs_2_
  72.2 0.0 copy-start.9
  72.2 0.0 collective-permute-done.10.refs_3_
  72.2 0.0 copy-start.10
  72.2 1.4 %collective-permute-start.15 = (bf16[2,128,512]{2,1,0:T(8,128)(2,1)S(1)}, bf16[2,128,512]{2,1,0:T(8,128)(2,1)S(1)}, u32[]{:S(2)}, u32[]{:S(2)}) collective-permute-start(bf16[2,128,512]{2,1,0:T(8,128)(2,1)S(1)} %get-tuple-element.52), channel_id=1, source_target_pairs={{0,8},{8,0},{16,24},{24,16},{1,9},{9,1},{17,25},{25,17},{2,10},{10... | collective-permute-start | bytes 786440 | tf_op jit(solution)/shard_map/ppermute | solution.py:303
  73.6 0.7 collective-permute-start.16
  74.3 1.4 %collective-permute-start.17 = (bf16[2,128,512]{2,1,0:T(8,128)(2,1)S(1)}, bf16[2,128,512]{2,1,0:T(8,128)(2,1)S(1)}, u32[]{:S(2)}, u32[]{:S(2)}) collective-permute-start(bf16[2,128,512]{2,1,0:T(8,128)(2,1)S(1)} %get-tuple-element.54), channel_id=1, source_target_pairs={{0,24},{8,16},{16,8},{24,0},{1,25},{9,17},{17,9},{25,1},{2,26},{10... | collective-permute-start | bytes 786440 | tf_op jit(solution)/shard_map/ppermute | solution.py:303
  75.8 5.6 %collective-permute-done.15.refs_5_ = bf16[2,128,512]{2,1,0:T(8,128)(2,1)S(1)} collective-permute-done((bf16[2,128,512]{2,1,0:T(8,128)(2,1)S(1)}, bf16[2,128,512]{2,1,0:T(8,128)(2,1)S(1)}, u32[]{:S(2)}, u32[]{:S(2)}) %collective-permute-start.15) | collective-permute-done | bytes 262176 | tf_op jit(solution)/shard_map/ppermute | solution.py:303
  81.4 4.9 %collective-permute-done.16.refs_6_ = bf16[2,128,512]{2,1,0:T(8,128)(2,1)S(1)} collective-permute-done((bf16[2,128,512]{2,1,0:T(8,128)(2,1)S(1)}, bf16[2,128,512]{2,1,0:T(8,128)(2,1)S(1)}, u32[]{:S(2)}, u32[]{:S(2)}) %collective-permute-start.16) | collective-permute-done | bytes 262176 | tf_op jit(solution)/shard_map/ppermute | solution.py:303
  86.3 1.8 %collective-permute-done.17.refs_7_ = bf16[2,128,512]{2,1,0:T(8,128)(2,1)S(1)} collective-permute-done((bf16[2,128,512]{2,1,0:T(8,128)(2,1)S(1)}, bf16[2,128,512]{2,1,0:T(8,128)(2,1)S(1)}, u32[]{:S(2)}, u32[]{:S(2)}) %collective-permute-start.17) | collective-permute-done | bytes 262176 | tf_op jit(solution)/shard_map/ppermute | solution.py:303
  88.1 0.0 copy-done.8
  88.1 0.0 copy-done.9
  88.1 0.0 copy-done.10
  88.1 0.0 copy-done.5
  88.1 0.0 copy-done.6
  88.1 0.0 copy-start.7
  88.1 0.7 copy-done.7
  88.8 2.6 %merge.1 = (bf16[128,2048]{1,0:T(8,128)(2,1)}, bf16[128,2048]{1,0:T(8,128)(2,1)}, bf16[128,2048]{1,0:T(8,128)(2,1)}) custom-call(s32[4]{0:T(128)} %iota_xor_fusion.order_ref.refs_0_.refs_1_, bf16[128,512]{1,0:T(8,128)(2,1)} %copy-done.3, bf16[128,512]{1,0:T(8,128)(2,1)} %copy-done.8, bf16[128,512]{1,0:T(8,128)(2,1)} %copy-done.9, ...), custom_call_target="tpu_custom_call" | custom-call | tf_op jit(solution)/shard_map/merge/pallas_call | solution.py:67
  (3 shorter events, 0.0 us)
Async XLA Ops:
  3.4 10.3 %collective-permute-start = (bf16[2,128,512]{2,1,0:T(8,128)(2,1)}, bf16[2,128,512]{2,1,0:T(8,128)(2,1)S(1)}, u32[]{:S(2)}, u32[]{:S(2)}) collective-permute-start(bf16[2,128,512]{2,1,0:T(8,128)(2,1)} %get-tuple-element.30), channel_id=1, source_target_pairs={{0,8},{8,0},{16,24},{24,16},{1,9},{9,1},{17,25},{25,17},{2,10},{10... | collective-permute-start | bytes 786440 | tf_op jit(solution)/shard_map/ppermute | solution.py:303
  6.3 14.6 %collective-permute-start.1 = (bf16[2,128,512]{2,1,0:T(8,128)(2,1)}, bf16[2,128,512]{2,1,0:T(8,128)(2,1)S(1)}, u32[]{:S(2)}, u32[]{:S(2)}) collective-permute-start(bf16[2,128,512]{2,1,0:T(8,128)(2,1)} %get-tuple-element.31), channel_id=1, source_target_pairs={{0,16},{8,24},{16,0},{24,8},{1,17},{9,25},{17,1},{25,9},{2,18},{10... | collective-permute-start | bytes 786440 | tf_op jit(solution)/shard_map/ppermute | solution.py:303
  7.9 13.1 %collective-permute-start.2 = (bf16[2,128,512]{2,1,0:T(8,128)(2,1)}, bf16[2,128,512]{2,1,0:T(8,128)(2,1)S(1)}, u32[]{:S(2)}, u32[]{:S(2)}) collective-permute-start(bf16[2,128,512]{2,1,0:T(8,128)(2,1)} %get-tuple-element.32), channel_id=1, source_target_pairs={{0,24},{8,16},{16,8},{24,0},{1,25},{9,17},{17,9},{25,1},{2,26},{10... | collective-permute-start | bytes 786440 | tf_op jit(solution)/shard_map/ppermute | solution.py:303
  10.1 21.0 %copy-start.2 = (bf16[2,128,512]{2,1,0:T(8,128)(2,1)S(1)}, bf16[2,128,512]{2,1,0:T(8,128)(2,1)}, u32[]{:S(2)}) copy-start(bf16[2,128,512]{2,1,0:T(8,128)(2,1)} %get-tuple-element.33.refs_7_) | copy-start | bytes 786436
  10.1 16.5 %collective-permute-start.3 = (bf16[2,128,512]{2,1,0:T(8,128)(2,1)}, bf16[2,128,512]{2,1,0:T(8,128)(2,1)S(1)}, u32[]{:S(2)}, u32[]{:S(2)}) collective-permute-start(bf16[2,128,512]{2,1,0:T(8,128)(2,1)} %get-tuple-element.34), channel_id=1, source_target_pairs={{0,8},{8,0},{16,24},{24,16},{1,9},{9,1},{17,25},{25,17},{2,10},{10... | collective-permute-start | bytes 786440 | tf_op jit(solution)/shard_map/ppermute | solution.py:303
  12.1 19.1 %collective-permute-start.4 = (bf16[2,128,512]{2,1,0:T(8,128)(2,1)}, bf16[2,128,512]{2,1,0:T(8,128)(2,1)S(1)}, u32[]{:S(2)}, u32[]{:S(2)}) collective-permute-start(bf16[2,128,512]{2,1,0:T(8,128)(2,1)} %get-tuple-element.35), channel_id=1, source_target_pairs={{0,16},{8,24},{16,0},{24,8},{1,17},{9,25},{17,1},{25,9},{2,18},{10... | collective-permute-start | bytes 786440 | tf_op jit(solution)/shard_map/ppermute | solution.py:303
  13.7 17.5 %collective-permute-start.5 = (bf16[2,128,512]{2,1,0:T(8,128)(2,1)}, bf16[2,128,512]{2,1,0:T(8,128)(2,1)S(1)}, u32[]{:S(2)}, u32[]{:S(2)}) collective-permute-start(bf16[2,128,512]{2,1,0:T(8,128)(2,1)} %get-tuple-element.36), channel_id=1, source_target_pairs={{0,24},{8,16},{16,8},{24,0},{1,25},{9,17},{17,9},{25,1},{2,26},{10... | collective-permute-start | bytes 786440 | tf_op jit(solution)/shard_map/ppermute | solution.py:303
  20.9 14.1 %copy-start.1 = (bf16[2,128,512]{2,1,0:T(8,128)(2,1)S(1)}, bf16[2,128,512]{2,1,0:T(8,128)(2,1)}, u32[]{:S(2)}) copy-start(bf16[2,128,512]{2,1,0:T(8,128)(2,1)} %get-tuple-element.29.refs_3_.refs_2_) | copy-start | bytes 786436
  20.9 14.1 %copy-start.4 = (s32[4]{0:T(128)S(1)}, s32[4]{0:T(128)}, u32[]{:S(2)}) copy-start(s32[4]{0:T(128)} %iota_xor_fusion.order_ref.refs_0_.refs_1_) | copy-start | bytes 52
  23.1 12.0 %collective-permute-start.6 = (bf16[4,2,128,512]{3,2,1,0:T(8,128)(2,1)}, bf16[4,2,128,512]{3,2,1,0:T(8,128)(2,1)}, u32[]{:S(2)}, u32[]{:S(2)}) collective-permute-start(bf16[4,2,128,512]{3,2,1,0:T(8,128)(2,1)} %pad_maximum_fusion), channel_id=1, source_target_pairs={{0,1},{1,2},{2,3},{3,4},{4,5},{5,6},{6,7},{8,9},{9,10},{10,11},{11... | collective-permute-start | bytes 3145736 | tf_op jit(solution)/shard_map/ppermute | solution.py:297
  25.3 9.7 %collective-permute-start.7 = (bf16[4,2,128,512]{3,2,1,0:T(8,128)(2,1)}, bf16[4,2,128,512]{3,2,1,0:T(8,128)(2,1)}, u32[]{:S(2)}, u32[]{:S(2)}) collective-permute-start(bf16[4,2,128,512]{3,2,1,0:T(8,128)(2,1)} %pad_maximum_fusion), channel_id=1, source_target_pairs={{1,0},{2,1},{3,2},{4,3},{5,4},{6,5},{7,6},{9,8},{10,9},{11,10},{12... | collective-permute-start | bytes 3145736 | tf_op jit(solution)/shard_map/ppermute | solution.py:297
  32.3 28.6 %collective-permute-start.11 = (bf16[4,2,128,512]{3,2,1,0:T(8,128)(2,1)}, bf16[4,2,128,512]{3,2,1,0:T(8,128)(2,1)S(1)}, u32[]{:S(2)}, u32[]{:S(2)}) collective-permute-start(bf16[4,2,128,512]{3,2,1,0:T(8,128)(2,1)} %pad_maximum_fusion.1), channel_id=1, source_target_pairs={{0,1},{1,2},{2,3},{3,4},{4,5},{5,6},{6,7},{8,9},{9,10},{10,11},{11... | collective-permute-start | bytes 3145736 | tf_op jit(solution)/shard_map/ppermute | solution.py:297
  33.6 27.9 %collective-permute-start.12 = (bf16[4,2,128,512]{3,2,1,0:T(8,128)(2,1)}, bf16[4,2,128,512]{3,2,1,0:T(8,128)(2,1)}, u32[]{:S(2)}, u32[]{:S(2)}) collective-permute-start(bf16[4,2,128,512]{3,2,1,0:T(8,128)(2,1)} %pad_maximum_fusion.1), channel_id=1, source_target_pairs={{1,0},{2,1},{3,2},{4,3},{5,4},{6,5},{7,6},{9,8},{10,9},{11,10},{12... | collective-permute-start | bytes 3145736 | tf_op jit(solution)/shard_map/ppermute | solution.py:297
  47.5 0.6 copy-start.3
  48.1 14.9 %collective-permute-start.13 = (f32[4,2,512]{2,1,0:T(2,128)S(1)}, f32[4,2,512]{2,1,0:T(2,128)S(1)}, u32[]{:S(2)}, u32[]{:S(2)}) collective-permute-start(f32[4,2,512]{2,1,0:T(2,128)S(1)} %get-tuple-element.41), channel_id=1, source_target_pairs={{0,1},{1,2},{2,3},{3,4},{4,5},{5,6},{6,7},{8,9},{9,10},{10,11},{11... | collective-permute-start | bytes 49160 | tf_op jit(solution)/shard_map/ppermute | solution.py:297
  58.1 4.9 %collective-permute-start.14 = (f32[4,2,512]{2,1,0:T(2,128)S(1)}, f32[4,2,512]{2,1,0:T(2,128)S(1)}, u32[]{:S(2)}, u32[]{:S(2)}) collective-permute-start(f32[4,2,512]{2,1,0:T(2,128)S(1)} %get-tuple-element.41), channel_id=1, source_target_pairs={{1,0},{2,1},{3,2},{4,3},{5,4},{6,5},{7,6},{9,8},{10,9},{11,10},{12... | collective-permute-start | bytes 49160 | tf_op jit(solution)/shard_map/ppermute | solution.py:297
  59.4 12.8 %collective-permute-start.8 = (bf16[128,512]{1,0:T(8,128)(2,1)S(1)}, bf16[128,512]{1,0:T(8,128)(2,1)S(1)}, u32[]{:S(2)}, u32[]{:S(2)}) collective-permute-start(bf16[128,512]{1,0:T(8,128)(2,1)S(1)} %get-tuple-element.38), channel_id=1, source_target_pairs={{0,8},{8,0},{16,24},{24,16},{1,9},{9,1},{17,25},{25,17},{2,10},{10... | collective-permute-start | bytes 393224 | tf_op jit(solution)/shard_map/ppermute | solution.py:303
  60.9 11.3 %collective-permute-start.9 = (bf16[128,512]{1,0:T(8,128)(2,1)S(1)}, bf16[128,512]{1,0:T(8,128)(2,1)S(1)}, u32[]{:S(2)}, u32[]{:S(2)}) collective-permute-start(bf16[128,512]{1,0:T(8,128)(2,1)S(1)} %get-tuple-element.39), channel_id=1, source_target_pairs={{0,16},{8,24},{16,0},{24,8},{1,17},{9,25},{17,1},{25,9},{2,18},{10... | collective-permute-start | bytes 393224 | tf_op jit(solution)/shard_map/ppermute | solution.py:303
  61.6 10.6 %collective-permute-start.10 = (bf16[128,512]{1,0:T(8,128)(2,1)S(1)}, bf16[128,512]{1,0:T(8,128)(2,1)S(1)}, u32[]{:S(2)}, u32[]{:S(2)}) collective-permute-start(bf16[128,512]{1,0:T(8,128)(2,1)S(1)} %get-tuple-element.40), channel_id=1, source_target_pairs={{0,24},{8,16},{16,8},{24,0},{1,25},{9,17},{17,9},{25,1},{2,26},{10... | collective-permute-start | bytes 393224 | tf_op jit(solution)/shard_map/ppermute | solution.py:303
  71.5 0.7 copy-start
  72.2 15.9 %copy-start.8 = (bf16[128,512]{1,0:T(8,128)(2,1)}, bf16[128,512]{1,0:T(8,128)(2,1)S(1)}, u32[]{:S(2)}) copy-start(bf16[128,512]{1,0:T(8,128)(2,1)S(1)} %collective-permute-done.8.refs_1_) | copy-start | bytes 393220
  72.2 15.9 %copy-start.9 = (bf16[128,512]{1,0:T(8,128)(2,1)}, bf16[128,512]{1,0:T(8,128)(2,1)S(1)}, u32[]{:S(2)}) copy-start(bf16[128,512]{1,0:T(8,128)(2,1)S(1)} %collective-permute-done.9.refs_2_) | copy-start | bytes 393220
  72.2 15.9 %copy-start.10 = (bf16[128,512]{1,0:T(8,128)(2,1)}, bf16[128,512]{1,0:T(8,128)(2,1)S(1)}, u32[]{:S(2)}) copy-start(bf16[128,512]{1,0:T(8,128)(2,1)S(1)} %collective-permute-done.10.refs_3_) | copy-start | bytes 393220
  72.2 9.2 %collective-permute-start.15 = (bf16[2,128,512]{2,1,0:T(8,128)(2,1)S(1)}, bf16[2,128,512]{2,1,0:T(8,128)(2,1)S(1)}, u32[]{:S(2)}, u32[]{:S(2)}) collective-permute-start(bf16[2,128,512]{2,1,0:T(8,128)(2,1)S(1)} %get-tuple-element.52), channel_id=1, source_target_pairs={{0,8},{8,0},{16,24},{24,16},{1,9},{9,1},{17,25},{25,17},{2,10},{10... | collective-permute-start | bytes 786440 | tf_op jit(solution)/shard_map/ppermute | solution.py:303
  73.6 12.6 %collective-permute-start.16 = (bf16[2,128,512]{2,1,0:T(8,128)(2,1)S(1)}, bf16[2,128,512]{2,1,0:T(8,128)(2,1)S(1)}, u32[]{:S(2)}, u32[]{:S(2)}) collective-permute-start(bf16[2,128,512]{2,1,0:T(8,128)(2,1)S(1)} %get-tuple-element.53), channel_id=1, source_target_pairs={{0,16},{8,24},{16,0},{24,8},{1,17},{9,25},{17,1},{25,9},{2,18},{10... | collective-permute-start | bytes 786440 | tf_op jit(solution)/shard_map/ppermute | solution.py:303
  74.3 13.8 %collective-permute-start.17 = (bf16[2,128,512]{2,1,0:T(8,128)(2,1)S(1)}, bf16[2,128,512]{2,1,0:T(8,128)(2,1)S(1)}, u32[]{:S(2)}, u32[]{:S(2)}) collective-permute-start(bf16[2,128,512]{2,1,0:T(8,128)(2,1)S(1)} %get-tuple-element.54), channel_id=1, source_target_pairs={{0,24},{8,16},{16,8},{24,0},{1,25},{9,17},{17,9},{25,1},{2,26},{10... | collective-permute-start | bytes 786440 | tf_op jit(solution)/shard_map/ppermute | solution.py:303
  81.4 6.7 %copy-start.5 = (bf16[2,128,512]{2,1,0:T(8,128)(2,1)}, bf16[2,128,512]{2,1,0:T(8,128)(2,1)S(1)}, u32[]{:S(2)}) copy-start(bf16[2,128,512]{2,1,0:T(8,128)(2,1)S(1)} %collective-permute-done.15.refs_5_) | copy-start | bytes 786436
  86.3 1.8 %copy-start.6 = (bf16[2,128,512]{2,1,0:T(8,128)(2,1)}, bf16[2,128,512]{2,1,0:T(8,128)(2,1)S(1)}, u32[]{:S(2)}) copy-start(bf16[2,128,512]{2,1,0:T(8,128)(2,1)S(1)} %collective-permute-done.16.refs_6_) | copy-start | bytes 786436
  88.1 0.7 copy-start.7

commit v3 on v2

v3 whole, which is shorter than its diff:
```python
import math

import jax
import jax.numpy as jnp
from jax import lax
from jax.experimental import pallas as pl
from jax.experimental.pallas import tpu as pltpu
from jax.sharding import PartitionSpec as P

HEADS = 16
HEAD_DIM = 128
HALF = 512
TILE = 512
SUB = 256
SPAN = SUB + 2 * HALF
CHUNKS = SPAN // SUB
NEG = -1e30
STRIP = 64
SCALE = HEAD_DIM ** -0.5
RATE = SCALE * math.log2(math.e)
VMEM_BYTES = 24 * 1024 * 1024
SMALL_BYTES = 8 * 1024 * 1024


def dot(a, b, contract):
    return lax.dot_general(
        a, b, ((contract[:1], contract[1:]), ((), ())), preferred_element_type=jnp.float32
    )


def rows_at(start, size):
    return pl.ds(pl.multiple_of(start, size), size)


def pack_kernel(*refs):
    ins, outs, sems = refs[:2], refs[2:-1], refs[-1]
    n = len(outs)
    width = outs[0].shape[2]
    me = lax.axis_index("head")
    copies = []
    for k, out in enumerate(outs):
        columns = pl.ds(pl.multiple_of((me ^ k) * width, 128), width)
        for which in range(2):
            copies.append(
                pltpu.make_async_copy(ins[which].at[:, columns], out.at[which], sems.at[2 * k + which])
            )
    for copy in copies:
        copy.start()
    for copy in copies:
        copy.wait()


def packed(n, first, second):
    r, width = first.shape[0], first.shape[1] // n
    return pl.pallas_call(
        pack_kernel,
        in_specs=[pl.BlockSpec(memory_space=pl.ANY)] * 2,
        out_specs=[pl.BlockSpec(memory_space=pltpu.VMEM)] * n,
        out_shape=[jax.ShapeDtypeStruct((2, r, width), first.dtype)] * n,
        scratch_shapes=[pltpu.SemaphoreType.DMA((2 * n,))],
        compiler_params=pltpu.CompilerParams(vmem_limit_bytes=SMALL_BYTES),
        name="pack",
    )(first, second)


def merge_kernel(n, *refs):
    ins, outs, sems = refs[:n], refs[n:-1], refs[-1]
    width = ins[0].shape[-1]
    me = lax.axis_index("head")
    copies = []
    for k in range(n):
        columns = pl.ds(pl.multiple_of((me ^ k) * width, 128), width)
        for which, out in enumerate(outs):
            source = ins[k] if len(outs) == 1 else ins[k].at[which]
            copies.append(
                pltpu.make_async_copy(source, out.at[:, columns], sems.at[len(outs) * k + which])
            )
    for copy in copies:
        copy.start()
    for copy in copies:
        copy.wait()


def merged(pieces):
    n = len(pieces)
    r, width = pieces[0].shape[-2:]
    count = 1 if pieces[0].ndim == 2 else 2
    return pl.pallas_call(
        lambda *refs: merge_kernel(n, *refs),
        in_specs=[pl.BlockSpec(memory_space=pltpu.VMEM)] * n,
        out_specs=[pl.BlockSpec(memory_space=pl.ANY)] * count,
        out_shape=[jax.ShapeDtypeStruct((r, n * width), pieces[0].dtype)] * count,
        scratch_shapes=[pltpu.SemaphoreType.DMA((count * n,))],
        compiler_params=pltpu.CompilerParams(vmem_limit_bytes=SMALL_BYTES),
        name="merge",
    )(*pieces)


def ahead_by(turn_ref):
    return (
        lax.broadcasted_iota(jnp.int32, (SUB, SUB), 0)
        - lax.broadcasted_iota(jnp.int32, (SUB, SUB), 1)
    ) * turn_ref[0]


def query_kernel(n, place_ref, halo_ref, turn_ref, *refs):
    kv_refs, refs = refs[:n], refs[n:]
    qd_refs, refs = refs[:n], refs[n:]
    far_ref, near_ref = refs[:2]
    dq_refs, refs = refs[2:2 + n], refs[2 + n:]
    stat_ref, part_ref, give_ref, k_ext, v_ext, k_flip, q_all, g_all, dq_all = refs[:9]
    s_buf, p_buf, w_buf, d_buf = refs[9:13]
    r, width = kv_refs[0].shape[1:]
    rows = n * r
    tiles = rows // TILE
    ahead = ahead_by(turn_ref)

    def each_head(h, _):
        lanes = rows_at(h * HEAD_DIM, HEAD_DIM)
        for i in range(HALF // r):
            at = halo_ref[i] * r
            for which, ext in ((0, k_ext), (1, v_ext)):
                ext[rows_at(at, r)] = far_ref[i, which, :, lanes]
                ext[rows_at(HALF + rows + at, r)] = near_ref[i, which, :, lanes]
        for k in range(n):
            at = place_ref[k] * r
            for which, ext in ((0, k_ext), (1, v_ext)):
                ext[rows_at(HALF + at, r)] = kv_refs[k][which, :, lanes]
            q_all[rows_at(at, r)] = qd_refs[k][0, :, lanes]
            g_all[rows_at(at, r)] = qd_refs[k][1, :, lanes]
        k_flip[...] = k_ext[...].T
        if tiles > 1:
            refs[13][...] = jnp.zeros_like(refs[13])

        def each_tile(tile):
            first = tile * TILE
            has_far = turn_ref[1] > 0
            if tiles > 1:
                has_far = jnp.logical_or(has_far, tile > 0)

            def products(sub):
                here = rows_at(first + sub * SUB, SUB)
                query, grad = q_all[here], g_all[here]
                top = jnp.full((8, SUB), NEG, jnp.float32)
                for c in range(CHUNKS):
                    at = slice(c * SUB, (c + 1) * SUB)
                    keys = rows_at(first + (sub + c) * SUB, SUB)
                    s = dot(k_ext[keys], query, (1, 1)) * RATE
                    keep = None
                    if c == 0:
                        keep = ahead >= 0
                    if c == CHUNKS - 1:
                        keep = ahead <= 0
                    if sub + c < HALF // SUB:
                        keep = has_far if keep is None else jnp.logical_and(keep, has_far)
                    if keep is not None:
                        s = jnp.where(keep, s, NEG)
                    s_buf[sub, at] = s
                    top = jnp.maximum(top, jnp.max(s.reshape(SUB // 8, 8, SUB), axis=0))
                for c in range(CHUNKS):
                    at = slice(c * SUB, (c + 1) * SUB)
                    keys = rows_at(first + (sub + c) * SUB, SUB)
                    p_buf[sub, at] = dot(v_ext[keys], grad, (1, 1))
                return jnp.max(top, axis=0, keepdims=True)

            def softmax(sub, top):
                here = rows_at(first + sub * SUB, SUB)
                total = jnp.zeros((8, SUB), jnp.float32)
                delta = jnp.zeros((8, SUB), jnp.float32)
                for i in range(0, SPAN, STRIP):
                    at = slice(i, i + STRIP)
                    e = jnp.exp2(s_buf[sub, at] - top)
                    s_buf[sub, at] = e
                    total += jnp.sum(e.reshape(STRIP // 8, 8, SUB), axis=0)
                    delta += jnp.sum((e * p_buf[sub, at]).reshape(STRIP // 8, 8, SUB), axis=0)
                total = jnp.sum(total, axis=0, keepdims=True)
                inverse = 1.0 / total
                delta = jnp.sum(delta, axis=0, keepdims=True) * inverse
                stat_ref[h, 0:1, here] = top + jnp.log2(total)
                stat_ref[h, 1:2, here] = delta
                mine = slice(sub * SUB, (sub + 1) * SUB)
                for i in range(0, SPAN, STRIP):
                    at = slice(i, i + STRIP)
                    to = slice(sub * SUB + i, sub * SUB + i + STRIP)
                    w = s_buf[sub, at] * inverse
                    w_buf[to, mine] = w.astype(jnp.bfloat16)
                    d_buf[to, mine] = (w * (p_buf[sub, at] - delta)).astype(jnp.bfloat16)

            def query_grad(sub):
                mine = slice(sub * SUB, (sub + 1) * SUB)
                span = slice(sub * SUB, sub * SUB + SPAN)
                flip = k_flip[:, rows_at(first + sub * SUB, SPAN) if tiles > 1 else span]
                dq = dot(flip, d_buf[span, mine], (1, 0))
                here = rows_at(first + sub * SUB, SUB)
                dq_all[here] = (dq * SCALE).T.astype(jnp.bfloat16)

            tops = [products(sub) for sub in range(TILE // SUB)]
            for sub in range(TILE // SUB):
                softmax(sub, tops[sub])
                query_grad(sub)
            queries, grads = q_all[rows_at(first, TILE)], g_all[rows_at(first, TILE)]
            for which, buf, right in ((0, d_buf, queries), (1, w_buf, grads)):
                if tiles > 1:
                    acc = refs[13]
                    acc[which, rows_at(first, SUB)] += dot(buf[:SUB, :SUB], right[:SUB], (1, 0))
                    acc[which, rows_at(first + SUB, SPAN - SUB)] += dot(
                        buf[SUB:SPAN], right, (1, 0)
                    )
                    acc[which, rows_at(first + SPAN, SUB)] += dot(
                        buf[SPAN:, SUB:], right[SUB:], (1, 0)
                    )
                else:
                    part_ref[which, :, lanes] = dot(buf[HALF:HALF + TILE], right, (1, 0))
                    give_ref[which, :SUB, lanes] = dot(
                        buf[HALF + TILE:SPAN], right, (1, 0)
                    ).astype(jnp.bfloat16)
                    give_ref[which, SUB:, lanes] = dot(
                        buf[SPAN:, SUB:], right[SUB:], (1, 0)
                    ).astype(jnp.bfloat16)

        if tiles > 1:
            pl.loop(0, tiles)(each_tile)
            part_ref[:, :, lanes] = refs[13][:, HALF:HALF + rows]
            give_ref[:, :, lanes] = refs[13][:, HALF + rows:].astype(jnp.bfloat16)
        else:
            each_tile(0)
        for k in range(n):
            dq_refs[k][:, lanes] = dq_all[rows_at(place_ref[k] * r, r)]
        return 0

    lax.fori_loop(0, width // HEAD_DIM, each_head, 0)


def query_part(place, halo, turn, kv, qd, far, near):
    n = len(kv)
    _, r, width = kv[0].shape
    rows = n * r
    heads = width // HEAD_DIM
    ext = rows + 2 * HALF
    here, scalars = pl.BlockSpec(memory_space=pltpu.VMEM), pl.BlockSpec(memory_space=pltpu.SMEM)
    scratch = [
        pltpu.VMEM((ext, HEAD_DIM), jnp.bfloat16),
        pltpu.VMEM((ext, HEAD_DIM), jnp.bfloat16),
        pltpu.VMEM((HEAD_DIM, ext), jnp.bfloat16),
        pltpu.VMEM((rows, HEAD_DIM), jnp.bfloat16),
        pltpu.VMEM((rows, HEAD_DIM), jnp.bfloat16),
        pltpu.VMEM((rows, HEAD_DIM), jnp.bfloat16),
        pltpu.VMEM((TILE // SUB, SPAN, SUB), jnp.float32),
        pltpu.VMEM((TILE // SUB, SPAN, SUB), jnp.float32),
        pltpu.VMEM((TILE + 2 * HALF, TILE), jnp.bfloat16),
        pltpu.VMEM((TILE + 2 * HALF, TILE), jnp.bfloat16),
    ]
    if rows != TILE:
        scratch.append(pltpu.VMEM((2, ext, HEAD_DIM), jnp.float32))
    outs = pl.pallas_call(
        lambda *refs: query_kernel(n, *refs),
        in_specs=[scalars] * 3 + [here] * (2 * n + 2),
        out_specs=[here] * (n + 3),
        scratch_shapes=scratch,
        out_shape=[jax.ShapeDtypeStruct((r, width), jnp.bfloat16)] * n
        + [
            jax.ShapeDtypeStruct((heads, 2, rows), jnp.float32),
            jax.ShapeDtypeStruct((2, rows, width), jnp.float32),
            jax.ShapeDtypeStruct((2, HALF, width), jnp.bfloat16),
        ],
        compiler_params=pltpu.CompilerParams(vmem_limit_bytes=VMEM_BYTES),
        cost_estimate=pl.CostEstimate(
            flops=10 * heads * rows * SPAN * HEAD_DIM,
            bytes_accessed=12 * rows * width,
            transcendentals=heads * rows * SPAN,
        ),
        name="query_part",
    )(place, halo, turn, *kv, *qd, far, near)
    return outs[:n], outs[n], outs[n + 1], outs[n + 2]


def key_kernel(n, place_ref, halo_ref, turn_ref, *refs):
    kv_refs, refs = refs[:n], refs[n:]
    far_ref, stat_ref, part_ref, got_ref = refs[:4]
    out_refs, (k_all, v_all, q_all, g_all, acc, w_buf, d_buf) = refs[4:4 + n], refs[4 + n:]
    r, width = kv_refs[0].shape[1:]
    rows = n * r
    ahead = ahead_by(turn_ref)
    steps = HALF // SUB

    def each_head(h, _):
        lanes = rows_at(h * HEAD_DIM, HEAD_DIM)
        for k in range(n):
            at = rows_at(place_ref[k] * r, r)
            k_all[at] = kv_refs[k][0, :, lanes]
            v_all[at] = kv_refs[k][1, :, lanes]
        for i in range(HALF // r):
            at = rows_at(halo_ref[i] * r, r)
            q_all[at] = far_ref[i, 0, :, lanes]
            g_all[at] = far_ref[i, 1, :, lanes]
        acc[...] = part_ref[:, :, lanes]
        for a in range(steps):
            at = slice(rows - HALF + a * SUB, rows - HALF + (a + 1) * SUB)
            there = slice((steps - 1 - a) * SUB, (steps - a) * SUB)
            acc[:, at] += got_ref[:, there, lanes].astype(jnp.float32)
        for b in range(steps):
            here = slice(b * SUB, (b + 1) * SUB)
            there = slice((steps - 1 - b) * SUB, (steps - b) * SUB)
            query, grad = q_all[here], g_all[here]
            log_total = stat_ref[h, 0:1, there]
            delta = stat_ref[h, 1:2, there]
            for a in range(b + 1):
                at = slice(a * SUB, (a + 1) * SUB)
                w = jnp.exp2(dot(k_all[at], query, (1, 1)) * RATE - log_total)
                if a == b:
                    w = jnp.where(ahead <= 0, w, 0.0)
                w_buf[at, here] = w.astype(jnp.bfloat16)
                ds = w * (dot(v_all[at], grad, (1, 1)) - delta)
                d_buf[at, here] = ds.astype(jnp.bfloat16)
        for which, buf, right in ((0, d_buf, q_all), (1, w_buf, g_all)):
            for a in range(steps):
                at = slice(a * SUB, (a + 1) * SUB)
                acc[which, at] += dot(buf[at, a * SUB:], right[a * SUB:], (1, 0))
        for k in range(n):
            at = rows_at(place_ref[k] * r, r)
            out_refs[k][0, :, lanes] = (acc[0, at] * SCALE).astype(jnp.bfloat16)
            out_refs[k][1, :, lanes] = acc[1, at].astype(jnp.bfloat16)
        return 0

    lax.fori_loop(0, width // HEAD_DIM, each_head, 0)


def key_part(place, halo, turn, kv, far, stat, part, got):
    n = len(kv)
    _, r, width = kv[0].shape
    rows = n * r
    heads = width // HEAD_DIM
    here, scalars = pl.BlockSpec(memory_space=pltpu.VMEM), pl.BlockSpec(memory_space=pltpu.SMEM)
    return pl.pallas_call(
        lambda *refs: key_kernel(n, *refs),
        in_specs=[scalars] * 3 + [here] * (n + 4),
        out_specs=[here] * n,
        scratch_shapes=[
            pltpu.VMEM((rows, HEAD_DIM), jnp.bfloat16),
            pltpu.VMEM((rows, HEAD_DIM), jnp.bfloat16),
            pltpu.VMEM((HALF, HEAD_DIM), jnp.bfloat16),
            pltpu.VMEM((HALF, HEAD_DIM), jnp.bfloat16),
            pltpu.VMEM((2, rows, HEAD_DIM), jnp.float32),
            pltpu.VMEM((HALF, HALF), jnp.bfloat16),
            pltpu.VMEM((HALF, HALF), jnp.bfloat16),
        ],
        out_shape=[jax.ShapeDtypeStruct((2, r, width), jnp.bfloat16)] * n,
        compiler_params=pltpu.CompilerParams(vmem_limit_bytes=VMEM_BYTES),
        cost_estimate=pl.CostEstimate(
            flops=8 * heads * HALF * (HALF // 2 + SUB // 2) * HEAD_DIM,
            bytes_accessed=24 * rows * width,
            transcendentals=heads * HALF * (HALF // 2 + SUB // 2),
        ),
        name="key_part",
    )(place, halo, turn, *kv, far, stat, part, got)


def swapped(array, first):
    count = lax.axis_size("blk")
    pairs = [(i, i + 1) for i in range(first, count - 1, 2)]
    return lax.ppermute(array, "blk", pairs + [(j, i) for i, j in pairs])


def exchanged(pieces):
    n = len(pieces)
    return [pieces[0]] + [
        lax.ppermute(pieces[k], "head", [(i, i ^ k) for i in range(n)]) for k in range(1, n)
    ]


def shards(query, key_in, value, grad_out):
    n = lax.axis_size("head")
    blocks = HALF // query.shape[0]
    index = lax.axis_index("blk").astype(jnp.int32)
    odd = index & 1
    order = lax.axis_index("head").astype(jnp.int32) ^ jnp.arange(n, dtype=jnp.int32)
    place = order ^ (odd * (n - 2))
    if n == blocks:
        halo = place
    else:
        halo = jnp.arange(blocks, dtype=jnp.int32) ^ (blocks - 2)
    has_far = jnp.logical_and(index > 0, index < lax.axis_size("blk") - 1)
    turn = jnp.stack([1 - 2 * odd, has_far.astype(jnp.int32)])

    def edge(pieces, far):
        stacked = jnp.stack(pieces)
        if n == blocks:
            return stacked
        local = jnp.take(stacked, place, axis=0)
        return local[:blocks] if far else local[n - blocks:]

    kv_own = packed(n, key_in, value)
    qd_own = packed(n, query, grad_out)
    kv = exchanged(kv_own)
    qd = exchanged(qd_own)
    kv, qd_own = lax.optimization_barrier((kv, qd_own))
    kv_far = swapped(edge(kv, True), 1)
    kv_near = swapped(edge(kv, False), 0)
    qd_far = swapped(edge(qd, True), 1)
    dq, stat, part, give = query_part(place, halo, turn, kv, qd, kv_far, kv_near)
    stat_far = swapped(stat[:, :, :HALF], 1)
    got = swapped(give, 0)
    dkv = key_part(place, halo, turn, kv, qd_far, stat_far, part, got)
    dq, dkv = lax.optimization_barrier((exchanged(dq), dkv))
    return *merged(dq), *merged(exchanged(dkv))


def solution(mesh):
    spec = P(("blk", "head"), None)
    return jax.shard_map(
        shards, mesh=mesh, in_specs=(spec,) * 4, out_specs=(spec,) * 3, check_vma=False
    )
```

time: 91.9 us -> 80.5 us (0.88)
  the two profiles are of different devices: /device:TPU:0 before, /device:TPU:8 now
where the time goes in v3:
time: 80.5 us; the launch traced here: 80.2 us
  waiting for transfers between devices  32.5 us (40%)
  starting transfers between devices  23.3 us (29%)
  Pallas kernels  18.1 us (22%)
  local copies, waits for them, and re-layouts  4.16 us (5%)
  other arithmetic  1.35 us (2%)
    ppermute x12, waiting for transfers between devices, exchanged(): lax.ppermute(pieces[k], 'head', [(i, i ^ k) for i in range(n)])  29.3 us
    ppermute x12, starting transfers between devices, exchanged(): lax.ppermute(pieces[k], 'head', [(i, i ^ k) for i in range(n)])  14.1 us
    pallas_call x1, Pallas kernels, query_part(): pl.pallas_call(lambda *refs: query_kernel(n, *refs), in_specs=[scalars] *...  11.6 us
    ppermute x5, starting transfers between devices, swapped(): return lax.ppermute(array, 'blk', pairs + [(j, i) for i, j in pairs])  9.21 us
    unnamed x8, local copies, waits for them, and re-layouts  4.16 us
    pallas_call x1, Pallas kernels, key_part(): pl.pallas_call(lambda *refs: key_kernel(n, *refs), in_specs=[scalars] * 3...  3.4 us
    ppermute x5, waiting for transfers between devices, swapped(): return lax.ppermute(array, 'blk', pairs + [(j, i) for i, j in pairs])  3.14 us
    pallas_call x2, Pallas kernels, merged(): pl.pallas_call(lambda *refs: merge_kernel(n, *refs), in_specs=[pl.BlockSp...  1.84 us
  transfers between devices with their start and end apart: 17, of which 8 were waited for; matrix products, arithmetic and copies ran while one was open for 0% of the time, Pallas kernels for 21%

profile of v3, /device:TPU:8, one launch (start us, length us, event | category | flops | bytes accessed | tf_op | source)
XLA Modules:
  0.0 80.2 jit_solution(10258532678323972071)
XLA Ops:
  0.6 0.0 copy-start
  0.6 1.0 %copy-done = bf16[128,2048]{1,0:T(8,128)(2,1)S(1)} copy-done((bf16[128,2048]{1,0:T(8,128)(2,1)S(1)}, bf16[128,2048]{1,0:T(8,128)(2,1)}, u32[]{:S(2)}) %copy-start) | copy-done | bytes 524312
  1.7 0.0 copy-start.1
  1.7 1.0 %copy-done.1 = bf16[128,2048]{1,0:T(8,128)(2,1)S(1)} copy-done((bf16[128,2048]{1,0:T(8,128)(2,1)S(1)}, bf16[128,2048]{1,0:T(8,128)(2,1)}, u32[]{:S(2)}) %copy-start.1) | copy-done | bytes 524312
  2.7 0.2 pack.2
  3.0 1.6 %collective-permute-start = (bf16[2,128,512]{2,1,0:T(8,128)(2,1)S(1)}, bf16[2,128,512]{2,1,0:T(8,128)(2,1)S(1)}, u32[]{:S(2)}, u32[]{:S(2)}) collective-permute-start(bf16[2,128,512]{2,1,0:T(8,128)(2,1)S(1)} %get-tuple-element.37), channel_id=1, source_target_pairs={{0,8},{8,0},{16,24},{24,16},{1,9},{9,1},{17,25},{25,17},{2,10},{10... | collective-permute-start | bytes 786440 | tf_op jit(solution)/shard_map/ppermute | solution.py:367
  4.5 1.5 %collective-permute-start.1 = (bf16[2,128,512]{2,1,0:T(8,128)(2,1)S(1)}, bf16[2,128,512]{2,1,0:T(8,128)(2,1)S(1)}, u32[]{:S(2)}, u32[]{:S(2)}) collective-permute-start(bf16[2,128,512]{2,1,0:T(8,128)(2,1)S(1)} %get-tuple-element.38), channel_id=1, source_target_pairs={{0,16},{8,24},{16,0},{24,8},{1,17},{9,25},{17,1},{25,9},{2,18},{10... | collective-permute-start | bytes 786440 | tf_op jit(solution)/shard_map/ppermute | solution.py:367
  6.0 0.5 collective-permute-start.2
  6.5 0.0 copy-start.2
  6.5 1.0 %copy-done.2 = bf16[128,2048]{1,0:T(8,128)(2,1)S(1)} copy-done((bf16[128,2048]{1,0:T(8,128)(2,1)S(1)}, bf16[128,2048]{1,0:T(8,128)(2,1)}, u32[]{:S(2)}) %copy-start.2) | copy-done | bytes 524312
  7.6 0.0 copy-start.3
  7.6 1.0 %copy-done.3 = bf16[128,2048]{1,0:T(8,128)(2,1)S(1)} copy-done((bf16[128,2048]{1,0:T(8,128)(2,1)S(1)}, bf16[128,2048]{1,0:T(8,128)(2,1)}, u32[]{:S(2)}) %copy-start.3) | copy-done | bytes 524312
  8.6 1.0 %pack.3 = (bf16[2,128,512]{2,1,0:T(8,128)(2,1)S(1)}, bf16[2,128,512]{2,1,0:T(8,128)(2,1)}, bf16[2,128,512]{2,1,0:T(8,128)(2,1)}, bf16[2,128,512]{2,1,0:T(8,128)(2,1)S(1)}) custom-call(bf16[128,2048]{1,0:T(8,128)(2,1)S(1)} %copy-done.2, bf16[128,2048]{1,0:T(8,128)(2,1)S(1)} %copy-done.3), custom_call_target="tpu_custom_call" | custom-call | tf_op jit(solution)/shard_map/pack/pallas_call | solution.py:55
  9.6 2.6 %collective-permute-done.refs_4_ = bf16[2,128,512]{2,1,0:T(8,128)(2,1)S(1)} collective-permute-done((bf16[2,128,512]{2,1,0:T(8,128)(2,1)S(1)}, bf16[2,128,512]{2,1,0:T(8,128)(2,1)S(1)}, u32[]{:S(2)}, u32[]{:S(2)}) %collective-permute-start) | collective-permute-done | bytes 262176 | tf_op jit(solution)/shard_map/ppermute | solution.py:367
  12.2 5.7 %collective-permute-done.1.refs_5_ = bf16[2,128,512]{2,1,0:T(8,128)(2,1)S(1)} collective-permute-done((bf16[2,128,512]{2,1,0:T(8,128)(2,1)S(1)}, bf16[2,128,512]{2,1,0:T(8,128)(2,1)S(1)}, u32[]{:S(2)}, u32[]{:S(2)}) %collective-permute-start.1) | collective-permute-done | bytes 262176 | tf_op jit(solution)/shard_map/ppermute | solution.py:367
  17.9 0.0 collective-permute-done.2.refs_6_
  17.9 1.1 %pad_maximum_fusion = bf16[4,2,128,512]{3,2,1,0:T(8,128)(2,1)} fusion(bf16[1,2,128,512]{3,2,1,0:T(8,128)(2,1)S(1)} %bitcast.13, bf16[1,2,128,512]{3,2,1,0:T(8,128)(2,1)S(1)} %bitcast.12, bf16[1,2,128,512]{3,2,1,0:T(8,128)(2,1)S(1)} %bitcast.11, bf16[1,2,128,512]{3,2,1,0:T(8,128)(2,1)S(1)} %bitcast.10), kind=kLoop, calls=%fused_computation | loop fusion | flops 1572864 | bytes 2097152 | tf_op jit(solution)/shard_map/stack | solution.py:386
  19.0 1.9 %collective-permute-start.6 = (bf16[4,2,128,512]{3,2,1,0:T(8,128)(2,1)}, bf16[4,2,128,512]{3,2,1,0:T(8,128)(2,1)S(1)}, u32[]{:S(2)}, u32[]{:S(2)}) collective-permute-start(bf16[4,2,128,512]{3,2,1,0:T(8,128)(2,1)} %pad_maximum_fusion), channel_id=1, source_target_pairs={{1,2},{3,4},{5,6},{2,1},{4,3},{6,5},{9,10},{11,12},{13,14},{10,9},... | collective-permute-start | bytes 3145736 | tf_op jit(solution)/shard_map/ppermute | solution.py:361
  21.0 1.7 %collective-permute-start.7 = (bf16[4,2,128,512]{3,2,1,0:T(8,128)(2,1)}, bf16[4,2,128,512]{3,2,1,0:T(8,128)(2,1)}, u32[]{:S(2)}, u32[]{:S(2)}) collective-permute-start(bf16[4,2,128,512]{3,2,1,0:T(8,128)(2,1)} %pad_maximum_fusion), channel_id=1, source_target_pairs={{0,1},{2,3},{4,5},{6,7},{1,0},{3,2},{5,4},{7,6},{8,9},{10,11},{12,... | collective-permute-start | bytes 3145736 | tf_op jit(solution)/shard_map/ppermute | solution.py:361
  22.7 1.2 %collective-permute-start.3 = (bf16[2,128,512]{2,1,0:T(8,128)(2,1)}, bf16[2,128,512]{2,1,0:T(8,128)(2,1)S(1)}, u32[]{:S(2)}, u32[]{:S(2)}) collective-permute-start(bf16[2,128,512]{2,1,0:T(8,128)(2,1)} %get-tuple-element.41), channel_id=1, source_target_pairs={{0,8},{8,0},{16,24},{24,16},{1,9},{9,1},{17,25},{25,17},{2,10},{10... | collective-permute-start | bytes 786440 | tf_op jit(solution)/shard_map/ppermute | solution.py:367
  23.9 0.8 %collective-permute-start.4 = (bf16[2,128,512]{2,1,0:T(8,128)(2,1)}, bf16[2,128,512]{2,1,0:T(8,128)(2,1)S(1)}, u32[]{:S(2)}, u32[]{:S(2)}) collective-permute-start(bf16[2,128,512]{2,1,0:T(8,128)(2,1)} %get-tuple-element.42), channel_id=1, source_target_pairs={{0,16},{8,24},{16,0},{24,8},{1,17},{9,25},{17,1},{25,9},{2,18},{10... | collective-permute-start | bytes 786440 | tf_op jit(solution)/shard_map/ppermute | solution.py:367
  24.8 1.4 %collective-permute-start.5 = (bf16[2,128,512]{2,1,0:T(8,128)(2,1)S(1)}, bf16[2,128,512]{2,1,0:T(8,128)(2,1)S(1)}, u32[]{:S(2)}, u32[]{:S(2)}) collective-permute-start(bf16[2,128,512]{2,1,0:T(8,128)(2,1)S(1)} %get-tuple-element.43), channel_id=1, source_target_pairs={{0,24},{8,16},{16,8},{24,0},{1,25},{9,17},{17,9},{25,1},{2,26},{10... | collective-permute-start | bytes 786440 | tf_op jit(solution)/shard_map/ppermute | solution.py:367
  26.2 0.1 pad_add_fusion.refs_2_
  26.3 5.8 %collective-permute-done.3.refs_8_ = bf16[2,128,512]{2,1,0:T(8,128)(2,1)S(1)} collective-permute-done((bf16[2,128,512]{2,1,0:T(8,128)(2,1)}, bf16[2,128,512]{2,1,0:T(8,128)(2,1)S(1)}, u32[]{:S(2)}, u32[]{:S(2)}) %collective-permute-start.3) | collective-permute-done | bytes 262176 | tf_op jit(solution)/shard_map/ppermute | solution.py:367
  32.1 4.2 %collective-permute-done.4.refs_9_ = bf16[2,128,512]{2,1,0:T(8,128)(2,1)S(1)} collective-permute-done((bf16[2,128,512]{2,1,0:T(8,128)(2,1)}, bf16[2,128,512]{2,1,0:T(8,128)(2,1)S(1)}, u32[]{:S(2)}, u32[]{:S(2)}) %collective-permute-start.4) | collective-permute-done | bytes 262176 | tf_op jit(solution)/shard_map/ppermute | solution.py:367
  36.3 1.5 %collective-permute-done.5.refs_10_ = bf16[2,128,512]{2,1,0:T(8,128)(2,1)S(1)} collective-permute-done((bf16[2,128,512]{2,1,0:T(8,128)(2,1)S(1)}, bf16[2,128,512]{2,1,0:T(8,128)(2,1)S(1)}, u32[]{:S(2)}, u32[]{:S(2)}) %collective-permute-start.5) | collective-permute-done | bytes 262176 | tf_op jit(solution)/shard_map/ppermute | solution.py:367
  37.8 0.1 pad_maximum_fusion.1
  37.9 1.9 %collective-permute-start.11 = (bf16[4,2,128,512]{3,2,1,0:T(8,128)(2,1)S(1)}, bf16[4,2,128,512]{3,2,1,0:T(8,128)(2,1)S(1)}, u32[]{:S(2)}, u32[]{:S(2)}) collective-permute-start(bf16[4,2,128,512]{3,2,1,0:T(8,128)(2,1)S(1)} %pad_maximum_fusion.1), channel_id=1, source_target_pairs={{1,2},{3,4},{5,6},{2,1},{4,3},{6,5},{9,10},{11,12},{13,14},{10,9},... | collective-permute-start | bytes 3145736 | tf_op jit(solution)/shard_map/ppermute | solution.py:361
  39.8 0.0 collective-permute-done.6.refs_11_
  39.9 0.0 collective-permute-done.7.refs_12_
  39.9 11.6 %query_part.1 = (bf16[128,512]{1,0:T(8,128)(2,1)S(1)}, bf16[128,512]{1,0:T(8,128)(2,1)S(1)}, bf16[128,512]{1,0:T(8,128)(2,1)S(1)}, bf16[128,512]{1,0:T(8,128)(2,...) custom-call(s32[4]{0:T(128)S(1)} %xor_xor_fusion.refs_0_.refs_1_, ...), custom_call_target="tpu_custom_call" | custom-call | flops 3355443200 | bytes 3145728 | tf_op jit(solution)/shard_map/query_part/pallas_call | solution.py:255
  51.5 1.7 %collective-permute-start.13 = (bf16[2,512,512]{2,1,0:T(8,128)(2,1)S(1)}, bf16[2,512,512]{2,1,0:T(8,128)(2,1)S(1)}, u32[]{:S(2)}, u32[]{:S(2)}) collective-permute-start(bf16[2,512,512]{2,1,0:T(8,128)(2,1)S(1)} %get-tuple-element.54), channel_id=1, source_target_pairs={{0,1},{2,3},{4,5},{6,7},{1,0},{3,2},{5,4},{7,6},{8,9},{10,11},{12,... | collective-permute-start | bytes 3145736 | tf_op jit(solution)/shard_map/ppermute | solution.py:361
  53.2 1.7 %collective-permute-start.10 = (bf16[128,512]{1,0:T(8,128)(2,1)S(1)}, bf16[128,512]{1,0:T(8,128)(2,1)S(1)}, u32[]{:S(2)}, u32[]{:S(2)}) collective-permute-start(bf16[128,512]{1,0:T(8,128)(2,1)S(1)} %get-tuple-element.51), channel_id=1, source_target_pairs={{0,24},{8,16},{16,8},{24,0},{1,25},{9,17},{17,9},{25,1},{2,26},{10... | collective-permute-start | bytes 393224 | tf_op jit(solution)/shard_map/ppermute | solution.py:367
  55.0 0.6 collective-permute-start.8
  55.5 1.2 %collective-permute-start.9 = (bf16[128,512]{1,0:T(8,128)(2,1)S(1)}, bf16[128,512]{1,0:T(8,128)(2,1)S(1)}, u32[]{:S(2)}, u32[]{:S(2)}) collective-permute-start(bf16[128,512]{1,0:T(8,128)(2,1)S(1)} %get-tuple-element.50), channel_id=1, source_target_pairs={{0,16},{8,24},{16,0},{24,8},{1,17},{9,25},{17,1},{25,9},{2,18},{10... | collective-permute-start | bytes 393224 | tf_op jit(solution)/shard_map/ppermute | solution.py:367
  56.7 0.0 collective-permute-done.11.refs_7_
  56.7 1.9 %collective-permute-start.12 = (f32[4,2,512]{2,1,0:T(2,128)S(1)}, f32[4,2,512]{2,1,0:T(2,128)S(1)}, u32[]{:S(2)}, u32[]{:S(2)}) collective-permute-start(f32[4,2,512]{2,1,0:T(2,128)S(1)} %get-tuple-element.52), channel_id=1, source_target_pairs={{1,2},{3,4},{5,6},{2,1},{4,3},{6,5},{9,10},{11,12},{13,14},{10,9},... | collective-permute-start | bytes 49160 | tf_op jit(solution)/shard_map/ppermute | solution.py:361
  58.6 3.1 %collective-permute-done.12.refs_8_ = f32[4,2,512]{2,1,0:T(2,128)S(1)} collective-permute-done((f32[4,2,512]{2,1,0:T(2,128)S(1)}, f32[4,2,512]{2,1,0:T(2,128)S(1)}, u32[]{:S(2)}, u32[]{:S(2)}) %collective-permute-start.12) | collective-permute-done | bytes 16416 | tf_op jit(solution)/shard_map/ppermute | solution.py:361
  61.7 0.0 collective-permute-done.13.refs_10_
  61.7 3.4 %key_part.1 = (bf16[2,128,512]{2,1,0:T(8,128)(2,1)S(1)}, bf16[2,128,512]{2,1,0:T(8,128)(2,1)S(1)}, bf16[2,128,512]{2,1,0:T(8,128)(2,1)S(1)}, bf16[2,128,512]{2,1,0:T(8,128)(2,1)S(1)}) custom-call(s32[4]{0:T(128)S(1)} %xor_xor_fusion.refs_0_.refs_1_, s32[4]{0:T(128)S(1)} %xor_xor_fusion.refs_0_.refs_1_, s32[2]{0:T(128)S(1)} %pad_add_fusion.refs_2_, ...), custom_call_target="tpu_custom_call" | custom-call | flops 805306368 | bytes 6291456 | tf_op jit(solution)/shard_map/key_part/pallas_call | solution.py:334
  65.2 0.0 collective-permute-done.10.refs_3_
  65.2 0.0 collective-permute-done.8.refs_1_
  65.2 0.0 collective-permute-done.9.refs_2_
  65.2 0.8 %collective-permute-start.14 = (bf16[2,128,512]{2,1,0:T(8,128)(2,1)S(1)}, bf16[2,128,512]{2,1,0:T(8,128)(2,1)S(1)}, u32[]{:S(2)}, u32[]{:S(2)}) collective-permute-start(bf16[2,128,512]{2,1,0:T(8,128)(2,1)S(1)} %get-tuple-element.64), channel_id=1, source_target_pairs={{0,8},{8,0},{16,24},{24,16},{1,9},{9,1},{17,25},{25,17},{2,10},{10... | collective-permute-start | bytes 786440 | tf_op jit(solution)/shard_map/ppermute | solution.py:367
  66.0 1.5 %collective-permute-start.15 = (bf16[2,128,512]{2,1,0:T(8,128)(2,1)S(1)}, bf16[2,128,512]{2,1,0:T(8,128)(2,1)S(1)}, u32[]{:S(2)}, u32[]{:S(2)}) collective-permute-start(bf16[2,128,512]{2,1,0:T(8,128)(2,1)S(1)} %get-tuple-element.65), channel_id=1, source_target_pairs={{0,16},{8,24},{16,0},{24,8},{1,17},{9,25},{17,1},{25,9},{2,18},{10... | collective-permute-start | bytes 786440 | tf_op jit(solution)/shard_map/ppermute | solution.py:367
  67.6 1.2 %collective-permute-start.16 = (bf16[2,128,512]{2,1,0:T(8,128)(2,1)S(1)}, bf16[2,128,512]{2,1,0:T(8,128)(2,1)S(1)}, u32[]{:S(2)}, u32[]{:S(2)}) collective-permute-start(bf16[2,128,512]{2,1,0:T(8,128)(2,1)S(1)} %get-tuple-element.66), channel_id=1, source_target_pairs={{0,24},{8,16},{16,8},{24,0},{1,25},{9,17},{17,9},{25,1},{2,26},{10... | collective-permute-start | bytes 786440 | tf_op jit(solution)/shard_map/ppermute | solution.py:367
  68.7 0.8 %merge.2 = bf16[128,2048]{1,0:T(8,128)(2,1)} custom-call(bf16[128,512]{1,0:T(8,128)(2,1)S(1)} %get-tuple-element.59.refs_0_, bf16[128,512]{1,0:T(8,128)(2,1)S(1)} %collective-permute-done.8.refs_1_, bf16[128,512]{1,0:T(8,128)(2,1)S(1)} %collective-permute-done.9.refs_2_, bf16[128,512]{1,0:T(8,128)(2,1)S(1)} %collective-permute-done.10.refs_3_), custom_call_target="tpu_custom_call" | custom-call | tf_op jit(solution)/shard_map/merge/pallas_call | solution.py:88
  69.6 4.9 %collective-permute-done.14.refs_1_ = bf16[2,128,512]{2,1,0:T(8,128)(2,1)S(1)} collective-permute-done((bf16[2,128,512]{2,1,0:T(8,128)(2,1)S(1)}, bf16[2,128,512]{2,1,0:T(8,128)(2,1)S(1)}, u32[]{:S(2)}, u32[]{:S(2)}) %collective-permute-start.14) | collective-permute-done | bytes 262176 | tf_op jit(solution)/shard_map/ppermute | solution.py:367
  74.5 4.6 %collective-permute-done.15.refs_2_ = bf16[2,128,512]{2,1,0:T(8,128)(2,1)S(1)} collective-permute-done((bf16[2,128,512]{2,1,0:T(8,128)(2,1)S(1)}, bf16[2,128,512]{2,1,0:T(8,128)(2,1)S(1)}, u32[]{:S(2)}, u32[]{:S(2)}) %collective-permute-start.15) | collective-permute-done | bytes 262176 | tf_op jit(solution)/shard_map/ppermute | solution.py:367
  79.1 0.0 collective-permute-done.16.refs_3_
  79.1 1.0 %merge.3 = (bf16[128,2048]{1,0:T(8,128)(2,1)}, bf16[128,2048]{1,0:T(8,128)(2,1)}) custom-call(bf16[2,128,512]{2,1,0:T(8,128)(2,1)S(1)} %get-tuple-element.63.refs_0_, bf16[2,128,512]{2,1,0:T(8,128)(2,1)S(1)} %collective-permute-done.14.refs_1_, bf16[2,128,512]{2,1,0:T(8,128)(2,1)S(1)} %collective-permute-done.15.refs_2_, ...), custom_call_target="tpu_custom_call" | custom-call | tf_op jit(solution)/shard_map/merge/pallas_call | solution.py:88
  (1 shorter events, 0.0 us)
Async XLA Ops:
  0.6 1.0 %copy-start = (bf16[128,2048]{1,0:T(8,128)(2,1)S(1)}, bf16[128,2048]{1,0:T(8,128)(2,1)}, u32[]{:S(2)}) copy-start(bf16[128,2048]{1,0:T(8,128)(2,1)} %refs_0_.2) | copy-start | bytes 1572868
  1.7 1.0 %copy-start.1 = (bf16[128,2048]{1,0:T(8,128)(2,1)S(1)}, bf16[128,2048]{1,0:T(8,128)(2,1)}, u32[]{:S(2)}) copy-start(bf16[128,2048]{1,0:T(8,128)(2,1)} %refs_1_.2) | copy-start | bytes 1572868
  3.0 9.3 %collective-permute-start = (bf16[2,128,512]{2,1,0:T(8,128)(2,1)S(1)}, bf16[2,128,512]{2,1,0:T(8,128)(2,1)S(1)}, u32[]{:S(2)}, u32[]{:S(2)}) collective-permute-start(bf16[2,128,512]{2,1,0:T(8,128)(2,1)S(1)} %get-tuple-element.37), channel_id=1, source_target_pairs={{0,8},{8,0},{16,24},{24,16},{1,9},{9,1},{17,25},{25,17},{2,10},{10... | collective-permute-start | bytes 786440 | tf_op jit(solution)/shard_map/ppermute | solution.py:367
  4.5 13.4 %collective-permute-start.1 = (bf16[2,128,512]{2,1,0:T(8,128)(2,1)S(1)}, bf16[2,128,512]{2,1,0:T(8,128)(2,1)S(1)}, u32[]{:S(2)}, u32[]{:S(2)}) collective-permute-start(bf16[2,128,512]{2,1,0:T(8,128)(2,1)S(1)} %get-tuple-element.38), channel_id=1, source_target_pairs={{0,16},{8,24},{16,0},{24,8},{1,17},{9,25},{17,1},{25,9},{2,18},{10... | collective-permute-start | bytes 786440 | tf_op jit(solution)/shard_map/ppermute | solution.py:367
  6.0 11.9 %collective-permute-start.2 = (bf16[2,128,512]{2,1,0:T(8,128)(2,1)S(1)}, bf16[2,128,512]{2,1,0:T(8,128)(2,1)S(1)}, u32[]{:S(2)}, u32[]{:S(2)}) collective-permute-start(bf16[2,128,512]{2,1,0:T(8,128)(2,1)S(1)} %get-tuple-element.39), channel_id=1, source_target_pairs={{0,24},{8,16},{16,8},{24,0},{1,25},{9,17},{17,9},{25,1},{2,26},{10... | collective-permute-start | bytes 786440 | tf_op jit(solution)/shard_map/ppermute | solution.py:367
  6.5 1.0 %copy-start.2 = (bf16[128,2048]{1,0:T(8,128)(2,1)S(1)}, bf16[128,2048]{1,0:T(8,128)(2,1)}, u32[]{:S(2)}) copy-start(bf16[128,2048]{1,0:T(8,128)(2,1)} %refs_0_.3) | copy-start | bytes 1572868
  7.6 1.0 %copy-start.3 = (bf16[128,2048]{1,0:T(8,128)(2,1)S(1)}, bf16[128,2048]{1,0:T(8,128)(2,1)}, u32[]{:S(2)}) copy-start(bf16[128,2048]{1,0:T(8,128)(2,1)} %refs_1_.3) | copy-start | bytes 1572868
  19.0 20.8 %collective-permute-start.6 = (bf16[4,2,128,512]{3,2,1,0:T(8,128)(2,1)}, bf16[4,2,128,512]{3,2,1,0:T(8,128)(2,1)S(1)}, u32[]{:S(2)}, u32[]{:S(2)}) collective-permute-start(bf16[4,2,128,512]{3,2,1,0:T(8,128)(2,1)} %pad_maximum_fusion), channel_id=1, source_target_pairs={{1,2},{3,4},{5,6},{2,1},{4,3},{6,5},{9,10},{11,12},{13,14},{10,9},... | collective-permute-start | bytes 3145736 | tf_op jit(solution)/shard_map/ppermute | solution.py:361
  21.0 18.9 %collective-permute-start.7 = (bf16[4,2,128,512]{3,2,1,0:T(8,128)(2,1)}, bf16[4,2,128,512]{3,2,1,0:T(8,128)(2,1)}, u32[]{:S(2)}, u32[]{:S(2)}) collective-permute-start(bf16[4,2,128,512]{3,2,1,0:T(8,128)(2,1)} %pad_maximum_fusion), channel_id=1, source_target_pairs={{0,1},{2,3},{4,5},{6,7},{1,0},{3,2},{5,4},{7,6},{8,9},{10,11},{12,... | collective-permute-start | bytes 3145736 | tf_op jit(solution)/shard_map/ppermute | solution.py:361
  22.7 9.4 %collective-permute-start.3 = (bf16[2,128,512]{2,1,0:T(8,128)(2,1)}, bf16[2,128,512]{2,1,0:T(8,128)(2,1)S(1)}, u32[]{:S(2)}, u32[]{:S(2)}) collective-permute-start(bf16[2,128,512]{2,1,0:T(8,128)(2,1)} %get-tuple-element.41), channel_id=1, source_target_pairs={{0,8},{8,0},{16,24},{24,16},{1,9},{9,1},{17,25},{25,17},{2,10},{10... | collective-permute-start | bytes 786440 | tf_op jit(solution)/shard_map/ppermute | solution.py:367
  23.9 12.3 %collective-permute-start.4 = (bf16[2,128,512]{2,1,0:T(8,128)(2,1)}, bf16[2,128,512]{2,1,0:T(8,128)(2,1)S(1)}, u32[]{:S(2)}, u32[]{:S(2)}) collective-permute-start(bf16[2,128,512]{2,1,0:T(8,128)(2,1)} %get-tuple-element.42), channel_id=1, source_target_pairs={{0,16},{8,24},{16,0},{24,8},{1,17},{9,25},{17,1},{25,9},{2,18},{10... | collective-permute-start | bytes 786440 | tf_op jit(solution)/shard_map/ppermute | solution.py:367
  24.8 13.0 %collective-permute-start.5 = (bf16[2,128,512]{2,1,0:T(8,128)(2,1)S(1)}, bf16[2,128,512]{2,1,0:T(8,128)(2,1)S(1)}, u32[]{:S(2)}, u32[]{:S(2)}) collective-permute-start(bf16[2,128,512]{2,1,0:T(8,128)(2,1)S(1)} %get-tuple-element.43), channel_id=1, source_target_pairs={{0,24},{8,16},{16,8},{24,0},{1,25},{9,17},{17,9},{25,1},{2,26},{10... | collective-permute-start | bytes 786440 | tf_op jit(solution)/shard_map/ppermute | solution.py:367
  37.9 18.8 %collective-permute-start.11 = (bf16[4,2,128,512]{3,2,1,0:T(8,128)(2,1)S(1)}, bf16[4,2,128,512]{3,2,1,0:T(8,128)(2,1)S(1)}, u32[]{:S(2)}, u32[]{:S(2)}) collective-permute-start(bf16[4,2,128,512]{3,2,1,0:T(8,128)(2,1)S(1)} %pad_maximum_fusion.1), channel_id=1, source_target_pairs={{1,2},{3,4},{5,6},{2,1},{4,3},{6,5},{9,10},{11,12},{13,14},{10,9},... | collective-permute-start | bytes 3145736 | tf_op jit(solution)/shard_map/ppermute | solution.py:361
  51.5 10.3 %collective-permute-start.13 = (bf16[2,512,512]{2,1,0:T(8,128)(2,1)S(1)}, bf16[2,512,512]{2,1,0:T(8,128)(2,1)S(1)}, u32[]{:S(2)}, u32[]{:S(2)}) collective-permute-start(bf16[2,512,512]{2,1,0:T(8,128)(2,1)S(1)} %get-tuple-element.54), channel_id=1, source_target_pairs={{0,1},{2,3},{4,5},{6,7},{1,0},{3,2},{5,4},{7,6},{8,9},{10,11},{12,... | collective-permute-start | bytes 3145736 | tf_op jit(solution)/shard_map/ppermute | solution.py:361
  53.2 12.0 %collective-permute-start.10 = (bf16[128,512]{1,0:T(8,128)(2,1)S(1)}, bf16[128,512]{1,0:T(8,128)(2,1)S(1)}, u32[]{:S(2)}, u32[]{:S(2)}) collective-permute-start(bf16[128,512]{1,0:T(8,128)(2,1)S(1)} %get-tuple-element.51), channel_id=1, source_target_pairs={{0,24},{8,16},{16,8},{24,0},{1,25},{9,17},{17,9},{25,1},{2,26},{10... | collective-permute-start | bytes 393224 | tf_op jit(solution)/shard_map/ppermute | solution.py:367
  55.0 10.2 %collective-permute-start.8 = (bf16[128,512]{1,0:T(8,128)(2,1)S(1)}, bf16[128,512]{1,0:T(8,128)(2,1)S(1)}, u32[]{:S(2)}, u32[]{:S(2)}) collective-permute-start(bf16[128,512]{1,0:T(8,128)(2,1)S(1)} %get-tuple-element.49), channel_id=1, source_target_pairs={{0,8},{8,0},{16,24},{24,16},{1,9},{9,1},{17,25},{25,17},{2,10},{10... | collective-permute-start | bytes 393224 | tf_op jit(solution)/shard_map/ppermute | solution.py:367
  55.5 9.7 %collective-permute-start.9 = (bf16[128,512]{1,0:T(8,128)(2,1)S(1)}, bf16[128,512]{1,0:T(8,128)(2,1)S(1)}, u32[]{:S(2)}, u32[]{:S(2)}) collective-permute-start(bf16[128,512]{1,0:T(8,128)(2,1)S(1)} %get-tuple-element.50), channel_id=1, source_target_pairs={{0,16},{8,24},{16,0},{24,8},{1,17},{9,25},{17,1},{25,9},{2,18},{10... | collective-permute-start | bytes 393224 | tf_op jit(solution)/shard_map/ppermute | solution.py:367
  56.7 5.0 %collective-permute-start.12 = (f32[4,2,512]{2,1,0:T(2,128)S(1)}, f32[4,2,512]{2,1,0:T(2,128)S(1)}, u32[]{:S(2)}, u32[]{:S(2)}) collective-permute-start(f32[4,2,512]{2,1,0:T(2,128)S(1)} %get-tuple-element.52), channel_id=1, source_target_pairs={{1,2},{3,4},{5,6},{2,1},{4,3},{6,5},{9,10},{11,12},{13,14},{10,9},... | collective-permute-start | bytes 49160 | tf_op jit(solution)/shard_map/ppermute | solution.py:361
  65.2 9.3 %collective-permute-start.14 = (bf16[2,128,512]{2,1,0:T(8,128)(2,1)S(1)}, bf16[2,128,512]{2,1,0:T(8,128)(2,1)S(1)}, u32[]{:S(2)}, u32[]{:S(2)}) collective-permute-start(bf16[2,128,512]{2,1,0:T(8,128)(2,1)S(1)} %get-tuple-element.64), channel_id=1, source_target_pairs={{0,8},{8,0},{16,24},{24,16},{1,9},{9,1},{17,25},{25,17},{2,10},{10... | collective-permute-start | bytes 786440 | tf_op jit(solution)/shard_map/ppermute | solution.py:367
  66.0 13.1 %collective-permute-start.15 = (bf16[2,128,512]{2,1,0:T(8,128)(2,1)S(1)}, bf16[2,128,512]{2,1,0:T(8,128)(2,1)S(1)}, u32[]{:S(2)}, u32[]{:S(2)}) collective-permute-start(bf16[2,128,512]{2,1,0:T(8,128)(2,1)S(1)} %get-tuple-element.65), channel_id=1, source_target_pairs={{0,16},{8,24},{16,0},{24,8},{1,17},{9,25},{17,1},{25,9},{2,18},{10... | collective-permute-start | bytes 786440 | tf_op jit(solution)/shard_map/ppermute | solution.py:367
  67.6 11.6 %collective-permute-start.16 = (bf16[2,128,512]{2,1,0:T(8,128)(2,1)S(1)}, bf16[2,128,512]{2,1,0:T(8,128)(2,1)S(1)}, u32[]{:S(2)}, u32[]{:S(2)}) collective-permute-start(bf16[2,128,512]{2,1,0:T(8,128)(2,1)S(1)} %get-tuple-element.66), channel_id=1, source_target_pairs={{0,24},{8,16},{16,8},{24,0},{1,25},{9,17},{17,9},{25,1},{2,26},{10... | collective-permute-start | bytes 786440 | tf_op jit(solution)/shard_map/ppermute | solution.py:367

commit v4 on v3

--- a/solution.py
+++ b/solution.py
@@ -15,6 +15,7 @@
 SPAN = SUB + 2 * HALF
 CHUNKS = SPAN // SUB
 NEG = -1e30
+HINT = 30_000_000_000
 STRIP = 64
 SCALE = HEAD_DIM ** -0.5
 RATE = SCALE * math.log2(math.e)
@@ -54,13 +55,37 @@
     r, width = first.shape[0], first.shape[1] // n
     return pl.pallas_call(
         pack_kernel,
-        in_specs=[pl.BlockSpec(memory_space=pl.ANY)] * 2,
+        in_specs=[pl.BlockSpec(memory_space=pltpu.HBM)] * 2,
         out_specs=[pl.BlockSpec(memory_space=pltpu.VMEM)] * n,
         out_shape=[jax.ShapeDtypeStruct((2, r, width), first.dtype)] * n,
         scratch_shapes=[pltpu.SemaphoreType.DMA((2 * n,))],
         compiler_params=pltpu.CompilerParams(vmem_limit_bytes=SMALL_BYTES),
         name="pack",
     )(first, second)
+
+
+def stack_kernel(*refs):
+    n = (len(refs) - 2)
+    ins, out, sems = refs[:n], refs[n], refs[n + 1]
+    copies = [pltpu.make_async_copy(ins[k], out.at[k], sems.at[k]) for k in range(n)]
+    for copy in copies:
+        copy.start()
+    for copy in copies:
+        copy.wait()
+
+
+def stacked(pieces, flops=0):
+    n = len(pieces)
+    return pl.pallas_call(
+        stack_kernel,
+        in_specs=[pl.BlockSpec(memory_space=pltpu.VMEM)] * n,
+        out_specs=pl.BlockSpec(memory_space=pltpu.VMEM),
+        out_shape=jax.ShapeDtypeStruct((n, *pieces[0].shape), pieces[0].dtype),
+        scratch_shapes=[pltpu.SemaphoreType.DMA((n,))],
+        compiler_params=pltpu.CompilerParams(vmem_limit_bytes=SMALL_BYTES),
+        cost_estimate=pl.CostEstimate(flops=flops, bytes_accessed=0, transcendentals=0),
+        name="stack",
+    )(*pieces)
 
 
 def merge_kernel(n, *refs):
@@ -103,11 +128,15 @@
     ) * turn_ref[0]
 
 
-def query_kernel(n, place_ref, halo_ref, turn_ref, *refs):
+def members(refs):
+    return [ref.at[i] for ref in refs for i in range(ref.shape[0])]
+
+
+def query_kernel(n, groups, place_ref, halo_ref, turn_ref, *refs):
     kv_refs, refs = refs[:n], refs[n:]
-    qd_refs, refs = refs[:n], refs[n:]
-    far_ref, near_ref = refs[:2]
-    dq_refs, refs = refs[2:2 + n], refs[2 + n:]
+    qd_ref, refs = refs[0], refs[1:]
+    far_refs, near_refs, refs = refs[:groups], refs[groups:2 * groups], refs[2 * groups:]
+    dq_refs, refs = refs[:n], refs[n:]
     stat_ref, part_ref, give_ref, k_ext, v_ext, k_flip, q_all, g_all, dq_all = refs[:9]
     s_buf, p_buf, w_buf, d_buf = refs[9:13]
     r, width = kv_refs[0].shape[1:]
@@ -117,17 +146,17 @@
 
     def each_head(h, _):
         lanes = rows_at(h * HEAD_DIM, HEAD_DIM)
-        for i in range(HALF // r):
+        for i, (far, near) in enumerate(zip(members(far_refs), members(near_refs))):
             at = halo_ref[i] * r
             for which, ext in ((0, k_ext), (1, v_ext)):
-                ext[rows_at(at, r)] = far_ref[i, which, :, lanes]
-                ext[rows_at(HALF + rows + at, r)] = near_ref[i, which, :, lanes]
+                ext[rows_at(at, r)] = far[which, :, lanes]
+                ext[rows_at(HALF + rows + at, r)] = near[which, :, lanes]
         for k in range(n):
             at = place_ref[k] * r
             for which, ext in ((0, k_ext), (1, v_ext)):
                 ext[rows_at(HALF + at, r)] = kv_refs[k][which, :, lanes]
-            q_all[rows_at(at, r)] = qd_refs[k][0, :, lanes]
-            g_all[rows_at(at, r)] = qd_refs[k][1, :, lanes]
+            q_all[rows_at(at, r)] = qd_ref[k, 0, :, lanes]
+            g_all[rows_at(at, r)] = qd_ref[k, 1, :, lanes]
         k_flip[...] = k_ext[...].T
         if tiles > 1:
             refs[13][...] = jnp.zeros_like(refs[13])
@@ -253,8 +282,8 @@
     if rows != TILE:
         scratch.append(pltpu.VMEM((2, ext, HEAD_DIM), jnp.float32))
     outs = pl.pallas_call(
-        lambda *refs: query_kernel(n, *refs),
-        in_specs=[scalars] * 3 + [here] * (2 * n + 2),
+        lambda *refs: query_kernel(n, len(far), *refs),
+        in_specs=[scalars] * 3 + [here] * (n + 1 + 2 * len(far)),
         out_specs=[here] * (n + 3),
         scratch_shapes=scratch,
         out_shape=[jax.ShapeDtypeStruct((r, width), jnp.bfloat16)] * n
@@ -270,7 +299,7 @@
             transcendentals=heads * rows * SPAN,
         ),
         name="query_part",
-    )(place, halo, turn, *kv, *qd, far, near)
+    )(place, halo, turn, *kv, qd, *far, *near)
     return outs[:n], outs[n], outs[n + 1], outs[n + 2]
 
 
@@ -382,21 +411,20 @@
     has_far = jnp.logical_and(index > 0, index < lax.axis_size("blk") - 1)
     turn = jnp.stack([1 - 2 * odd, has_far.astype(jnp.int32)])
 
-    def edge(pieces, far):
-        stacked = jnp.stack(pieces)
-        if n == blocks:
-            return stacked
-        local = jnp.take(stacked, place, axis=0)
-        return local[:blocks] if far else local[n - blocks:]
-
-    kv_own = packed(n, key_in, value)
-    qd_own = packed(n, query, grad_out)
-    kv = exchanged(kv_own)
-    qd = exchanged(qd_own)
-    kv, qd_own = lax.optimization_barrier((kv, qd_own))
-    kv_far = swapped(edge(kv, True), 1)
-    kv_near = swapped(edge(kv, False), 0)
-    qd_far = swapped(edge(qd, True), 1)
+    kv = exchanged(packed(n, key_in, value))
+    qd = exchanged(packed(n, query, grad_out))
+    if n == blocks:
+        groups = [stacked(kv[:-1]), kv[-1][None]]
+        kv_far = [swapped(group, 1) for group in groups]
+        kv_near = [swapped(group, 0) for group in groups]
+        qd = stacked(qd, HINT)
+        qd_far = swapped(qd, 1)
+    else:
+        local, qd = jnp.stack(kv), jnp.stack(qd)
+        local = jnp.take(local, place, axis=0)
+        kv_far = [swapped(local[:blocks], 1)]
+        kv_near = [swapped(local[n - blocks:], 0)]
+        qd_far = swapped(jnp.take(qd, place[:blocks], axis=0), 1)
     dq, stat, part, give = query_part(place, halo, turn, kv, qd, kv_far, kv_near)
     stat_far = swapped(stat[:, :, :HALF], 1)
     got = swapped(give, 0)

time: 80.5 us -> 72.3 us (0.90)
  the two profiles are of different devices: /device:TPU:8 before, /device:TPU:0 now
where the time goes in v4:
time: 72.3 us; the launch traced here: 72 us
  waiting for transfers between devices  26.4 us (37%)
  starting transfers between devices  23.8 us (33%)
  Pallas kernels  16.8 us (23%)
  local copies, waits for them, and re-layouts  4.16 us (6%)
  between operations  0.77 us (1%)
    ppermute x12, waiting for transfers between devices, exchanged(): lax.ppermute(pieces[k], 'head', [(i, i ^ k) for i in range(n)])  25.7 us
    ppermute x12, starting transfers between devices, exchanged(): lax.ppermute(pieces[k], 'head', [(i, i ^ k) for i in range(n)])  17.9 us
    pallas_call x1, Pallas kernels, query_part(): pl.pallas_call(lambda *refs: query_kernel(n, len(far), *refs), in_specs=[...  10.9 us
    ppermute x7, starting transfers between devices, swapped(): return lax.ppermute(array, 'blk', pairs + [(j, i) for i, j in pairs])  5.89 us
    unnamed x8, local copies, waits for them, and re-layouts  4.16 us
    pallas_call x1, Pallas kernels, key_part(): pl.pallas_call(lambda *refs: key_kernel(n, *refs), in_specs=[scalars] * 3...  3.4 us
    pallas_call x2, Pallas kernels, merged(): pl.pallas_call(lambda *refs: merge_kernel(n, *refs), in_specs=[pl.BlockSp...  1.84 us
  transfers between devices with their start and end apart: 19, of which 7 were waited for; matrix products, arithmetic and copies ran while one was open for 0% of the time, Pallas kernels for 22%

profile of v4, /device:TPU:0, one launch (start us, length us, event | category | flops | bytes accessed | tf_op | source)
XLA Modules:
  0.0 72.0 jit_solution(8428469096174773213)
XLA Ops:
  0.6 0.0 copy-start
  0.6 1.0 %copy-done = bf16[128,2048]{1,0:T(8,128)(2,1)S(1)} copy-done((bf16[128,2048]{1,0:T(8,128)(2,1)S(1)}, bf16[128,2048]{1,0:T(8,128)(2,1)}, u32[]{:S(2)}) %copy-start) | copy-done | bytes 524312
  1.7 0.0 copy-start.1
  1.7 1.0 %copy-done.1 = bf16[128,2048]{1,0:T(8,128)(2,1)S(1)} copy-done((bf16[128,2048]{1,0:T(8,128)(2,1)S(1)}, bf16[128,2048]{1,0:T(8,128)(2,1)}, u32[]{:S(2)}) %copy-start.1) | copy-done | bytes 524312
  2.7 0.2 pack.2
  3.0 3.0 %collective-permute-start = (bf16[2,128,512]{2,1,0:T(8,128)(2,1)S(1)}, bf16[2,128,512]{2,1,0:T(8,128)(2,1)S(1)}, u32[]{:S(2)}, u32[]{:S(2)}) collective-permute-start(bf16[2,128,512]{2,1,0:T(8,128)(2,1)S(1)} %get-tuple-element.33), channel_id=1, source_target_pairs={{0,8},{8,0},{16,24},{24,16},{1,9},{9,1},{17,25},{25,17},{2,10},{10... | collective-permute-start | bytes 786440 | tf_op jit(solution)/shard_map/ppermute | solution.py:396
  6.0 1.5 %collective-permute-start.1 = (bf16[2,128,512]{2,1,0:T(8,128)(2,1)S(1)}, bf16[2,128,512]{2,1,0:T(8,128)(2,1)S(1)}, u32[]{:S(2)}, u32[]{:S(2)}) collective-permute-start(bf16[2,128,512]{2,1,0:T(8,128)(2,1)S(1)} %get-tuple-element.34), channel_id=1, source_target_pairs={{0,16},{8,24},{16,0},{24,8},{1,17},{9,25},{17,1},{25,9},{2,18},{10... | collective-permute-start | bytes 786440 | tf_op jit(solution)/shard_map/ppermute | solution.py:396
  7.5 0.0 copy-start.2
  7.5 1.0 %copy-done.2 = bf16[128,2048]{1,0:T(8,128)(2,1)S(1)} copy-done((bf16[128,2048]{1,0:T(8,128)(2,1)S(1)}, bf16[128,2048]{1,0:T(8,128)(2,1)}, u32[]{:S(2)}) %copy-start.2) | copy-done | bytes 524312
  8.5 0.0 copy-start.3
  8.5 1.0 %copy-done.3 = bf16[128,2048]{1,0:T(8,128)(2,1)S(1)} copy-done((bf16[128,2048]{1,0:T(8,128)(2,1)S(1)}, bf16[128,2048]{1,0:T(8,128)(2,1)}, u32[]{:S(2)}) %copy-start.3) | copy-done | bytes 524312
  9.6 0.2 pack.3
  9.8 0.6 collective-permute-start.3
  10.4 1.4 %collective-permute-start.2 = (bf16[2,128,512]{2,1,0:T(8,128)(2,1)S(1)}, bf16[2,128,512]{2,1,0:T(8,128)(2,1)S(1)}, u32[]{:S(2)}, u32[]{:S(2)}) collective-permute-start(bf16[2,128,512]{2,1,0:T(8,128)(2,1)S(1)} %get-tuple-element.35), channel_id=1, source_target_pairs={{0,24},{8,16},{16,8},{24,0},{1,25},{9,17},{17,9},{25,1},{2,26},{10... | collective-permute-start | bytes 786440 | tf_op jit(solution)/shard_map/ppermute | solution.py:396
  11.8 1.5 %collective-permute-start.4 = (bf16[2,128,512]{2,1,0:T(8,128)(2,1)S(1)}, bf16[2,128,512]{2,1,0:T(8,128)(2,1)S(1)}, u32[]{:S(2)}, u32[]{:S(2)}) collective-permute-start(bf16[2,128,512]{2,1,0:T(8,128)(2,1)S(1)} %get-tuple-element.38), channel_id=1, source_target_pairs={{0,16},{8,24},{16,0},{24,8},{1,17},{9,25},{17,1},{25,9},{2,18},{10... | collective-permute-start | bytes 786440 | tf_op jit(solution)/shard_map/ppermute | solution.py:396
  13.4 0.0 collective-permute-done.refs_1_.refs_4_
  13.4 2.7 %collective-permute-start.5 = (bf16[2,128,512]{2,1,0:T(8,128)(2,1)S(1)}, bf16[2,128,512]{2,1,0:T(8,128)(2,1)S(1)}, u32[]{:S(2)}, u32[]{:S(2)}) collective-permute-start(bf16[2,128,512]{2,1,0:T(8,128)(2,1)S(1)} %get-tuple-element.39), channel_id=1, source_target_pairs={{0,24},{8,16},{16,8},{24,0},{1,25},{9,17},{17,9},{25,1},{2,26},{10... | collective-permute-start | bytes 786440 | tf_op jit(solution)/shard_map/ppermute | solution.py:396
  16.1 0.1 pad_add_fusion.refs_2_
  16.2 0.0 collective-permute-done.1.refs_2_.refs_5_
  16.2 0.1 stack.20
  16.3 0.7 collective-permute-start.6
  17.0 2.1 %collective-permute-done.3.refs_1_ = bf16[2,128,512]{2,1,0:T(8,128)(2,1)S(1)} collective-permute-done((bf16[2,128,512]{2,1,0:T(8,128)(2,1)S(1)}, bf16[2,128,512]{2,1,0:T(8,128)(2,1)S(1)}, u32[]{:S(2)}, u32[]{:S(2)}) %collective-permute-start.3) | collective-permute-done | bytes 262176 | tf_op jit(solution)/shard_map/ppermute | solution.py:396
  19.1 0.9 %collective-permute-start.8 = (bf16[3,2,128,512]{3,2,1,0:T(8,128)(2,1)S(1)}, bf16[3,2,128,512]{3,2,1,0:T(8,128)(2,1)S(1)}, u32[]{:S(2)}, u32[]{:S(2)}) collective-permute-start(bf16[3,2,128,512]{3,2,1,0:T(8,128)(2,1)S(1)} %stack.20), channel_id=1, source_target_pairs={{0,1},{2,3},{4,5},{6,7},{1,0},{3,2},{5,4},{7,6},{8,9},{10,11},{12,... | collective-permute-start | bytes 2359304 | tf_op jit(solution)/shard_map/ppermute | solution.py:390
  20.0 6.0 %collective-permute-done.2.refs_6_ = bf16[2,128,512]{2,1,0:T(8,128)(2,1)S(1)} collective-permute-done((bf16[2,128,512]{2,1,0:T(8,128)(2,1)S(1)}, bf16[2,128,512]{2,1,0:T(8,128)(2,1)S(1)}, u32[]{:S(2)}, u32[]{:S(2)}) %collective-permute-start.2) | collective-permute-done | bytes 262176 | tf_op jit(solution)/shard_map/ppermute | solution.py:396
  26.0 0.7 collective-permute-start.7
  26.6 4.0 %collective-permute-done.4.refs_2_ = bf16[2,128,512]{2,1,0:T(8,128)(2,1)S(1)} collective-permute-done((bf16[2,128,512]{2,1,0:T(8,128)(2,1)S(1)}, bf16[2,128,512]{2,1,0:T(8,128)(2,1)S(1)}, u32[]{:S(2)}, u32[]{:S(2)}) %collective-permute-start.4) | collective-permute-done | bytes 262176 | tf_op jit(solution)/shard_map/ppermute | solution.py:396
  30.6 0.0 collective-permute-start.9
  30.6 0.0 collective-permute-done.5.refs_3_
  30.6 0.1 stack.19.refs_7_
  30.7 0.7 %collective-permute-start.13 = (bf16[4,2,128,512]{3,2,1,0:T(8,128)(2,1)S(1)}, bf16[4,2,128,512]{3,2,1,0:T(8,128)(2,1)S(1)}, u32[]{:S(2)}, u32[]{:S(2)}) collective-permute-start(bf16[4,2,128,512]{3,2,1,0:T(8,128)(2,1)S(1)} %stack.19.refs_7_), channel_id=1, source_target_pairs={{1,2},{3,4},{5,6},{2,1},{4,3},{6,5},{9,10},{11,12},{13,14},{10,9},... | collective-permute-start | bytes 3145736 | tf_op jit(solution)/shard_map/ppermute | solution.py:390
  31.4 0.0 collective-permute-done.7.refs_9_
  31.5 0.7 collective-permute-done.9.refs_11_
  32.1 0.0 collective-permute-done.6.refs_8_
  32.1 0.0 collective-permute-done.8.refs_10_
  32.1 10.9 %query_part.1 = (bf16[128,512]{1,0:T(8,128)(2,1)S(1)}, bf16[128,512]{1,0:T(8,128)(2,1)S(1)}, bf16[128,512]{1,0:T(8,128)(2,1)S(1)}, bf16[128,512]{1,0:T(8,128)(2,...) custom-call(s32[4]{0:T(128)S(1)} %xor_xor_fusion.refs_0_.refs_1_, ...), custom_call_target="tpu_custom_call" | custom-call | flops 3355443200 | bytes 3145728 | tf_op jit(solution)/shard_map/query_part/pallas_call | solution.py:284
  43.1 2.3 %collective-permute-start.15 = (bf16[2,512,512]{2,1,0:T(8,128)(2,1)S(1)}, bf16[2,512,512]{2,1,0:T(8,128)(2,1)S(1)}, u32[]{:S(2)}, u32[]{:S(2)}) collective-permute-start(bf16[2,512,512]{2,1,0:T(8,128)(2,1)S(1)} %get-tuple-element.46), channel_id=1, source_target_pairs={{0,1},{2,3},{4,5},{6,7},{1,0},{3,2},{5,4},{7,6},{8,9},{10,11},{12,... | collective-permute-start | bytes 3145736 | tf_op jit(solution)/shard_map/ppermute | solution.py:390
  45.4 0.7 collective-permute-start.14
  46.0 1.3 %collective-permute-start.10 = (bf16[128,512]{1,0:T(8,128)(2,1)S(1)}, bf16[128,512]{1,0:T(8,128)(2,1)S(1)}, u32[]{:S(2)}, u32[]{:S(2)}) collective-permute-start(bf16[128,512]{1,0:T(8,128)(2,1)S(1)} %get-tuple-element.41), channel_id=1, source_target_pairs={{0,8},{8,0},{16,24},{24,16},{1,9},{9,1},{17,25},{25,17},{2,10},{10... | collective-permute-start | bytes 393224 | tf_op jit(solution)/shard_map/ppermute | solution.py:396
  47.3 0.8 %collective-permute-start.11 = (bf16[128,512]{1,0:T(8,128)(2,1)S(1)}, bf16[128,512]{1,0:T(8,128)(2,1)S(1)}, u32[]{:S(2)}, u32[]{:S(2)}) collective-permute-start(bf16[128,512]{1,0:T(8,128)(2,1)S(1)} %get-tuple-element.42), channel_id=1, source_target_pairs={{0,16},{8,24},{16,0},{24,8},{1,17},{9,25},{17,1},{25,9},{2,18},{10... | collective-permute-start | bytes 393224 | tf_op jit(solution)/shard_map/ppermute | solution.py:396
  48.1 0.0 collective-permute-done.14.refs_8_
  48.1 1.4 %collective-permute-start.12 = (bf16[128,512]{1,0:T(8,128)(2,1)S(1)}, bf16[128,512]{1,0:T(8,128)(2,1)S(1)}, u32[]{:S(2)}, u32[]{:S(2)}) collective-permute-start(bf16[128,512]{1,0:T(8,128)(2,1)S(1)} %get-tuple-element.43), channel_id=1, source_target_pairs={{0,24},{8,16},{16,8},{24,0},{1,25},{9,17},{17,9},{25,1},{2,26},{10... | collective-permute-start | bytes 393224 | tf_op jit(solution)/shard_map/ppermute | solution.py:396
  49.6 0.0 collective-permute-done.13.refs_7_
  49.6 0.0 collective-permute-done.15.refs_10_
  49.6 3.4 %key_part.1 = (bf16[2,128,512]{2,1,0:T(8,128)(2,1)S(1)}, bf16[2,128,512]{2,1,0:T(8,128)(2,1)S(1)}, bf16[2,128,512]{2,1,0:T(8,128)(2,1)S(1)}, bf16[2,128,512]{2,1,0:T(8,128)(2,1)S(1)}) custom-call(s32[4]{0:T(128)S(1)} %xor_xor_fusion.refs_0_.refs_1_, s32[4]{0:T(128)S(1)} %xor_xor_fusion.refs_0_.refs_1_, s32[2]{0:T(128)S(1)} %pad_add_fusion.refs_2_, ...), custom_call_target="tpu_custom_call" | custom-call | flops 805306368 | bytes 6291456 | tf_op jit(solution)/shard_map/key_part/pallas_call | solution.py:363
  53.0 0.0 collective-permute-done.10.refs_1_
  53.0 0.0 collective-permute-done.11.refs_2_
  53.0 2.4 %collective-permute-done.12.refs_3_ = bf16[128,512]{1,0:T(8,128)(2,1)S(1)} collective-permute-done((bf16[128,512]{1,0:T(8,128)(2,1)S(1)}, bf16[128,512]{1,0:T(8,128)(2,1)S(1)}, u32[]{:S(2)}, u32[]{:S(2)}) %collective-permute-start.12) | collective-permute-done | bytes 131104 | tf_op jit(solution)/shard_map/ppermute | solution.py:396
  55.4 0.9 %collective-permute-start.16 = (bf16[2,128,512]{2,1,0:T(8,128)(2,1)S(1)}, bf16[2,128,512]{2,1,0:T(8,128)(2,1)S(1)}, u32[]{:S(2)}, u32[]{:S(2)}) collective-permute-start(bf16[2,128,512]{2,1,0:T(8,128)(2,1)S(1)} %get-tuple-element.56), channel_id=1, source_target_pairs={{0,8},{8,0},{16,24},{24,16},{1,9},{9,1},{17,25},{25,17},{2,10},{10... | collective-permute-start | bytes 786440 | tf_op jit(solution)/shard_map/ppermute | solution.py:396
  56.3 1.2 %collective-permute-start.17 = (bf16[2,128,512]{2,1,0:T(8,128)(2,1)S(1)}, bf16[2,128,512]{2,1,0:T(8,128)(2,1)S(1)}, u32[]{:S(2)}, u32[]{:S(2)}) collective-permute-start(bf16[2,128,512]{2,1,0:T(8,128)(2,1)S(1)} %get-tuple-element.57), channel_id=1, source_target_pairs={{0,16},{8,24},{16,0},{24,8},{1,17},{9,25},{17,1},{25,9},{2,18},{10... | collective-permute-start | bytes 786440 | tf_op jit(solution)/shard_map/ppermute | solution.py:396
  57.5 1.4 %collective-permute-start.18 = (bf16[2,128,512]{2,1,0:T(8,128)(2,1)S(1)}, bf16[2,128,512]{2,1,0:T(8,128)(2,1)S(1)}, u32[]{:S(2)}, u32[]{:S(2)}) collective-permute-start(bf16[2,128,512]{2,1,0:T(8,128)(2,1)S(1)} %get-tuple-element.58), channel_id=1, source_target_pairs={{0,24},{8,16},{16,8},{24,0},{1,25},{9,17},{17,9},{25,1},{2,26},{10... | collective-permute-start | bytes 786440 | tf_op jit(solution)/shard_map/ppermute | solution.py:396
  58.9 0.8 %merge.2 = bf16[128,2048]{1,0:T(8,128)(2,1)} custom-call(bf16[128,512]{1,0:T(8,128)(2,1)S(1)} %get-tuple-element.51.refs_0_, bf16[128,512]{1,0:T(8,128)(2,1)S(1)} %collective-permute-done.10.refs_1_, bf16[128,512]{1,0:T(8,128)(2,1)S(1)} %collective-permute-done.11.refs_2_, bf16[128,512]{1,0:T(8,128)(2,1)S(1)} %collective-permute-done.12.refs_3_), custom_call_target="tpu_custom_call" | custom-call | tf_op jit(solution)/shard_map/merge/pallas_call | solution.py:113
  59.7 4.6 %collective-permute-done.16.refs_1_ = bf16[2,128,512]{2,1,0:T(8,128)(2,1)S(1)} collective-permute-done((bf16[2,128,512]{2,1,0:T(8,128)(2,1)S(1)}, bf16[2,128,512]{2,1,0:T(8,128)(2,1)S(1)}, u32[]{:S(2)}, u32[]{:S(2)}) %collective-permute-start.16) | collective-permute-done | bytes 262176 | tf_op jit(solution)/shard_map/ppermute | solution.py:396
  64.3 6.6 %collective-permute-done.17.refs_2_ = bf16[2,128,512]{2,1,0:T(8,128)(2,1)S(1)} collective-permute-done((bf16[2,128,512]{2,1,0:T(8,128)(2,1)S(1)}, bf16[2,128,512]{2,1,0:T(8,128)(2,1)S(1)}, u32[]{:S(2)}, u32[]{:S(2)}) %collective-permute-start.17) | collective-permute-done | bytes 262176 | tf_op jit(solution)/shard_map/ppermute | solution.py:396
  70.9 0.0 collective-permute-done.18.refs_3_
  70.9 1.0 %merge.3 = (bf16[128,2048]{1,0:T(8,128)(2,1)}, bf16[128,2048]{1,0:T(8,128)(2,1)}) custom-call(bf16[2,128,512]{2,1,0:T(8,128)(2,1)S(1)} %get-tuple-element.55.refs_0_, bf16[2,128,512]{2,1,0:T(8,128)(2,1)S(1)} %collective-permute-done.16.refs_1_, bf16[2,128,512]{2,1,0:T(8,128)(2,1)S(1)} %collective-permute-done.17.refs_2_, ...), custom_call_target="tpu_custom_call" | custom-call | tf_op jit(solution)/shard_map/merge/pallas_call | solution.py:113
  (1 shorter events, 0.0 us)
Async XLA Ops:
  0.6 1.0 %copy-start = (bf16[128,2048]{1,0:T(8,128)(2,1)S(1)}, bf16[128,2048]{1,0:T(8,128)(2,1)}, u32[]{:S(2)}) copy-start(bf16[128,2048]{1,0:T(8,128)(2,1)} %refs_0_.2) | copy-start | bytes 1572868
  1.7 1.0 %copy-start.1 = (bf16[128,2048]{1,0:T(8,128)(2,1)S(1)}, bf16[128,2048]{1,0:T(8,128)(2,1)}, u32[]{:S(2)}) copy-start(bf16[128,2048]{1,0:T(8,128)(2,1)} %refs_1_.2) | copy-start | bytes 1572868
  3.0 10.4 %collective-permute-start = (bf16[2,128,512]{2,1,0:T(8,128)(2,1)S(1)}, bf16[2,128,512]{2,1,0:T(8,128)(2,1)S(1)}, u32[]{:S(2)}, u32[]{:S(2)}) collective-permute-start(bf16[2,128,512]{2,1,0:T(8,128)(2,1)S(1)} %get-tuple-element.33), channel_id=1, source_target_pairs={{0,8},{8,0},{16,24},{24,16},{1,9},{9,1},{17,25},{25,17},{2,10},{10... | collective-permute-start | bytes 786440 | tf_op jit(solution)/shard_map/ppermute | solution.py:396
  6.0 10.2 %collective-permute-start.1 = (bf16[2,128,512]{2,1,0:T(8,128)(2,1)S(1)}, bf16[2,128,512]{2,1,0:T(8,128)(2,1)S(1)}, u32[]{:S(2)}, u32[]{:S(2)}) collective-permute-start(bf16[2,128,512]{2,1,0:T(8,128)(2,1)S(1)} %get-tuple-element.34), channel_id=1, source_target_pairs={{0,16},{8,24},{16,0},{24,8},{1,17},{9,25},{17,1},{25,9},{2,18},{10... | collective-permute-start | bytes 786440 | tf_op jit(solution)/shard_map/ppermute | solution.py:396
  7.5 1.0 %copy-start.2 = (bf16[128,2048]{1,0:T(8,128)(2,1)S(1)}, bf16[128,2048]{1,0:T(8,128)(2,1)}, u32[]{:S(2)}) copy-start(bf16[128,2048]{1,0:T(8,128)(2,1)} %refs_0_.3) | copy-start | bytes 1572868
  8.5 1.0 %copy-start.3 = (bf16[128,2048]{1,0:T(8,128)(2,1)S(1)}, bf16[128,2048]{1,0:T(8,128)(2,1)}, u32[]{:S(2)}) copy-start(bf16[128,2048]{1,0:T(8,128)(2,1)} %refs_1_.3) | copy-start | bytes 1572868
  9.8 9.3 %collective-permute-start.3 = (bf16[2,128,512]{2,1,0:T(8,128)(2,1)S(1)}, bf16[2,128,512]{2,1,0:T(8,128)(2,1)S(1)}, u32[]{:S(2)}, u32[]{:S(2)}) collective-permute-start(bf16[2,128,512]{2,1,0:T(8,128)(2,1)S(1)} %get-tuple-element.37), channel_id=1, source_target_pairs={{0,8},{8,0},{16,24},{24,16},{1,9},{9,1},{17,25},{25,17},{2,10},{10... | collective-permute-start | bytes 786440 | tf_op jit(solution)/shard_map/ppermute | solution.py:396
  10.4 15.5 %collective-permute-start.2 = (bf16[2,128,512]{2,1,0:T(8,128)(2,1)S(1)}, bf16[2,128,512]{2,1,0:T(8,128)(2,1)S(1)}, u32[]{:S(2)}, u32[]{:S(2)}) collective-permute-start(bf16[2,128,512]{2,1,0:T(8,128)(2,1)S(1)} %get-tuple-element.35), channel_id=1, source_target_pairs={{0,24},{8,16},{16,8},{24,0},{1,25},{9,17},{17,9},{25,1},{2,26},{10... | collective-permute-start | bytes 786440 | tf_op jit(solution)/shard_map/ppermute | solution.py:396
  11.8 18.7 %collective-permute-start.4 = (bf16[2,128,512]{2,1,0:T(8,128)(2,1)S(1)}, bf16[2,128,512]{2,1,0:T(8,128)(2,1)S(1)}, u32[]{:S(2)}, u32[]{:S(2)}) collective-permute-start(bf16[2,128,512]{2,1,0:T(8,128)(2,1)S(1)} %get-tuple-element.38), channel_id=1, source_target_pairs={{0,16},{8,24},{16,0},{24,8},{1,17},{9,25},{17,1},{25,9},{2,18},{10... | collective-permute-start | bytes 786440 | tf_op jit(solution)/shard_map/ppermute | solution.py:396
  13.4 17.2 %collective-permute-start.5 = (bf16[2,128,512]{2,1,0:T(8,128)(2,1)S(1)}, bf16[2,128,512]{2,1,0:T(8,128)(2,1)S(1)}, u32[]{:S(2)}, u32[]{:S(2)}) collective-permute-start(bf16[2,128,512]{2,1,0:T(8,128)(2,1)S(1)} %get-tuple-element.39), channel_id=1, source_target_pairs={{0,24},{8,16},{16,8},{24,0},{1,25},{9,17},{17,9},{25,1},{2,26},{10... | collective-permute-start | bytes 786440 | tf_op jit(solution)/shard_map/ppermute | solution.py:396
  16.3 15.8 %collective-permute-start.6 = (bf16[3,2,128,512]{3,2,1,0:T(8,128)(2,1)S(1)}, bf16[3,2,128,512]{3,2,1,0:T(8,128)(2,1)S(1)}, u32[]{:S(2)}, u32[]{:S(2)}) collective-permute-start(bf16[3,2,128,512]{3,2,1,0:T(8,128)(2,1)S(1)} %stack.20), channel_id=1, source_target_pairs={{1,2},{3,4},{5,6},{2,1},{4,3},{6,5},{9,10},{11,12},{13,14},{10,9},... | collective-permute-start | bytes 2359304 | tf_op jit(solution)/shard_map/ppermute | solution.py:390
  19.1 13.0 %collective-permute-start.8 = (bf16[3,2,128,512]{3,2,1,0:T(8,128)(2,1)S(1)}, bf16[3,2,128,512]{3,2,1,0:T(8,128)(2,1)S(1)}, u32[]{:S(2)}, u32[]{:S(2)}) collective-permute-start(bf16[3,2,128,512]{3,2,1,0:T(8,128)(2,1)S(1)} %stack.20), channel_id=1, source_target_pairs={{0,1},{2,3},{4,5},{6,7},{1,0},{3,2},{5,4},{7,6},{8,9},{10,11},{12,... | collective-permute-start | bytes 2359304 | tf_op jit(solution)/shard_map/ppermute | solution.py:390
  26.0 5.5 %collective-permute-start.7 = (bf16[1,2,128,512]{3,2,1,0:T(8,128)(2,1)S(1)}, bf16[1,2,128,512]{3,2,1,0:T(8,128)(2,1)S(1)}, u32[]{:S(2)}, u32[]{:S(2)}) collective-permute-start(bf16[1,2,128,512]{3,2,1,0:T(8,128)(2,1)S(1)} %bitcast.3), channel_id=1, source_target_pairs={{1,2},{3,4},{5,6},{2,1},{4,3},{6,5},{9,10},{11,12},{13,14},{10,9},... | collective-permute-start | bytes 786440 | tf_op jit(solution)/shard_map/ppermute | solution.py:390
  30.6 1.5 %collective-permute-start.9 = (bf16[1,2,128,512]{3,2,1,0:T(8,128)(2,1)S(1)}, bf16[1,2,128,512]{3,2,1,0:T(8,128)(2,1)S(1)}, u32[]{:S(2)}, u32[]{:S(2)}) collective-permute-start(bf16[1,2,128,512]{3,2,1,0:T(8,128)(2,1)S(1)} %bitcast.4), channel_id=1, source_target_pairs={{0,1},{2,3},{4,5},{6,7},{1,0},{3,2},{5,4},{7,6},{8,9},{10,11},{12,... | collective-permute-start | bytes 786440 | tf_op jit(solution)/shard_map/ppermute | solution.py:390
  30.7 18.9 %collective-permute-start.13 = (bf16[4,2,128,512]{3,2,1,0:T(8,128)(2,1)S(1)}, bf16[4,2,128,512]{3,2,1,0:T(8,128)(2,1)S(1)}, u32[]{:S(2)}, u32[]{:S(2)}) collective-permute-start(bf16[4,2,128,512]{3,2,1,0:T(8,128)(2,1)S(1)} %stack.19.refs_7_), channel_id=1, source_target_pairs={{1,2},{3,4},{5,6},{2,1},{4,3},{6,5},{9,10},{11,12},{13,14},{10,9},... | collective-permute-start | bytes 3145736 | tf_op jit(solution)/shard_map/ppermute | solution.py:390
  43.1 6.5 %collective-permute-start.15 = (bf16[2,512,512]{2,1,0:T(8,128)(2,1)S(1)}, bf16[2,512,512]{2,1,0:T(8,128)(2,1)S(1)}, u32[]{:S(2)}, u32[]{:S(2)}) collective-permute-start(bf16[2,512,512]{2,1,0:T(8,128)(2,1)S(1)} %get-tuple-element.46), channel_id=1, source_target_pairs={{0,1},{2,3},{4,5},{6,7},{1,0},{3,2},{5,4},{7,6},{8,9},{10,11},{12,... | collective-permute-start | bytes 3145736 | tf_op jit(solution)/shard_map/ppermute | solution.py:390
  45.4 2.8 %collective-permute-start.14 = (f32[4,2,512]{2,1,0:T(2,128)S(1)}, f32[4,2,512]{2,1,0:T(2,128)S(1)}, u32[]{:S(2)}, u32[]{:S(2)}) collective-permute-start(f32[4,2,512]{2,1,0:T(2,128)S(1)} %get-tuple-element.44), channel_id=1, source_target_pairs={{1,2},{3,4},{5,6},{2,1},{4,3},{6,5},{9,10},{11,12},{13,14},{10,9},... | collective-permute-start | bytes 49160 | tf_op jit(solution)/shard_map/ppermute | solution.py:390
  46.0 7.0 %collective-permute-start.10 = (bf16[128,512]{1,0:T(8,128)(2,1)S(1)}, bf16[128,512]{1,0:T(8,128)(2,1)S(1)}, u32[]{:S(2)}, u32[]{:S(2)}) collective-permute-start(bf16[128,512]{1,0:T(8,128)(2,1)S(1)} %get-tuple-element.41), channel_id=1, source_target_pairs={{0,8},{8,0},{16,24},{24,16},{1,9},{9,1},{17,25},{25,17},{2,10},{10... | collective-permute-start | bytes 393224 | tf_op jit(solution)/shard_map/ppermute | solution.py:396
  47.3 5.7 %collective-permute-start.11 = (bf16[128,512]{1,0:T(8,128)(2,1)S(1)}, bf16[128,512]{1,0:T(8,128)(2,1)S(1)}, u32[]{:S(2)}, u32[]{:S(2)}) collective-permute-start(bf16[128,512]{1,0:T(8,128)(2,1)S(1)} %get-tuple-element.42), channel_id=1, source_target_pairs={{0,16},{8,24},{16,0},{24,8},{1,17},{9,25},{17,1},{25,9},{2,18},{10... | collective-permute-start | bytes 393224 | tf_op jit(solution)/shard_map/ppermute | solution.py:396
  48.1 7.3 %collective-permute-start.12 = (bf16[128,512]{1,0:T(8,128)(2,1)S(1)}, bf16[128,512]{1,0:T(8,128)(2,1)S(1)}, u32[]{:S(2)}, u32[]{:S(2)}) collective-permute-start(bf16[128,512]{1,0:T(8,128)(2,1)S(1)} %get-tuple-element.43), channel_id=1, source_target_pairs={{0,24},{8,16},{16,8},{24,0},{1,25},{9,17},{17,9},{25,1},{2,26},{10... | collective-permute-start | bytes 393224 | tf_op jit(solution)/shard_map/ppermute | solution.py:396
  55.4 8.9 %collective-permute-start.16 = (bf16[2,128,512]{2,1,0:T(8,128)(2,1)S(1)}, bf16[2,128,512]{2,1,0:T(8,128)(2,1)S(1)}, u32[]{:S(2)}, u32[]{:S(2)}) collective-permute-start(bf16[2,128,512]{2,1,0:T(8,128)(2,1)S(1)} %get-tuple-element.56), channel_id=1, source_target_pairs={{0,8},{8,0},{16,24},{24,16},{1,9},{9,1},{17,25},{25,17},{2,10},{10... | collective-permute-start | bytes 786440 | tf_op jit(solution)/shard_map/ppermute | solution.py:396
  56.3 14.6 %collective-permute-start.17 = (bf16[2,128,512]{2,1,0:T(8,128)(2,1)S(1)}, bf16[2,128,512]{2,1,0:T(8,128)(2,1)S(1)}, u32[]{:S(2)}, u32[]{:S(2)}) collective-permute-start(bf16[2,128,512]{2,1,0:T(8,128)(2,1)S(1)} %get-tuple-element.57), channel_id=1, source_target_pairs={{0,16},{8,24},{16,0},{24,8},{1,17},{9,25},{17,1},{25,9},{2,18},{10... | collective-permute-start | bytes 786440 | tf_op jit(solution)/shard_map/ppermute | solution.py:396
  57.5 13.4 %collective-permute-start.18 = (bf16[2,128,512]{2,1,0:T(8,128)(2,1)S(1)}, bf16[2,128,512]{2,1,0:T(8,128)(2,1)S(1)}, u32[]{:S(2)}, u32[]{:S(2)}) collective-permute-start(bf16[2,128,512]{2,1,0:T(8,128)(2,1)S(1)} %get-tuple-element.58), channel_id=1, source_target_pairs={{0,24},{8,16},{16,8},{24,0},{1,25},{9,17},{17,9},{25,1},{2,26},{10... | collective-permute-start | bytes 786440 | tf_op jit(solution)/shard_map/ppermute | solution.py:396

commit v5 on v4

--- a/solution.py
+++ b/solution.py
@@ -106,7 +106,7 @@
         copy.wait()
 
 
-def merged(pieces):
+def merged(pieces, flops=0):
     n = len(pieces)
     r, width = pieces[0].shape[-2:]
     count = 1 if pieces[0].ndim == 2 else 2
@@ -117,6 +117,7 @@
         out_shape=[jax.ShapeDtypeStruct((r, n * width), pieces[0].dtype)] * count,
         scratch_shapes=[pltpu.SemaphoreType.DMA((count * n,))],
         compiler_params=pltpu.CompilerParams(vmem_limit_bytes=SMALL_BYTES),
+        cost_estimate=pl.CostEstimate(flops=flops, bytes_accessed=0, transcendentals=0),
         name="merge",
     )(*pieces)
 
@@ -376,7 +377,7 @@
         out_shape=[jax.ShapeDtypeStruct((2, r, width), jnp.bfloat16)] * n,
         compiler_params=pltpu.CompilerParams(vmem_limit_bytes=VMEM_BYTES),
         cost_estimate=pl.CostEstimate(
-            flops=8 * heads * HALF * (HALF // 2 + SUB // 2) * HEAD_DIM,
+            flops=HINT,
             bytes_accessed=24 * rows * width,
             transcendentals=heads * HALF * (HALF // 2 + SUB // 2),
         ),
@@ -392,9 +393,11 @@
 
 def exchanged(pieces):
     n = len(pieces)
-    return [pieces[0]] + [
-        lax.ppermute(pieces[k], "head", [(i, i ^ k) for i in range(n)]) for k in range(1, n)
-    ]
+    moved = {
+        k: lax.ppermute(pieces[k], "head", [(i, i ^ k) for i in range(n)])
+        for k in range(1, n)
+    }
+    return [pieces[0]] + [moved[k] for k in range(1, n)]
 
 
 def shards(query, key_in, value, grad_out):
@@ -419,18 +422,19 @@
         kv_near = [swapped(group, 0) for group in groups]
         qd = stacked(qd, HINT)
         qd_far = swapped(qd, 1)
+        key_halo = place
     else:
         local, qd = jnp.stack(kv), jnp.stack(qd)
         local = jnp.take(local, place, axis=0)
         kv_far = [swapped(local[:blocks], 1)]
         kv_near = [swapped(local[n - blocks:], 0)]
         qd_far = swapped(jnp.take(qd, place[:blocks], axis=0), 1)
+        key_halo = halo
     dq, stat, part, give = query_part(place, halo, turn, kv, qd, kv_far, kv_near)
     stat_far = swapped(stat[:, :, :HALF], 1)
     got = swapped(give, 0)
-    dkv = key_part(place, halo, turn, kv, qd_far, stat_far, part, got)
-    dq, dkv = lax.optimization_barrier((exchanged(dq), dkv))
-    return *merged(dq), *merged(exchanged(dkv))
+    dkv = key_part(place, key_halo, turn, kv, qd_far, stat_far, part, got)
+    return *merged(exchanged(dq), HINT), *merged(exchanged(dkv))
 
 
 def solution(mesh):

time: 72.3 us -> 70.2 us (0.971)
  the two profiles are of different devices: /device:TPU:0 before, /device:TPU:8 now
where the time goes in v5:
time: 70.2 us; the launch traced here: 69.9 us
  starting transfers between devices  26.4 us (38%)
  waiting for transfers between devices  21.6 us (31%)
  Pallas kernels  16.9 us (24%)
  local copies, waits for them, and re-layouts  4.16 us (6%)
  between operations  0.75 us (1%)
    ppermute x12, waiting for transfers between devices, exchanged(): lax.ppermute(pieces[k], 'head', [(i, i ^ k) for i in range(n)])  20.2 us
    ppermute x12, starting transfers between devices, exchanged(): lax.ppermute(pieces[k], 'head', [(i, i ^ k) for i in range(n)])  16.5 us
    pallas_call x1, Pallas kernels, query_part(): pl.pallas_call(lambda *refs: query_kernel(n, len(far), *refs), in_specs=[...  11 us
    ppermute x7, starting transfers between devices, swapped(): return lax.ppermute(array, 'blk', pairs + [(j, i) for i, j in pairs])  9.88 us
    unnamed x8, local copies, waits for them, and re-layouts  4.16 us
    pallas_call x1, Pallas kernels, key_part(): pl.pallas_call(lambda *refs: key_kernel(n, *refs), in_specs=[scalars] * 3...  3.4 us
    pallas_call x2, Pallas kernels, merged(): pl.pallas_call(lambda *refs: merge_kernel(n, *refs), in_specs=[pl.BlockSp...  1.84 us
  transfers between devices with their start and end apart: 19, of which 7 were waited for; matrix products, arithmetic and copies ran while one was open for 0% of the time, Pallas kernels for 22%

profile of v5, /device:TPU:8, one launch (start us, length us, event | category | flops | bytes accessed | tf_op | source)
XLA Modules:
  0.0 69.9 jit_solution(9627375509463329557)
XLA Ops:
  0.6 0.0 copy-start
  0.6 1.0 %copy-done = bf16[128,2048]{1,0:T(8,128)(2,1)S(1)} copy-done((bf16[128,2048]{1,0:T(8,128)(2,1)S(1)}, bf16[128,2048]{1,0:T(8,128)(2,1)}, u32[]{:S(2)}) %copy-start) | copy-done | bytes 524312
  1.7 0.0 copy-start.1
  1.7 1.0 %copy-done.1 = bf16[128,2048]{1,0:T(8,128)(2,1)S(1)} copy-done((bf16[128,2048]{1,0:T(8,128)(2,1)S(1)}, bf16[128,2048]{1,0:T(8,128)(2,1)}, u32[]{:S(2)}) %copy-start.1) | copy-done | bytes 524312
  2.7 0.2 pack.2
  3.0 1.6 %collective-permute-start = (bf16[2,128,512]{2,1,0:T(8,128)(2,1)S(1)}, bf16[2,128,512]{2,1,0:T(8,128)(2,1)S(1)}, u32[]{:S(2)}, u32[]{:S(2)}) collective-permute-start(bf16[2,128,512]{2,1,0:T(8,128)(2,1)S(1)} %get-tuple-element.25), channel_id=1, source_target_pairs={{0,8},{8,0},{16,24},{24,16},{1,9},{9,1},{17,25},{25,17},{2,10},{10... | collective-permute-start | bytes 786440 | tf_op jit(solution)/shard_map/ppermute | solution.py:397
  4.5 1.5 %collective-permute-start.1 = (bf16[2,128,512]{2,1,0:T(8,128)(2,1)S(1)}, bf16[2,128,512]{2,1,0:T(8,128)(2,1)S(1)}, u32[]{:S(2)}, u32[]{:S(2)}) collective-permute-start(bf16[2,128,512]{2,1,0:T(8,128)(2,1)S(1)} %get-tuple-element.26), channel_id=1, source_target_pairs={{0,16},{8,24},{16,0},{24,8},{1,17},{9,25},{17,1},{25,9},{2,18},{10... | collective-permute-start | bytes 786440 | tf_op jit(solution)/shard_map/ppermute | solution.py:397
  6.0 0.0 copy-start.2
  6.0 1.0 %copy-done.2 = bf16[128,2048]{1,0:T(8,128)(2,1)S(1)} copy-done((bf16[128,2048]{1,0:T(8,128)(2,1)S(1)}, bf16[128,2048]{1,0:T(8,128)(2,1)}, u32[]{:S(2)}) %copy-start.2) | copy-done | bytes 524312
  7.1 0.0 copy-start.3
  7.1 1.0 %copy-done.3 = bf16[128,2048]{1,0:T(8,128)(2,1)S(1)} copy-done((bf16[128,2048]{1,0:T(8,128)(2,1)S(1)}, bf16[128,2048]{1,0:T(8,128)(2,1)}, u32[]{:S(2)}) %copy-start.3) | copy-done | bytes 524312
  8.1 0.2 pack.3
  8.4 0.6 collective-permute-start.3
  9.0 1.4 %collective-permute-start.2 = (bf16[2,128,512]{2,1,0:T(8,128)(2,1)S(1)}, bf16[2,128,512]{2,1,0:T(8,128)(2,1)S(1)}, u32[]{:S(2)}, u32[]{:S(2)}) collective-permute-start(bf16[2,128,512]{2,1,0:T(8,128)(2,1)S(1)} %get-tuple-element.27), channel_id=1, source_target_pairs={{0,24},{8,16},{16,8},{24,0},{1,25},{9,17},{17,9},{25,1},{2,26},{10... | collective-permute-start | bytes 786440 | tf_op jit(solution)/shard_map/ppermute | solution.py:397
  10.4 1.5 %collective-permute-start.4 = (bf16[2,128,512]{2,1,0:T(8,128)(2,1)S(1)}, bf16[2,128,512]{2,1,0:T(8,128)(2,1)S(1)}, u32[]{:S(2)}, u32[]{:S(2)}) collective-permute-start(bf16[2,128,512]{2,1,0:T(8,128)(2,1)S(1)} %get-tuple-element.30), channel_id=1, source_target_pairs={{0,16},{8,24},{16,0},{24,8},{1,17},{9,25},{17,1},{25,9},{2,18},{10... | collective-permute-start | bytes 786440 | tf_op jit(solution)/shard_map/ppermute | solution.py:397
  11.9 0.0 collective-permute-done.refs_1_.refs_4_
  11.9 2.7 %collective-permute-start.5 = (bf16[2,128,512]{2,1,0:T(8,128)(2,1)S(1)}, bf16[2,128,512]{2,1,0:T(8,128)(2,1)S(1)}, u32[]{:S(2)}, u32[]{:S(2)}) collective-permute-start(bf16[2,128,512]{2,1,0:T(8,128)(2,1)S(1)} %get-tuple-element.31), channel_id=1, source_target_pairs={{0,24},{8,16},{16,8},{24,0},{1,25},{9,17},{17,9},{25,1},{2,26},{10... | collective-permute-start | bytes 786440 | tf_op jit(solution)/shard_map/ppermute | solution.py:397
  14.7 0.1 pad_add_fusion.refs_2_
  14.7 0.0 collective-permute-done.1.refs_2_.refs_5_
  14.7 0.1 stack.20
  14.8 1.9 %collective-permute-start.6 = (bf16[3,2,128,512]{3,2,1,0:T(8,128)(2,1)S(1)}, bf16[3,2,128,512]{3,2,1,0:T(8,128)(2,1)S(1)}, u32[]{:S(2)}, u32[]{:S(2)}) collective-permute-start(bf16[3,2,128,512]{3,2,1,0:T(8,128)(2,1)S(1)} %stack.20), channel_id=1, source_target_pairs={{1,2},{3,4},{5,6},{2,1},{4,3},{6,5},{9,10},{11,12},{13,14},{10,9},... | collective-permute-start | bytes 2359304 | tf_op jit(solution)/shard_map/ppermute | solution.py:391
  16.8 0.9 %collective-permute-done.3.refs_1_ = bf16[2,128,512]{2,1,0:T(8,128)(2,1)S(1)} collective-permute-done((bf16[2,128,512]{2,1,0:T(8,128)(2,1)S(1)}, bf16[2,128,512]{2,1,0:T(8,128)(2,1)S(1)}, u32[]{:S(2)}, u32[]{:S(2)}) %collective-permute-start.3) | collective-permute-done | bytes 262176 | tf_op jit(solution)/shard_map/ppermute | solution.py:397
  17.7 0.8 %collective-permute-start.8 = (bf16[3,2,128,512]{3,2,1,0:T(8,128)(2,1)S(1)}, bf16[3,2,128,512]{3,2,1,0:T(8,128)(2,1)S(1)}, u32[]{:S(2)}, u32[]{:S(2)}) collective-permute-start(bf16[3,2,128,512]{3,2,1,0:T(8,128)(2,1)S(1)} %stack.20), channel_id=1, source_target_pairs={{0,1},{2,3},{4,5},{6,7},{1,0},{3,2},{5,4},{7,6},{8,9},{10,11},{12,... | collective-permute-start | bytes 2359304 | tf_op jit(solution)/shard_map/ppermute | solution.py:391
  18.5 6.0 %collective-permute-done.2.refs_6_ = bf16[2,128,512]{2,1,0:T(8,128)(2,1)S(1)} collective-permute-done((bf16[2,128,512]{2,1,0:T(8,128)(2,1)S(1)}, bf16[2,128,512]{2,1,0:T(8,128)(2,1)S(1)}, u32[]{:S(2)}, u32[]{:S(2)}) %collective-permute-start.2) | collective-permute-done | bytes 262176 | tf_op jit(solution)/shard_map/ppermute | solution.py:397
  24.5 1.9 %collective-permute-start.7 = (bf16[1,2,128,512]{3,2,1,0:T(8,128)(2,1)S(1)}, bf16[1,2,128,512]{3,2,1,0:T(8,128)(2,1)S(1)}, u32[]{:S(2)}, u32[]{:S(2)}) collective-permute-start(bf16[1,2,128,512]{3,2,1,0:T(8,128)(2,1)S(1)} %bitcast.3), channel_id=1, source_target_pairs={{1,2},{3,4},{5,6},{2,1},{4,3},{6,5},{9,10},{11,12},{13,14},{10,9},... | collective-permute-start | bytes 786440 | tf_op jit(solution)/shard_map/ppermute | solution.py:391
  26.4 2.7 %collective-permute-done.4.refs_2_ = bf16[2,128,512]{2,1,0:T(8,128)(2,1)S(1)} collective-permute-done((bf16[2,128,512]{2,1,0:T(8,128)(2,1)S(1)}, bf16[2,128,512]{2,1,0:T(8,128)(2,1)S(1)}, u32[]{:S(2)}, u32[]{:S(2)}) %collective-permute-start.4) | collective-permute-done | bytes 262176 | tf_op jit(solution)/shard_map/ppermute | solution.py:397
  29.1 0.0 collective-permute-start.9
  29.1 0.0 collective-permute-done.5.refs_3_
  29.1 0.1 stack.19.refs_7_
  29.3 2.5 %collective-permute-start.13 = (bf16[4,2,128,512]{3,2,1,0:T(8,128)(2,1)S(1)}, bf16[4,2,128,512]{3,2,1,0:T(8,128)(2,1)S(1)}, u32[]{:S(2)}, u32[]{:S(2)}) collective-permute-start(bf16[4,2,128,512]{3,2,1,0:T(8,128)(2,1)S(1)} %stack.19.refs_7_), channel_id=1, source_target_pairs={{1,2},{3,4},{5,6},{2,1},{4,3},{6,5},{9,10},{11,12},{13,14},{10,9},... | collective-permute-start | bytes 3145736 | tf_op jit(solution)/shard_map/ppermute | solution.py:391
  31.7 0.4 collective-permute-done.7.refs_9_
  32.2 0.0 collective-permute-done.9.refs_11_
  32.2 0.0 collective-permute-done.6.refs_8_
  32.2 0.0 collective-permute-done.8.refs_10_
  32.2 11.0 %query_part.1 = (bf16[128,512]{1,0:T(8,128)(2,1)S(1)}, bf16[128,512]{1,0:T(8,128)(2,1)S(1)}, bf16[128,512]{1,0:T(8,128)(2,1)S(1)}, bf16[128,512]{1,0:T(8,128)(2,...) custom-call(s32[4]{0:T(128)S(1)} %xor_xor_fusion.refs_0_.refs_1_, ...), custom_call_target="tpu_custom_call" | custom-call | flops 3355443200 | bytes 3145728 | tf_op jit(solution)/shard_map/query_part/pallas_call | solution.py:285
  43.2 0.8 %collective-permute-start.15 = (bf16[2,512,512]{2,1,0:T(8,128)(2,1)S(1)}, bf16[2,512,512]{2,1,0:T(8,128)(2,1)S(1)}, u32[]{:S(2)}, u32[]{:S(2)}) collective-permute-start(bf16[2,512,512]{2,1,0:T(8,128)(2,1)S(1)} %get-tuple-element.38), channel_id=1, source_target_pairs={{0,1},{2,3},{4,5},{6,7},{1,0},{3,2},{5,4},{7,6},{8,9},{10,11},{12,... | collective-permute-start | bytes 3145736 | tf_op jit(solution)/shard_map/ppermute | solution.py:391
  43.9 2.0 %collective-permute-start.14 = (f32[4,2,512]{2,1,0:T(2,128)S(1)}, f32[4,2,512]{2,1,0:T(2,128)S(1)}, u32[]{:S(2)}, u32[]{:S(2)}) collective-permute-start(f32[4,2,512]{2,1,0:T(2,128)S(1)} %get-tuple-element.36), channel_id=1, source_target_pairs={{1,2},{3,4},{5,6},{2,1},{4,3},{6,5},{9,10},{11,12},{13,14},{10,9},... | collective-permute-start | bytes 49160 | tf_op jit(solution)/shard_map/ppermute | solution.py:391
  45.9 1.3 %collective-permute-start.10 = (bf16[128,512]{1,0:T(8,128)(2,1)S(1)}, bf16[128,512]{1,0:T(8,128)(2,1)S(1)}, u32[]{:S(2)}, u32[]{:S(2)}) collective-permute-start(bf16[128,512]{1,0:T(8,128)(2,1)S(1)} %get-tuple-element.33), channel_id=1, source_target_pairs={{0,8},{8,0},{16,24},{24,16},{1,9},{9,1},{17,25},{25,17},{2,10},{10... | collective-permute-start | bytes 393224 | tf_op jit(solution)/shard_map/ppermute | solution.py:397
  47.2 0.8 %collective-permute-start.11 = (bf16[128,512]{1,0:T(8,128)(2,1)S(1)}, bf16[128,512]{1,0:T(8,128)(2,1)S(1)}, u32[]{:S(2)}, u32[]{:S(2)}) collective-permute-start(bf16[128,512]{1,0:T(8,128)(2,1)S(1)} %get-tuple-element.34), channel_id=1, source_target_pairs={{0,16},{8,24},{16,0},{24,8},{1,17},{9,25},{17,1},{25,9},{2,18},{10... | collective-permute-start | bytes 393224 | tf_op jit(solution)/shard_map/ppermute | solution.py:397
  48.0 0.9 %collective-permute-done.14.refs_8_ = f32[4,2,512]{2,1,0:T(2,128)S(1)} collective-permute-done((f32[4,2,512]{2,1,0:T(2,128)S(1)}, f32[4,2,512]{2,1,0:T(2,128)S(1)}, u32[]{:S(2)}, u32[]{:S(2)}) %collective-permute-start.14) | collective-permute-done | bytes 16416 | tf_op jit(solution)/shard_map/ppermute | solution.py:391
  49.0 1.5 %collective-permute-start.12 = (bf16[128,512]{1,0:T(8,128)(2,1)S(1)}, bf16[128,512]{1,0:T(8,128)(2,1)S(1)}, u32[]{:S(2)}, u32[]{:S(2)}) collective-permute-start(bf16[128,512]{1,0:T(8,128)(2,1)S(1)} %get-tuple-element.35), channel_id=1, source_target_pairs={{0,24},{8,16},{16,8},{24,0},{1,25},{9,17},{17,9},{25,1},{2,26},{10... | collective-permute-start | bytes 393224 | tf_op jit(solution)/shard_map/ppermute | solution.py:397
  50.5 0.0 collective-permute-done.13.refs_7_
  50.5 0.0 collective-permute-done.15.refs_10_
  50.5 3.4 %key_part.1 = (bf16[2,128,512]{2,1,0:T(8,128)(2,1)S(1)}, bf16[2,128,512]{2,1,0:T(8,128)(2,1)S(1)}, bf16[2,128,512]{2,1,0:T(8,128)(2,1)S(1)}, bf16[2,128,512]{2,1,0:T(8,128)(2,1)S(1)}) custom-call(s32[4]{0:T(128)S(1)} %xor_xor_fusion.refs_0_.refs_1_, s32[4]{0:T(128)S(1)} %xor_xor_fusion.refs_0_.refs_1_, s32[2]{0:T(128)S(1)} %pad_add_fusion.refs_2_, ...), custom_call_target="tpu_custom_call" | custom-call | flops 30000001024 | bytes 6291456 | tf_op jit(solution)/shard_map/key_part/pallas_call | solution.py:364
  53.9 1.6 %collective-permute-start.16 = (bf16[2,128,512]{2,1,0:T(8,128)(2,1)S(1)}, bf16[2,128,512]{2,1,0:T(8,128)(2,1)S(1)}, u32[]{:S(2)}, u32[]{:S(2)}) collective-permute-start(bf16[2,128,512]{2,1,0:T(8,128)(2,1)S(1)} %get-tuple-element.40), channel_id=1, source_target_pairs={{0,8},{8,0},{16,24},{24,16},{1,9},{9,1},{17,25},{25,17},{2,10},{10... | collective-permute-start | bytes 786440 | tf_op jit(solution)/shard_map/ppermute | solution.py:397
  55.4 0.5 collective-permute-start.17
  55.9 0.0 collective-permute-done.10.refs_1_
  55.9 1.5 %collective-permute-start.18 = (bf16[2,128,512]{2,1,0:T(8,128)(2,1)S(1)}, bf16[2,128,512]{2,1,0:T(8,128)(2,1)S(1)}, u32[]{:S(2)}, u32[]{:S(2)}) collective-permute-start(bf16[2,128,512]{2,1,0:T(8,128)(2,1)S(1)} %get-tuple-element.42), channel_id=1, source_target_pairs={{0,24},{8,16},{16,8},{24,0},{1,25},{9,17},{17,9},{25,1},{2,26},{10... | collective-permute-start | bytes 786440 | tf_op jit(solution)/shard_map/ppermute | solution.py:397
  57.4 0.0 collective-permute-done.11.refs_2_
  57.4 0.0 collective-permute-done.12.refs_3_
  57.4 0.8 %merge.2 = bf16[128,2048]{1,0:T(8,128)(2,1)} custom-call(bf16[128,512]{1,0:T(8,128)(2,1)S(1)} %get-tuple-element.32.refs_0_, bf16[128,512]{1,0:T(8,128)(2,1)S(1)} %collective-permute-done.10.refs_1_, bf16[128,512]{1,0:T(8,128)(2,1)S(1)} %collective-permute-done.11.refs_2_, bf16[128,512]{1,0:T(8,128)(2,1)S(1)} %collective-permute-done.12.refs_3_), custom_call_target="tpu_custom_call" | custom-call | flops 30000001024 | tf_op jit(solution)/shard_map/merge/pallas_call | solution.py:113
  58.3 4.9 %collective-permute-done.16.refs_1_ = bf16[2,128,512]{2,1,0:T(8,128)(2,1)S(1)} collective-permute-done((bf16[2,128,512]{2,1,0:T(8,128)(2,1)S(1)}, bf16[2,128,512]{2,1,0:T(8,128)(2,1)S(1)}, u32[]{:S(2)}, u32[]{:S(2)}) %collective-permute-start.16) | collective-permute-done | bytes 262176 | tf_op jit(solution)/shard_map/ppermute | solution.py:397
  63.1 5.7 %collective-permute-done.17.refs_2_ = bf16[2,128,512]{2,1,0:T(8,128)(2,1)S(1)} collective-permute-done((bf16[2,128,512]{2,1,0:T(8,128)(2,1)S(1)}, bf16[2,128,512]{2,1,0:T(8,128)(2,1)S(1)}, u32[]{:S(2)}, u32[]{:S(2)}) %collective-permute-start.17) | collective-permute-done | bytes 262176 | tf_op jit(solution)/shard_map/ppermute | solution.py:397
  68.8 0.0 collective-permute-done.18.refs_3_
  68.8 1.0 %merge.3 = (bf16[128,2048]{1,0:T(8,128)(2,1)}, bf16[128,2048]{1,0:T(8,128)(2,1)}) custom-call(bf16[2,128,512]{2,1,0:T(8,128)(2,1)S(1)} %get-tuple-element.39.refs_0_, bf16[2,128,512]{2,1,0:T(8,128)(2,1)S(1)} %collective-permute-done.16.refs_1_, bf16[2,128,512]{2,1,0:T(8,128)(2,1)S(1)} %collective-permute-done.17.refs_2_, ...), custom_call_target="tpu_custom_call" | custom-call | tf_op jit(solution)/shard_map/merge/pallas_call | solution.py:113
  (1 shorter events, 0.0 us)
Async XLA Ops:
  0.6 1.0 %copy-start = (bf16[128,2048]{1,0:T(8,128)(2,1)S(1)}, bf16[128,2048]{1,0:T(8,128)(2,1)}, u32[]{:S(2)}) copy-start(bf16[128,2048]{1,0:T(8,128)(2,1)} %refs_0_.2) | copy-start | bytes 1572868
  1.7 1.0 %copy-start.1 = (bf16[128,2048]{1,0:T(8,128)(2,1)S(1)}, bf16[128,2048]{1,0:T(8,128)(2,1)}, u32[]{:S(2)}) copy-start(bf16[128,2048]{1,0:T(8,128)(2,1)} %refs_1_.2) | copy-start | bytes 1572868
  3.0 9.0 %collective-permute-start = (bf16[2,128,512]{2,1,0:T(8,128)(2,1)S(1)}, bf16[2,128,512]{2,1,0:T(8,128)(2,1)S(1)}, u32[]{:S(2)}, u32[]{:S(2)}) collective-permute-start(bf16[2,128,512]{2,1,0:T(8,128)(2,1)S(1)} %get-tuple-element.25), channel_id=1, source_target_pairs={{0,8},{8,0},{16,24},{24,16},{1,9},{9,1},{17,25},{25,17},{2,10},{10... | collective-permute-start | bytes 786440 | tf_op jit(solution)/shard_map/ppermute | solution.py:397
  4.5 10.2 %collective-permute-start.1 = (bf16[2,128,512]{2,1,0:T(8,128)(2,1)S(1)}, bf16[2,128,512]{2,1,0:T(8,128)(2,1)S(1)}, u32[]{:S(2)}, u32[]{:S(2)}) collective-permute-start(bf16[2,128,512]{2,1,0:T(8,128)(2,1)S(1)} %get-tuple-element.26), channel_id=1, source_target_pairs={{0,16},{8,24},{16,0},{24,8},{1,17},{9,25},{17,1},{25,9},{2,18},{10... | collective-permute-start | bytes 786440 | tf_op jit(solution)/shard_map/ppermute | solution.py:397
  6.0 1.0 %copy-start.2 = (bf16[128,2048]{1,0:T(8,128)(2,1)S(1)}, bf16[128,2048]{1,0:T(8,128)(2,1)}, u32[]{:S(2)}) copy-start(bf16[128,2048]{1,0:T(8,128)(2,1)} %refs_0_.3) | copy-start | bytes 1572868
  7.1 1.0 %copy-start.3 = (bf16[128,2048]{1,0:T(8,128)(2,1)S(1)}, bf16[128,2048]{1,0:T(8,128)(2,1)}, u32[]{:S(2)}) copy-start(bf16[128,2048]{1,0:T(8,128)(2,1)} %refs_1_.3) | copy-start | bytes 1572868
  8.4 9.3 %collective-permute-start.3 = (bf16[2,128,512]{2,1,0:T(8,128)(2,1)S(1)}, bf16[2,128,512]{2,1,0:T(8,128)(2,1)S(1)}, u32[]{:S(2)}, u32[]{:S(2)}) collective-permute-start(bf16[2,128,512]{2,1,0:T(8,128)(2,1)S(1)} %get-tuple-element.29), channel_id=1, source_target_pairs={{0,8},{8,0},{16,24},{24,16},{1,9},{9,1},{17,25},{25,17},{2,10},{10... | collective-permute-start | bytes 786440 | tf_op jit(solution)/shard_map/ppermute | solution.py:397
  9.0 15.5 %collective-permute-start.2 = (bf16[2,128,512]{2,1,0:T(8,128)(2,1)S(1)}, bf16[2,128,512]{2,1,0:T(8,128)(2,1)S(1)}, u32[]{:S(2)}, u32[]{:S(2)}) collective-permute-start(bf16[2,128,512]{2,1,0:T(8,128)(2,1)S(1)} %get-tuple-element.27), channel_id=1, source_target_pairs={{0,24},{8,16},{16,8},{24,0},{1,25},{9,17},{17,9},{25,1},{2,26},{10... | collective-permute-start | bytes 786440 | tf_op jit(solution)/shard_map/ppermute | solution.py:397
  10.4 18.7 %collective-permute-start.4 = (bf16[2,128,512]{2,1,0:T(8,128)(2,1)S(1)}, bf16[2,128,512]{2,1,0:T(8,128)(2,1)S(1)}, u32[]{:S(2)}, u32[]{:S(2)}) collective-permute-start(bf16[2,128,512]{2,1,0:T(8,128)(2,1)S(1)} %get-tuple-element.30), channel_id=1, source_target_pairs={{0,16},{8,24},{16,0},{24,8},{1,17},{9,25},{17,1},{25,9},{2,18},{10... | collective-permute-start | bytes 786440 | tf_op jit(solution)/shard_map/ppermute | solution.py:397
  11.9 17.2 %collective-permute-start.5 = (bf16[2,128,512]{2,1,0:T(8,128)(2,1)S(1)}, bf16[2,128,512]{2,1,0:T(8,128)(2,1)S(1)}, u32[]{:S(2)}, u32[]{:S(2)}) collective-permute-start(bf16[2,128,512]{2,1,0:T(8,128)(2,1)S(1)} %get-tuple-element.31), channel_id=1, source_target_pairs={{0,24},{8,16},{16,8},{24,0},{1,25},{9,17},{17,9},{25,1},{2,26},{10... | collective-permute-start | bytes 786440 | tf_op jit(solution)/shard_map/ppermute | solution.py:397
  14.8 17.4 %collective-permute-start.6 = (bf16[3,2,128,512]{3,2,1,0:T(8,128)(2,1)S(1)}, bf16[3,2,128,512]{3,2,1,0:T(8,128)(2,1)S(1)}, u32[]{:S(2)}, u32[]{:S(2)}) collective-permute-start(bf16[3,2,128,512]{3,2,1,0:T(8,128)(2,1)S(1)} %stack.20), channel_id=1, source_target_pairs={{1,2},{3,4},{5,6},{2,1},{4,3},{6,5},{9,10},{11,12},{13,14},{10,9},... | collective-permute-start | bytes 2359304 | tf_op jit(solution)/shard_map/ppermute | solution.py:391
  17.7 14.5 %collective-permute-start.8 = (bf16[3,2,128,512]{3,2,1,0:T(8,128)(2,1)S(1)}, bf16[3,2,128,512]{3,2,1,0:T(8,128)(2,1)S(1)}, u32[]{:S(2)}, u32[]{:S(2)}) collective-permute-start(bf16[3,2,128,512]{3,2,1,0:T(8,128)(2,1)S(1)} %stack.20), channel_id=1, source_target_pairs={{0,1},{2,3},{4,5},{6,7},{1,0},{3,2},{5,4},{7,6},{8,9},{10,11},{12,... | collective-permute-start | bytes 2359304 | tf_op jit(solution)/shard_map/ppermute | solution.py:391
  24.5 7.7 %collective-permute-start.7 = (bf16[1,2,128,512]{3,2,1,0:T(8,128)(2,1)S(1)}, bf16[1,2,128,512]{3,2,1,0:T(8,128)(2,1)S(1)}, u32[]{:S(2)}, u32[]{:S(2)}) collective-permute-start(bf16[1,2,128,512]{3,2,1,0:T(8,128)(2,1)S(1)} %bitcast.3), channel_id=1, source_target_pairs={{1,2},{3,4},{5,6},{2,1},{4,3},{6,5},{9,10},{11,12},{13,14},{10,9},... | collective-permute-start | bytes 786440 | tf_op jit(solution)/shard_map/ppermute | solution.py:391
  29.1 3.1 %collective-permute-start.9 = (bf16[1,2,128,512]{3,2,1,0:T(8,128)(2,1)S(1)}, bf16[1,2,128,512]{3,2,1,0:T(8,128)(2,1)S(1)}, u32[]{:S(2)}, u32[]{:S(2)}) collective-permute-start(bf16[1,2,128,512]{3,2,1,0:T(8,128)(2,1)S(1)} %bitcast.4), channel_id=1, source_target_pairs={{0,1},{2,3},{4,5},{6,7},{1,0},{3,2},{5,4},{7,6},{8,9},{10,11},{12,... | collective-permute-start | bytes 786440 | tf_op jit(solution)/shard_map/ppermute | solution.py:391
  29.3 21.2 %collective-permute-start.13 = (bf16[4,2,128,512]{3,2,1,0:T(8,128)(2,1)S(1)}, bf16[4,2,128,512]{3,2,1,0:T(8,128)(2,1)S(1)}, u32[]{:S(2)}, u32[]{:S(2)}) collective-permute-start(bf16[4,2,128,512]{3,2,1,0:T(8,128)(2,1)S(1)} %stack.19.refs_7_), channel_id=1, source_target_pairs={{1,2},{3,4},{5,6},{2,1},{4,3},{6,5},{9,10},{11,12},{13,14},{10,9},... | collective-permute-start | bytes 3145736 | tf_op jit(solution)/shard_map/ppermute | solution.py:391
  43.2 7.3 %collective-permute-start.15 = (bf16[2,512,512]{2,1,0:T(8,128)(2,1)S(1)}, bf16[2,512,512]{2,1,0:T(8,128)(2,1)S(1)}, u32[]{:S(2)}, u32[]{:S(2)}) collective-permute-start(bf16[2,512,512]{2,1,0:T(8,128)(2,1)S(1)} %get-tuple-element.38), channel_id=1, source_target_pairs={{0,1},{2,3},{4,5},{6,7},{1,0},{3,2},{5,4},{7,6},{8,9},{10,11},{12,... | collective-permute-start | bytes 3145736 | tf_op jit(solution)/shard_map/ppermute | solution.py:391
  43.9 5.0 %collective-permute-start.14 = (f32[4,2,512]{2,1,0:T(2,128)S(1)}, f32[4,2,512]{2,1,0:T(2,128)S(1)}, u32[]{:S(2)}, u32[]{:S(2)}) collective-permute-start(f32[4,2,512]{2,1,0:T(2,128)S(1)} %get-tuple-element.36), channel_id=1, source_target_pairs={{1,2},{3,4},{5,6},{2,1},{4,3},{6,5},{9,10},{11,12},{13,14},{10,9},... | collective-permute-start | bytes 49160 | tf_op jit(solution)/shard_map/ppermute | solution.py:391
  45.9 10.0 %collective-permute-start.10 = (bf16[128,512]{1,0:T(8,128)(2,1)S(1)}, bf16[128,512]{1,0:T(8,128)(2,1)S(1)}, u32[]{:S(2)}, u32[]{:S(2)}) collective-permute-start(bf16[128,512]{1,0:T(8,128)(2,1)S(1)} %get-tuple-element.33), channel_id=1, source_target_pairs={{0,8},{8,0},{16,24},{24,16},{1,9},{9,1},{17,25},{25,17},{2,10},{10... | collective-permute-start | bytes 393224 | tf_op jit(solution)/shard_map/ppermute | solution.py:397
  47.2 10.2 %collective-permute-start.11 = (bf16[128,512]{1,0:T(8,128)(2,1)S(1)}, bf16[128,512]{1,0:T(8,128)(2,1)S(1)}, u32[]{:S(2)}, u32[]{:S(2)}) collective-permute-start(bf16[128,512]{1,0:T(8,128)(2,1)S(1)} %get-tuple-element.34), channel_id=1, source_target_pairs={{0,16},{8,24},{16,0},{24,8},{1,17},{9,25},{17,1},{25,9},{2,18},{10... | collective-permute-start | bytes 393224 | tf_op jit(solution)/shard_map/ppermute | solution.py:397
  49.0 8.5 %collective-permute-start.12 = (bf16[128,512]{1,0:T(8,128)(2,1)S(1)}, bf16[128,512]{1,0:T(8,128)(2,1)S(1)}, u32[]{:S(2)}, u32[]{:S(2)}) collective-permute-start(bf16[128,512]{1,0:T(8,128)(2,1)S(1)} %get-tuple-element.35), channel_id=1, source_target_pairs={{0,24},{8,16},{16,8},{24,0},{1,25},{9,17},{17,9},{25,1},{2,26},{10... | collective-permute-start | bytes 393224 | tf_op jit(solution)/shard_map/ppermute | solution.py:397
  53.9 9.3 %collective-permute-start.16 = (bf16[2,128,512]{2,1,0:T(8,128)(2,1)S(1)}, bf16[2,128,512]{2,1,0:T(8,128)(2,1)S(1)}, u32[]{:S(2)}, u32[]{:S(2)}) collective-permute-start(bf16[2,128,512]{2,1,0:T(8,128)(2,1)S(1)} %get-tuple-element.40), channel_id=1, source_target_pairs={{0,8},{8,0},{16,24},{24,16},{1,9},{9,1},{17,25},{25,17},{2,10},{10... | collective-permute-start | bytes 786440 | tf_op jit(solution)/shard_map/ppermute | solution.py:397
  55.4 13.4 %collective-permute-start.17 = (bf16[2,128,512]{2,1,0:T(8,128)(2,1)S(1)}, bf16[2,128,512]{2,1,0:T(8,128)(2,1)S(1)}, u32[]{:S(2)}, u32[]{:S(2)}) collective-permute-start(bf16[2,128,512]{2,1,0:T(8,128)(2,1)S(1)} %get-tuple-element.41), channel_id=1, source_target_pairs={{0,16},{8,24},{16,0},{24,8},{1,17},{9,25},{17,1},{25,9},{2,18},{10... | collective-permute-start | bytes 786440 | tf_op jit(solution)/shard_map/ppermute | solution.py:397
  55.9 12.9 %collective-permute-start.18 = (bf16[2,128,512]{2,1,0:T(8,128)(2,1)S(1)}, bf16[2,128,512]{2,1,0:T(8,128)(2,1)S(1)}, u32[]{:S(2)}, u32[]{:S(2)}) collective-permute-start(bf16[2,128,512]{2,1,0:T(8,128)(2,1)S(1)} %get-tuple-element.42), channel_id=1, source_target_pairs={{0,24},{8,16},{16,8},{24,0},{1,25},{9,17},{17,9},{25,1},{2,26},{10... | collective-permute-start | bytes 786440 | tf_op jit(solution)/shard_map/ppermute | solution.py:397

commit v6 on v5

--- a/solution.py
+++ b/solution.py
@@ -17,6 +17,8 @@
 NEG = -1e30
 HINT = 30_000_000_000
 STRIP = 64
+UNIT = 128
+UNITS = SPAN // UNIT
 SCALE = HEAD_DIM ** -0.5
 RATE = SCALE * math.log2(math.e)
 VMEM_BYTES = 24 * 1024 * 1024
@@ -139,7 +141,7 @@
     far_refs, near_refs, refs = refs[:groups], refs[groups:2 * groups], refs[2 * groups:]
     dq_refs, refs = refs[:n], refs[n:]
     stat_ref, part_ref, give_ref, k_ext, v_ext, k_flip, q_all, g_all, dq_all = refs[:9]
-    s_buf, p_buf, w_buf, d_buf = refs[9:13]
+    s_buf, p_buf, w_buf, d_buf, n_buf = refs[9:14]
     r, width = kv_refs[0].shape[1:]
     rows = n * r
     tiles = rows // TILE
@@ -160,7 +162,7 @@
             g_all[rows_at(at, r)] = qd_ref[k, 1, :, lanes]
         k_flip[...] = k_ext[...].T
         if tiles > 1:
-            refs[13][...] = jnp.zeros_like(refs[13])
+            refs[14][...] = jnp.zeros_like(refs[14])
 
         def each_tile(tile):
             first = tile * TILE
@@ -168,51 +170,66 @@
             if tiles > 1:
                 has_far = jnp.logical_or(has_far, tile > 0)
 
-            def products(sub):
-                here = rows_at(first + sub * SUB, SUB)
-                query, grad = q_all[here], g_all[here]
-                top = jnp.full((8, SUB), NEG, jnp.float32)
-                for c in range(CHUNKS):
-                    at = slice(c * SUB, (c + 1) * SUB)
-                    keys = rows_at(first + (sub + c) * SUB, SUB)
-                    s = dot(k_ext[keys], query, (1, 1)) * RATE
-                    keep = None
-                    if c == 0:
-                        keep = ahead >= 0
-                    if c == CHUNKS - 1:
-                        keep = ahead <= 0
-                    if sub + c < HALF // SUB:
-                        keep = has_far if keep is None else jnp.logical_and(keep, has_far)
-                    if keep is not None:
-                        s = jnp.where(keep, s, NEG)
-                    s_buf[sub, at] = s
-                    top = jnp.maximum(top, jnp.max(s.reshape(SUB // 8, 8, SUB), axis=0))
-                for c in range(CHUNKS):
-                    at = slice(c * SUB, (c + 1) * SUB)
-                    keys = rows_at(first + (sub + c) * SUB, SUB)
-                    p_buf[sub, at] = dot(v_ext[keys], grad, (1, 1))
-                return jnp.max(top, axis=0, keepdims=True)
-
-            def softmax(sub, top):
-                here = rows_at(first + sub * SUB, SUB)
-                total = jnp.zeros((8, SUB), jnp.float32)
-                delta = jnp.zeros((8, SUB), jnp.float32)
-                for i in range(0, SPAN, STRIP):
-                    at = slice(i, i + STRIP)
-                    e = jnp.exp2(s_buf[sub, at] - top)
-                    s_buf[sub, at] = e
-                    total += jnp.sum(e.reshape(STRIP // 8, 8, SUB), axis=0)
-                    delta += jnp.sum((e * p_buf[sub, at]).reshape(STRIP // 8, 8, SUB), axis=0)
+            subs = range(TILE // SUB)
+            heres = [rows_at(first + sub * SUB, SUB) for sub in subs]
+            query = [q_all[here] for here in heres]
+            grad = [g_all[here] for here in heres]
+            tops = [[] for _ in subs]
+            totals = [[] for _ in subs]
+            deltas = [[] for _ in subs]
+            ready = {}
+
+            def folded(x, op):
+                return op(x.reshape(x.shape[0] // 8, 8, SUB), axis=0)
+
+            def score(sub, u):
+                keys = rows_at(first + sub * SUB + u * UNIT, UNIT)
+                s = dot(k_ext[keys], query[sub], (1, 1)) * RATE
+                keep = None
+                c = u * UNIT // SUB
+                inside = slice(u * UNIT % SUB, u * UNIT % SUB + UNIT)
+                if c == 0:
+                    keep = ahead[inside] >= 0
+                if c == CHUNKS - 1:
+                    keep = ahead[inside] <= 0
+                if sub + c < HALF // SUB:
+                    keep = has_far if keep is None else jnp.logical_and(keep, has_far)
+                if keep is not None:
+                    s = jnp.where(keep, s, NEG)
+                top = jnp.max(folded(s, jnp.max), axis=0, keepdims=True)
+                e = jnp.exp2(s - top)
+                s_buf[sub, u * UNIT:(u + 1) * UNIT] = e
+                tops[sub].append(top)
+                totals[sub].append(folded(e, jnp.sum))
+
+            def product(sub, u):
+                keys = rows_at(first + sub * SUB + u * UNIT, UNIT)
+                at = slice(u * UNIT, (u + 1) * UNIT)
+                dp = dot(v_ext[keys], grad[sub], (1, 1))
+                p_buf[sub, at] = dp
+                deltas[sub].append(folded(s_buf[sub, at] * dp, jnp.sum))
+
+            def settle(sub):
+                top = tops[sub][0]
+                for other in tops[sub][1:]:
+                    top = jnp.maximum(top, other)
+                parts = [jnp.exp2(other - top) for other in tops[sub]]
+                total = sum(p * t for p, t in zip(parts, totals[sub]))
                 total = jnp.sum(total, axis=0, keepdims=True)
                 inverse = 1.0 / total
+                delta = sum(p * d for p, d in zip(parts, deltas[sub]))
                 delta = jnp.sum(delta, axis=0, keepdims=True) * inverse
-                stat_ref[h, 0:1, here] = top + jnp.log2(total)
-                stat_ref[h, 1:2, here] = delta
+                stat_ref[h, 0:1, heres[sub]] = top + jnp.log2(total)
+                stat_ref[h, 1:2, heres[sub]] = delta
+                ready[sub] = [p * inverse for p in parts], delta
+
+            def weigh(sub, u):
                 mine = slice(sub * SUB, (sub + 1) * SUB)
-                for i in range(0, SPAN, STRIP):
+                parts, delta = ready[sub]
+                for i in range(u * UNIT, (u + 1) * UNIT, STRIP):
                     at = slice(i, i + STRIP)
                     to = slice(sub * SUB + i, sub * SUB + i + STRIP)
-                    w = s_buf[sub, at] * inverse
+                    w = s_buf[sub, at] * parts[u]
                     w_buf[to, mine] = w.astype(jnp.bfloat16)
                     d_buf[to, mine] = (w * (p_buf[sub, at] - delta)).astype(jnp.bfloat16)
 
@@ -221,37 +238,45 @@
                 span = slice(sub * SUB, sub * SUB + SPAN)
                 flip = k_flip[:, rows_at(first + sub * SUB, SPAN) if tiles > 1 else span]
                 dq = dot(flip, d_buf[span, mine], (1, 0))
-                here = rows_at(first + sub * SUB, SUB)
-                dq_all[here] = (dq * SCALE).T.astype(jnp.bfloat16)
-
-            tops = [products(sub) for sub in range(TILE // SUB)]
-            for sub in range(TILE // SUB):
-                softmax(sub, tops[sub])
+                dq_all[heres[sub]] = (dq * SCALE).T.astype(jnp.bfloat16)
+
+            def key_grads(sub):
+                mine = slice(sub * SUB, (sub + 1) * SUB)
+                for which, buf, right in ((0, d_buf, query[sub]), (1, w_buf, grad[sub])):
+                    if tiles > 1:
+                        spot = rows_at(first + sub * SUB, SPAN)
+                        refs[14][which, spot] += dot(
+                            buf[sub * SUB:sub * SUB + SPAN, mine], right, (1, 0)
+                        )
+                        continue
+                    own = dot(buf[HALF:HALF + TILE, mine], right, (1, 0))
+                    near = dot(buf[HALF + TILE:SPAN + sub * SUB, mine], right, (1, 0))
+                    if sub == 0:
+                        part_ref[which, :, lanes] = own
+                        n_buf[which] = near
+                    else:
+                        part_ref[which, :, lanes] += own
+                        near0 = n_buf[which] + near[:SUB]
+                        give_ref[which, :SUB, lanes] = near0.astype(jnp.bfloat16)
+                        give_ref[which, SUB:, lanes] = near[SUB:].astype(jnp.bfloat16)
+
+            every = range(UNITS)
+            for sub in subs:
+                for u in every:
+                    score(sub, u)
+                    product(sub, u)
+            for sub in subs:
+                settle(sub)
+                for u in every:
+                    weigh(sub, u)
+            for sub in subs:
                 query_grad(sub)
-            queries, grads = q_all[rows_at(first, TILE)], g_all[rows_at(first, TILE)]
-            for which, buf, right in ((0, d_buf, queries), (1, w_buf, grads)):
-                if tiles > 1:
-                    acc = refs[13]
-                    acc[which, rows_at(first, SUB)] += dot(buf[:SUB, :SUB], right[:SUB], (1, 0))
-                    acc[which, rows_at(first + SUB, SPAN - SUB)] += dot(
-                        buf[SUB:SPAN], right, (1, 0)
-                    )
-                    acc[which, rows_at(first + SPAN, SUB)] += dot(
-                        buf[SPAN:, SUB:], right[SUB:], (1, 0)
-                    )
-                else:
-                    part_ref[which, :, lanes] = dot(buf[HALF:HALF + TILE], right, (1, 0))
-                    give_ref[which, :SUB, lanes] = dot(
-                        buf[HALF + TILE:SPAN], right, (1, 0)
-                    ).astype(jnp.bfloat16)
-                    give_ref[which, SUB:, lanes] = dot(
-                        buf[SPAN:, SUB:], right[SUB:], (1, 0)
-                    ).astype(jnp.bfloat16)
+                key_grads(sub)
 
         if tiles > 1:
             pl.loop(0, tiles)(each_tile)
-            part_ref[:, :, lanes] = refs[13][:, HALF:HALF + rows]
-            give_ref[:, :, lanes] = refs[13][:, HALF + rows:].astype(jnp.bfloat16)
+            part_ref[:, :, lanes] = refs[14][:, HALF:HALF + rows]
+            give_ref[:, :, lanes] = refs[14][:, HALF + rows:].astype(jnp.bfloat16)
         else:
             each_tile(0)
         for k in range(n):
@@ -279,6 +304,7 @@
         pltpu.VMEM((TILE // SUB, SPAN, SUB), jnp.float32),
         pltpu.VMEM((TILE + 2 * HALF, TILE), jnp.bfloat16),
         pltpu.VMEM((TILE + 2 * HALF, TILE), jnp.bfloat16),
+        pltpu.VMEM((2, SUB, HEAD_DIM), jnp.float32),
     ]
     if rows != TILE:
         scratch.append(pltpu.VMEM((2, ext, HEAD_DIM), jnp.float32))
@@ -332,7 +358,7 @@
             here = slice(b * SUB, (b + 1) * SUB)
             there = slice((steps - 1 - b) * SUB, (steps - b) * SUB)
             query, grad = q_all[here], g_all[here]
-            log_total = stat_ref[h, 0:1, there]
+            log_total = jnp.where(turn_ref[1] > 0, stat_ref[h, 0:1, there], -NEG)
             delta = stat_ref[h, 1:2, there]
             for a in range(b + 1):
                 at = slice(a * SUB, (a + 1) * SUB)
@@ -385,10 +411,17 @@
     )(place, halo, turn, *kv, far, stat, part, got)
 
 
-def swapped(array, first):
-    count = lax.axis_size("blk")
-    pairs = [(i, i + 1) for i in range(first, count - 1, 2)]
-    return lax.ppermute(array, "blk", pairs + [(j, i) for i, j in pairs])
+def swapped(array, first, idle=False):
+    count, n = lax.axis_size("blk"), lax.axis_size("head")
+    pairs = []
+    for h in range(n):
+        for b in range(count):
+            other = b + 1 if b % 2 == first else b - 1
+            if 0 <= other < count:
+                pairs.append((h * count + b, h * count + other))
+            elif idle:
+                pairs.append((h * count + b, (h ^ 1) * count + b))
+    return lax.ppermute(array, ("head", "blk"), pairs)
 
 
 def exchanged(pieces):
@@ -418,20 +451,20 @@
     qd = exchanged(packed(n, query, grad_out))
     if n == blocks:
         groups = [stacked(kv[:-1]), kv[-1][None]]
-        kv_far = [swapped(group, 1) for group in groups]
+        kv_far = [swapped(groups[0], 1), swapped(groups[1], 1, True)]
         kv_near = [swapped(group, 0) for group in groups]
         qd = stacked(qd, HINT)
-        qd_far = swapped(qd, 1)
+        qd_far = swapped(qd, 1, True)
         key_halo = place
     else:
         local, qd = jnp.stack(kv), jnp.stack(qd)
         local = jnp.take(local, place, axis=0)
         kv_far = [swapped(local[:blocks], 1)]
         kv_near = [swapped(local[n - blocks:], 0)]
-        qd_far = swapped(jnp.take(qd, place[:blocks], axis=0), 1)
+        qd_far = swapped(jnp.take(qd, place[:blocks], axis=0), 1, True)
         key_halo = halo
     dq, stat, part, give = query_part(place, halo, turn, kv, qd, kv_far, kv_near)
-    stat_far = swapped(stat[:, :, :HALF], 1)
+    stat_far = swapped(stat[:, :, :HALF], 1, True)
     got = swapped(give, 0)
     dkv = key_part(place, key_halo, turn, kv, qd_far, stat_far, part, got)
     return *merged(exchanged(dq), HINT), *merged(exchanged(dkv))

time: 70.2 us -> 66.9 us (0.953)
  the two profiles are of different devices: /device:TPU:8 before, /device:TPU:0 now
where the time goes in v6:
time: 66.9 us; the launch traced here: 66.6 us
  starting transfers between devices  24.8 us (37%)
  waiting for transfers between devices  21.6 us (32%)
  Pallas kernels  15.3 us (23%)
  local copies, waits for them, and re-layouts  4.16 us (6%)
  between operations  0.72 us (1%)
    ppermute x12, waiting for transfers between devices, exchanged(): lax.ppermute(pieces[k], 'head', [(i, i ^ k) for i in range(n)])  21 us
    ppermute x12, starting transfers between devices, exchanged(): lax.ppermute(pieces[k], 'head', [(i, i ^ k) for i in range(n)])  19 us
    pallas_call x1, Pallas kernels, query_part(): pl.pallas_call(lambda *refs: query_kernel(n, len(far), *refs), in_specs=[...  9.41 us
    ppermute x7, starting transfers between devices, swapped(): return lax.ppermute(array, ('head', 'blk'), pairs)  5.79 us
    unnamed x8, local copies, waits for them, and re-layouts  4.16 us
    pallas_call x1, Pallas kernels, key_part(): pl.pallas_call(lambda *refs: key_kernel(n, *refs), in_specs=[scalars] * 3...  3.39 us
    pallas_call x2, Pallas kernels, merged(): pl.pallas_call(lambda *refs: merge_kernel(n, *refs), in_specs=[pl.BlockSp...  1.84 us
  transfers between devices with their start and end apart: 19, of which 7 were waited for; matrix products, arithmetic and copies ran while one was open for 0% of the time, Pallas kernels for 21%

profile of v6, /device:TPU:0, one launch (start us, length us, event | category | flops | bytes accessed | tf_op | source)
XLA Modules:
  0.0 66.6 jit_solution(11311017021188563144)
XLA Ops:
  0.6 0.0 copy-start
  0.6 1.0 %copy-done = bf16[128,2048]{1,0:T(8,128)(2,1)S(1)} copy-done((bf16[128,2048]{1,0:T(8,128)(2,1)S(1)}, bf16[128,2048]{1,0:T(8,128)(2,1)}, u32[]{:S(2)}) %copy-start) | copy-done | bytes 524312
  1.7 0.0 copy-start.1
  1.7 1.0 %copy-done.1 = bf16[128,2048]{1,0:T(8,128)(2,1)S(1)} copy-done((bf16[128,2048]{1,0:T(8,128)(2,1)S(1)}, bf16[128,2048]{1,0:T(8,128)(2,1)}, u32[]{:S(2)}) %copy-start.1) | copy-done | bytes 524312
  2.7 0.2 pack.2
  3.0 3.0 %collective-permute-start = (bf16[2,128,512]{2,1,0:T(8,128)(2,1)S(1)}, bf16[2,128,512]{2,1,0:T(8,128)(2,1)S(1)}, u32[]{:S(2)}, u32[]{:S(2)}) collective-permute-start(bf16[2,128,512]{2,1,0:T(8,128)(2,1)S(1)} %get-tuple-element.25), channel_id=1, source_target_pairs={{0,8},{8,0},{16,24},{24,16},{1,9},{9,1},{17,25},{25,17},{2,10},{10... | collective-permute-start | bytes 786440 | tf_op jit(solution)/shard_map/ppermute | solution.py:430
  6.0 1.5 %collective-permute-start.1 = (bf16[2,128,512]{2,1,0:T(8,128)(2,1)S(1)}, bf16[2,128,512]{2,1,0:T(8,128)(2,1)S(1)}, u32[]{:S(2)}, u32[]{:S(2)}) collective-permute-start(bf16[2,128,512]{2,1,0:T(8,128)(2,1)S(1)} %get-tuple-element.26), channel_id=1, source_target_pairs={{0,16},{8,24},{16,0},{24,8},{1,17},{9,25},{17,1},{25,9},{2,18},{10... | collective-permute-start | bytes 786440 | tf_op jit(solution)/shard_map/ppermute | solution.py:430
  7.5 0.0 copy-start.2
  7.5 1.0 %copy-done.2 = bf16[128,2048]{1,0:T(8,128)(2,1)S(1)} copy-done((bf16[128,2048]{1,0:T(8,128)(2,1)S(1)}, bf16[128,2048]{1,0:T(8,128)(2,1)}, u32[]{:S(2)}) %copy-start.2) | copy-done | bytes 524312
  8.5 0.0 copy-start.3
  8.5 1.0 %copy-done.3 = bf16[128,2048]{1,0:T(8,128)(2,1)S(1)} copy-done((bf16[128,2048]{1,0:T(8,128)(2,1)S(1)}, bf16[128,2048]{1,0:T(8,128)(2,1)}, u32[]{:S(2)}) %copy-start.3) | copy-done | bytes 524312
  9.6 0.2 pack.3
  9.8 0.6 collective-permute-start.3
  10.4 1.4 %collective-permute-start.2 = (bf16[2,128,512]{2,1,0:T(8,128)(2,1)S(1)}, bf16[2,128,512]{2,1,0:T(8,128)(2,1)S(1)}, u32[]{:S(2)}, u32[]{:S(2)}) collective-permute-start(bf16[2,128,512]{2,1,0:T(8,128)(2,1)S(1)} %get-tuple-element.27), channel_id=1, source_target_pairs={{0,24},{8,16},{16,8},{24,0},{1,25},{9,17},{17,9},{25,1},{2,26},{10... | collective-permute-start | bytes 786440 | tf_op jit(solution)/shard_map/ppermute | solution.py:430
  11.8 1.5 %collective-permute-start.4 = (bf16[2,128,512]{2,1,0:T(8,128)(2,1)S(1)}, bf16[2,128,512]{2,1,0:T(8,128)(2,1)S(1)}, u32[]{:S(2)}, u32[]{:S(2)}) collective-permute-start(bf16[2,128,512]{2,1,0:T(8,128)(2,1)S(1)} %get-tuple-element.30), channel_id=1, source_target_pairs={{0,16},{8,24},{16,0},{24,8},{1,17},{9,25},{17,1},{25,9},{2,18},{10... | collective-permute-start | bytes 786440 | tf_op jit(solution)/shard_map/ppermute | solution.py:430
  13.4 0.0 collective-permute-done.refs_1_.refs_4_
  13.4 2.7 %collective-permute-start.5 = (bf16[2,128,512]{2,1,0:T(8,128)(2,1)S(1)}, bf16[2,128,512]{2,1,0:T(8,128)(2,1)S(1)}, u32[]{:S(2)}, u32[]{:S(2)}) collective-permute-start(bf16[2,128,512]{2,1,0:T(8,128)(2,1)S(1)} %get-tuple-element.31), channel_id=1, source_target_pairs={{0,24},{8,16},{16,8},{24,0},{1,25},{9,17},{17,9},{25,1},{2,26},{10... | collective-permute-start | bytes 786440 | tf_op jit(solution)/shard_map/ppermute | solution.py:430
  16.1 0.1 pad_add_fusion.refs_2_
  16.2 0.0 collective-permute-done.1.refs_2_.refs_5_
  16.2 0.1 stack.20
  16.3 0.7 %collective-permute-start.6 = (bf16[3,2,128,512]{3,2,1,0:T(8,128)(2,1)S(1)}, bf16[3,2,128,512]{3,2,1,0:T(8,128)(2,1)S(1)}, u32[]{:S(2)}, u32[]{:S(2)}) collective-permute-start(bf16[3,2,128,512]{3,2,1,0:T(8,128)(2,1)S(1)} %stack.20), channel_id=1, source_target_pairs={{1,2},{2,1},{3,4},{4,3},{5,6},{6,5},{9,10},{10,9},{11,12},{12,11},... | collective-permute-start | bytes 2359304 | tf_op jit(solution)/shard_map/ppermute | solution.py:424
  17.0 2.1 %collective-permute-done.3.refs_1_ = bf16[2,128,512]{2,1,0:T(8,128)(2,1)S(1)} collective-permute-done((bf16[2,128,512]{2,1,0:T(8,128)(2,1)S(1)}, bf16[2,128,512]{2,1,0:T(8,128)(2,1)S(1)}, u32[]{:S(2)}, u32[]{:S(2)}) %collective-permute-start.3) | collective-permute-done | bytes 262176 | tf_op jit(solution)/shard_map/ppermute | solution.py:430
  19.1 0.9 %collective-permute-start.8 = (bf16[3,2,128,512]{3,2,1,0:T(8,128)(2,1)S(1)}, bf16[3,2,128,512]{3,2,1,0:T(8,128)(2,1)S(1)}, u32[]{:S(2)}, u32[]{:S(2)}) collective-permute-start(bf16[3,2,128,512]{3,2,1,0:T(8,128)(2,1)S(1)} %stack.20), channel_id=1, source_target_pairs={{0,1},{1,0},{2,3},{3,2},{4,5},{5,4},{6,7},{7,6},{8,9},{9,8},{10,11... | collective-permute-start | bytes 2359304 | tf_op jit(solution)/shard_map/ppermute | solution.py:424
  20.0 6.0 %collective-permute-done.2.refs_6_ = bf16[2,128,512]{2,1,0:T(8,128)(2,1)S(1)} collective-permute-done((bf16[2,128,512]{2,1,0:T(8,128)(2,1)S(1)}, bf16[2,128,512]{2,1,0:T(8,128)(2,1)S(1)}, u32[]{:S(2)}, u32[]{:S(2)}) %collective-permute-start.2) | collective-permute-done | bytes 262176 | tf_op jit(solution)/shard_map/ppermute | solution.py:430
  26.0 1.4 %collective-permute-start.7 = (bf16[1,2,128,512]{3,2,1,0:T(8,128)(2,1)S(1)}, bf16[1,2,128,512]{3,2,1,0:T(8,128)(2,1)S(1)}, u32[]{:S(2)}, u32[]{:S(2)}) collective-permute-start(bf16[1,2,128,512]{3,2,1,0:T(8,128)(2,1)S(1)} %bitcast.3), channel_id=1, source_target_pairs={{0,8},{1,2},{2,1},{3,4},{4,3},{5,6},{6,5},{7,15},{8,0},{9,10},{10,... | collective-permute-start | bytes 786440 | tf_op jit(solution)/shard_map/ppermute | solution.py:424
  27.3 3.2 %collective-permute-done.4.refs_2_ = bf16[2,128,512]{2,1,0:T(8,128)(2,1)S(1)} collective-permute-done((bf16[2,128,512]{2,1,0:T(8,128)(2,1)S(1)}, bf16[2,128,512]{2,1,0:T(8,128)(2,1)S(1)}, u32[]{:S(2)}, u32[]{:S(2)}) %collective-permute-start.4) | collective-permute-done | bytes 262176 | tf_op jit(solution)/shard_map/ppermute | solution.py:430
  30.6 0.0 collective-permute-start.9
  30.6 0.0 collective-permute-done.5.refs_3_
  30.6 0.1 stack.19.refs_7_
  30.7 1.3 %collective-permute-start.13 = (bf16[4,2,128,512]{3,2,1,0:T(8,128)(2,1)S(1)}, bf16[4,2,128,512]{3,2,1,0:T(8,128)(2,1)S(1)}, u32[]{:S(2)}, u32[]{:S(2)}) collective-permute-start(bf16[4,2,128,512]{3,2,1,0:T(8,128)(2,1)S(1)} %stack.19.refs_7_), channel_id=1, source_target_pairs={{0,8},{1,2},{2,1},{3,4},{4,3},{5,6},{6,5},{7,15},{8,0},{9,10},{10,... | collective-permute-start | bytes 3145736 | tf_op jit(solution)/shard_map/ppermute | solution.py:424
  32.0 0.3 collective-permute-done.7.refs_9_
  32.3 0.0 collective-permute-done.9.refs_11_
  32.3 0.0 collective-permute-done.6.refs_8_
  32.3 0.0 collective-permute-done.8.refs_10_
  32.3 9.4 %query_part.1 = (bf16[128,512]{1,0:T(8,128)(2,1)S(1)}, bf16[128,512]{1,0:T(8,128)(2,1)S(1)}, bf16[128,512]{1,0:T(8,128)(2,1)S(1)}, bf16[128,512]{1,0:T(8,128)(2,...) custom-call(s32[4]{0:T(128)S(1)} %xor_xor_fusion.refs_0_.refs_1_, ...), custom_call_target="tpu_custom_call" | custom-call | flops 3355443200 | bytes 3145728 | tf_op jit(solution)/shard_map/query_part/pallas_call | solution.py:311
  41.8 0.2 collective-permute-start.15
  42.0 1.3 %collective-permute-start.14 = (f32[4,2,512]{2,1,0:T(2,128)S(1)}, f32[4,2,512]{2,1,0:T(2,128)S(1)}, u32[]{:S(2)}, u32[]{:S(2)}) collective-permute-start(f32[4,2,512]{2,1,0:T(2,128)S(1)} %get-tuple-element.36), channel_id=1, source_target_pairs={{0,8},{1,2},{2,1},{3,4},{4,3},{5,6},{6,5},{7,15},{8,0},{9,10},{10,... | collective-permute-start | bytes 49160 | tf_op jit(solution)/shard_map/ppermute | solution.py:424
  43.3 0.7 %collective-permute-start.10 = (bf16[128,512]{1,0:T(8,128)(2,1)S(1)}, bf16[128,512]{1,0:T(8,128)(2,1)S(1)}, u32[]{:S(2)}, u32[]{:S(2)}) collective-permute-start(bf16[128,512]{1,0:T(8,128)(2,1)S(1)} %get-tuple-element.33), channel_id=1, source_target_pairs={{0,8},{8,0},{16,24},{24,16},{1,9},{9,1},{17,25},{25,17},{2,10},{10... | collective-permute-start | bytes 393224 | tf_op jit(solution)/shard_map/ppermute | solution.py:430
  44.0 1.5 %collective-permute-start.11 = (bf16[128,512]{1,0:T(8,128)(2,1)S(1)}, bf16[128,512]{1,0:T(8,128)(2,1)S(1)}, u32[]{:S(2)}, u32[]{:S(2)}) collective-permute-start(bf16[128,512]{1,0:T(8,128)(2,1)S(1)} %get-tuple-element.34), channel_id=1, source_target_pairs={{0,16},{8,24},{16,0},{24,8},{1,17},{9,25},{17,1},{25,9},{2,18},{10... | collective-permute-start | bytes 393224 | tf_op jit(solution)/shard_map/ppermute | solution.py:430
  45.5 0.2 collective-permute-done.14.refs_8_
  45.8 2.4 %collective-permute-start.12 = (bf16[128,512]{1,0:T(8,128)(2,1)S(1)}, bf16[128,512]{1,0:T(8,128)(2,1)S(1)}, u32[]{:S(2)}, u32[]{:S(2)}) collective-permute-start(bf16[128,512]{1,0:T(8,128)(2,1)S(1)} %get-tuple-element.35), channel_id=1, source_target_pairs={{0,24},{8,16},{16,8},{24,0},{1,25},{9,17},{17,9},{25,1},{2,26},{10... | collective-permute-start | bytes 393224 | tf_op jit(solution)/shard_map/ppermute | solution.py:430
  48.1 0.0 collective-permute-done.13.refs_7_
  48.1 0.0 collective-permute-done.15.refs_10_
  48.1 3.4 %key_part.1 = (bf16[2,128,512]{2,1,0:T(8,128)(2,1)S(1)}, bf16[2,128,512]{2,1,0:T(8,128)(2,1)S(1)}, bf16[2,128,512]{2,1,0:T(8,128)(2,1)S(1)}, bf16[2,128,512]{2,1,0:T(8,128)(2,1)S(1)}) custom-call(s32[4]{0:T(128)S(1)} %xor_xor_fusion.refs_0_.refs_1_, s32[4]{0:T(128)S(1)} %xor_xor_fusion.refs_0_.refs_1_, s32[2]{0:T(128)S(1)} %pad_add_fusion.refs_2_, ...), custom_call_target="tpu_custom_call" | custom-call | flops 30000001024 | bytes 6291456 | tf_op jit(solution)/shard_map/key_part/pallas_call | solution.py:390
  51.5 0.7 %collective-permute-start.16 = (bf16[2,128,512]{2,1,0:T(8,128)(2,1)S(1)}, bf16[2,128,512]{2,1,0:T(8,128)(2,1)S(1)}, u32[]{:S(2)}, u32[]{:S(2)}) collective-permute-start(bf16[2,128,512]{2,1,0:T(8,128)(2,1)S(1)} %get-tuple-element.40), channel_id=1, source_target_pairs={{0,8},{8,0},{16,24},{24,16},{1,9},{9,1},{17,25},{25,17},{2,10},{10... | collective-permute-start | bytes 786440 | tf_op jit(solution)/shard_map/ppermute | solution.py:430
  52.2 0.5 collective-permute-start.17
  52.7 0.0 collective-permute-done.10.refs_1_
  52.7 2.4 %collective-permute-start.18 = (bf16[2,128,512]{2,1,0:T(8,128)(2,1)S(1)}, bf16[2,128,512]{2,1,0:T(8,128)(2,1)S(1)}, u32[]{:S(2)}, u32[]{:S(2)}) collective-permute-start(bf16[2,128,512]{2,1,0:T(8,128)(2,1)S(1)} %get-tuple-element.42), channel_id=1, source_target_pairs={{0,24},{8,16},{16,8},{24,0},{1,25},{9,17},{17,9},{25,1},{2,26},{10... | collective-permute-start | bytes 786440 | tf_op jit(solution)/shard_map/ppermute | solution.py:430
  55.1 0.0 collective-permute-done.11.refs_2_
  55.1 0.0 collective-permute-done.12.refs_3_
  55.1 0.8 %merge.2 = bf16[128,2048]{1,0:T(8,128)(2,1)} custom-call(bf16[128,512]{1,0:T(8,128)(2,1)S(1)} %get-tuple-element.32.refs_0_, bf16[128,512]{1,0:T(8,128)(2,1)S(1)} %collective-permute-done.10.refs_1_, bf16[128,512]{1,0:T(8,128)(2,1)S(1)} %collective-permute-done.11.refs_2_, bf16[128,512]{1,0:T(8,128)(2,1)S(1)} %collective-permute-done.12.refs_3_), custom_call_target="tpu_custom_call" | custom-call | flops 30000001024 | tf_op jit(solution)/shard_map/merge/pallas_call | solution.py:115
  55.9 4.9 %collective-permute-done.16.refs_1_ = bf16[2,128,512]{2,1,0:T(8,128)(2,1)S(1)} collective-permute-done((bf16[2,128,512]{2,1,0:T(8,128)(2,1)S(1)}, bf16[2,128,512]{2,1,0:T(8,128)(2,1)S(1)}, u32[]{:S(2)}, u32[]{:S(2)}) %collective-permute-start.16) | collective-permute-done | bytes 262176 | tf_op jit(solution)/shard_map/ppermute | solution.py:430
  60.8 4.8 %collective-permute-done.17.refs_2_ = bf16[2,128,512]{2,1,0:T(8,128)(2,1)S(1)} collective-permute-done((bf16[2,128,512]{2,1,0:T(8,128)(2,1)S(1)}, bf16[2,128,512]{2,1,0:T(8,128)(2,1)S(1)}, u32[]{:S(2)}, u32[]{:S(2)}) %collective-permute-start.17) | collective-permute-done | bytes 262176 | tf_op jit(solution)/shard_map/ppermute | solution.py:430
  65.6 0.0 collective-permute-done.18.refs_3_
  65.6 1.0 %merge.3 = (bf16[128,2048]{1,0:T(8,128)(2,1)}, bf16[128,2048]{1,0:T(8,128)(2,1)}) custom-call(bf16[2,128,512]{2,1,0:T(8,128)(2,1)S(1)} %get-tuple-element.39.refs_0_, bf16[2,128,512]{2,1,0:T(8,128)(2,1)S(1)} %collective-permute-done.16.refs_1_, bf16[2,128,512]{2,1,0:T(8,128)(2,1)S(1)} %collective-permute-done.17.refs_2_, ...), custom_call_target="tpu_custom_call" | custom-call | tf_op jit(solution)/shard_map/merge/pallas_call | solution.py:115
  (1 shorter events, 0.0 us)
Async XLA Ops:
  0.6 1.0 %copy-start = (bf16[128,2048]{1,0:T(8,128)(2,1)S(1)}, bf16[128,2048]{1,0:T(8,128)(2,1)}, u32[]{:S(2)}) copy-start(bf16[128,2048]{1,0:T(8,128)(2,1)} %refs_0_.2) | copy-start | bytes 1572868
  1.7 1.0 %copy-start.1 = (bf16[128,2048]{1,0:T(8,128)(2,1)S(1)}, bf16[128,2048]{1,0:T(8,128)(2,1)}, u32[]{:S(2)}) copy-start(bf16[128,2048]{1,0:T(8,128)(2,1)} %refs_1_.2) | copy-start | bytes 1572868
  3.0 10.4 %collective-permute-start = (bf16[2,128,512]{2,1,0:T(8,128)(2,1)S(1)}, bf16[2,128,512]{2,1,0:T(8,128)(2,1)S(1)}, u32[]{:S(2)}, u32[]{:S(2)}) collective-permute-start(bf16[2,128,512]{2,1,0:T(8,128)(2,1)S(1)} %get-tuple-element.25), channel_id=1, source_target_pairs={{0,8},{8,0},{16,24},{24,16},{1,9},{9,1},{17,25},{25,17},{2,10},{10... | collective-permute-start | bytes 786440 | tf_op jit(solution)/shard_map/ppermute | solution.py:430
  6.0 10.2 %collective-permute-start.1 = (bf16[2,128,512]{2,1,0:T(8,128)(2,1)S(1)}, bf16[2,128,512]{2,1,0:T(8,128)(2,1)S(1)}, u32[]{:S(2)}, u32[]{:S(2)}) collective-permute-start(bf16[2,128,512]{2,1,0:T(8,128)(2,1)S(1)} %get-tuple-element.26), channel_id=1, source_target_pairs={{0,16},{8,24},{16,0},{24,8},{1,17},{9,25},{17,1},{25,9},{2,18},{10... | collective-permute-start | bytes 786440 | tf_op jit(solution)/shard_map/ppermute | solution.py:430
  7.5 1.0 %copy-start.2 = (bf16[128,2048]{1,0:T(8,128)(2,1)S(1)}, bf16[128,2048]{1,0:T(8,128)(2,1)}, u32[]{:S(2)}) copy-start(bf16[128,2048]{1,0:T(8,128)(2,1)} %refs_0_.3) | copy-start | bytes 1572868
  8.5 1.0 %copy-start.3 = (bf16[128,2048]{1,0:T(8,128)(2,1)S(1)}, bf16[128,2048]{1,0:T(8,128)(2,1)}, u32[]{:S(2)}) copy-start(bf16[128,2048]{1,0:T(8,128)(2,1)} %refs_1_.3) | copy-start | bytes 1572868
  9.8 9.3 %collective-permute-start.3 = (bf16[2,128,512]{2,1,0:T(8,128)(2,1)S(1)}, bf16[2,128,512]{2,1,0:T(8,128)(2,1)S(1)}, u32[]{:S(2)}, u32[]{:S(2)}) collective-permute-start(bf16[2,128,512]{2,1,0:T(8,128)(2,1)S(1)} %get-tuple-element.29), channel_id=1, source_target_pairs={{0,8},{8,0},{16,24},{24,16},{1,9},{9,1},{17,25},{25,17},{2,10},{10... | collective-permute-start | bytes 786440 | tf_op jit(solution)/shard_map/ppermute | solution.py:430
  10.4 15.5 %collective-permute-start.2 = (bf16[2,128,512]{2,1,0:T(8,128)(2,1)S(1)}, bf16[2,128,512]{2,1,0:T(8,128)(2,1)S(1)}, u32[]{:S(2)}, u32[]{:S(2)}) collective-permute-start(bf16[2,128,512]{2,1,0:T(8,128)(2,1)S(1)} %get-tuple-element.27), channel_id=1, source_target_pairs={{0,24},{8,16},{16,8},{24,0},{1,25},{9,17},{17,9},{25,1},{2,26},{10... | collective-permute-start | bytes 786440 | tf_op jit(solution)/shard_map/ppermute | solution.py:430
  11.8 18.7 %collective-permute-start.4 = (bf16[2,128,512]{2,1,0:T(8,128)(2,1)S(1)}, bf16[2,128,512]{2,1,0:T(8,128)(2,1)S(1)}, u32[]{:S(2)}, u32[]{:S(2)}) collective-permute-start(bf16[2,128,512]{2,1,0:T(8,128)(2,1)S(1)} %get-tuple-element.30), channel_id=1, source_target_pairs={{0,16},{8,24},{16,0},{24,8},{1,17},{9,25},{17,1},{25,9},{2,18},{10... | collective-permute-start | bytes 786440 | tf_op jit(solution)/shard_map/ppermute | solution.py:430
  13.4 17.2 %collective-permute-start.5 = (bf16[2,128,512]{2,1,0:T(8,128)(2,1)S(1)}, bf16[2,128,512]{2,1,0:T(8,128)(2,1)S(1)}, u32[]{:S(2)}, u32[]{:S(2)}) collective-permute-start(bf16[2,128,512]{2,1,0:T(8,128)(2,1)S(1)} %get-tuple-element.31), channel_id=1, source_target_pairs={{0,24},{8,16},{16,8},{24,0},{1,25},{9,17},{17,9},{25,1},{2,26},{10... | collective-permute-start | bytes 786440 | tf_op jit(solution)/shard_map/ppermute | solution.py:430
  16.3 16.0 %collective-permute-start.6 = (bf16[3,2,128,512]{3,2,1,0:T(8,128)(2,1)S(1)}, bf16[3,2,128,512]{3,2,1,0:T(8,128)(2,1)S(1)}, u32[]{:S(2)}, u32[]{:S(2)}) collective-permute-start(bf16[3,2,128,512]{3,2,1,0:T(8,128)(2,1)S(1)} %stack.20), channel_id=1, source_target_pairs={{1,2},{2,1},{3,4},{4,3},{5,6},{6,5},{9,10},{10,9},{11,12},{12,11},... | collective-permute-start | bytes 2359304 | tf_op jit(solution)/shard_map/ppermute | solution.py:424
  19.1 13.2 %collective-permute-start.8 = (bf16[3,2,128,512]{3,2,1,0:T(8,128)(2,1)S(1)}, bf16[3,2,128,512]{3,2,1,0:T(8,128)(2,1)S(1)}, u32[]{:S(2)}, u32[]{:S(2)}) collective-permute-start(bf16[3,2,128,512]{3,2,1,0:T(8,128)(2,1)S(1)} %stack.20), channel_id=1, source_target_pairs={{0,1},{1,0},{2,3},{3,2},{4,5},{5,4},{6,7},{7,6},{8,9},{9,8},{10,11... | collective-permute-start | bytes 2359304 | tf_op jit(solution)/shard_map/ppermute | solution.py:424
  26.0 6.4 %collective-permute-start.7 = (bf16[1,2,128,512]{3,2,1,0:T(8,128)(2,1)S(1)}, bf16[1,2,128,512]{3,2,1,0:T(8,128)(2,1)S(1)}, u32[]{:S(2)}, u32[]{:S(2)}) collective-permute-start(bf16[1,2,128,512]{3,2,1,0:T(8,128)(2,1)S(1)} %bitcast.3), channel_id=1, source_target_pairs={{0,8},{1,2},{2,1},{3,4},{4,3},{5,6},{6,5},{7,15},{8,0},{9,10},{10,... | collective-permute-start | bytes 786440 | tf_op jit(solution)/shard_map/ppermute | solution.py:424
  30.6 1.8 %collective-permute-start.9 = (bf16[1,2,128,512]{3,2,1,0:T(8,128)(2,1)S(1)}, bf16[1,2,128,512]{3,2,1,0:T(8,128)(2,1)S(1)}, u32[]{:S(2)}, u32[]{:S(2)}) collective-permute-start(bf16[1,2,128,512]{3,2,1,0:T(8,128)(2,1)S(1)} %bitcast.4), channel_id=1, source_target_pairs={{0,1},{1,0},{2,3},{3,2},{4,5},{5,4},{6,7},{7,6},{8,9},{9,8},{10,11... | collective-permute-start | bytes 786440 | tf_op jit(solution)/shard_map/ppermute | solution.py:424
  30.7 17.4 %collective-permute-start.13 = (bf16[4,2,128,512]{3,2,1,0:T(8,128)(2,1)S(1)}, bf16[4,2,128,512]{3,2,1,0:T(8,128)(2,1)S(1)}, u32[]{:S(2)}, u32[]{:S(2)}) collective-permute-start(bf16[4,2,128,512]{3,2,1,0:T(8,128)(2,1)S(1)} %stack.19.refs_7_), channel_id=1, source_target_pairs={{0,8},{1,2},{2,1},{3,4},{4,3},{5,6},{6,5},{7,15},{8,0},{9,10},{10,... | collective-permute-start | bytes 3145736 | tf_op jit(solution)/shard_map/ppermute | solution.py:424
  41.8 6.4 %collective-permute-start.15 = (bf16[2,512,512]{2,1,0:T(8,128)(2,1)S(1)}, bf16[2,512,512]{2,1,0:T(8,128)(2,1)S(1)}, u32[]{:S(2)}, u32[]{:S(2)}) collective-permute-start(bf16[2,512,512]{2,1,0:T(8,128)(2,1)S(1)} %get-tuple-element.38), channel_id=1, source_target_pairs={{0,1},{1,0},{2,3},{3,2},{4,5},{5,4},{6,7},{7,6},{8,9},{9,8},{10,11... | collective-permute-start | bytes 3145736 | tf_op jit(solution)/shard_map/ppermute | solution.py:424
  42.0 3.8 %collective-permute-start.14 = (f32[4,2,512]{2,1,0:T(2,128)S(1)}, f32[4,2,512]{2,1,0:T(2,128)S(1)}, u32[]{:S(2)}, u32[]{:S(2)}) collective-permute-start(f32[4,2,512]{2,1,0:T(2,128)S(1)} %get-tuple-element.36), channel_id=1, source_target_pairs={{0,8},{1,2},{2,1},{3,4},{4,3},{5,6},{6,5},{7,15},{8,0},{9,10},{10,... | collective-permute-start | bytes 49160 | tf_op jit(solution)/shard_map/ppermute | solution.py:424
  43.3 9.4 %collective-permute-start.10 = (bf16[128,512]{1,0:T(8,128)(2,1)S(1)}, bf16[128,512]{1,0:T(8,128)(2,1)S(1)}, u32[]{:S(2)}, u32[]{:S(2)}) collective-permute-start(bf16[128,512]{1,0:T(8,128)(2,1)S(1)} %get-tuple-element.33), channel_id=1, source_target_pairs={{0,8},{8,0},{16,24},{24,16},{1,9},{9,1},{17,25},{25,17},{2,10},{10... | collective-permute-start | bytes 393224 | tf_op jit(solution)/shard_map/ppermute | solution.py:430
  44.0 11.1 %collective-permute-start.11 = (bf16[128,512]{1,0:T(8,128)(2,1)S(1)}, bf16[128,512]{1,0:T(8,128)(2,1)S(1)}, u32[]{:S(2)}, u32[]{:S(2)}) collective-permute-start(bf16[128,512]{1,0:T(8,128)(2,1)S(1)} %get-tuple-element.34), channel_id=1, source_target_pairs={{0,16},{8,24},{16,0},{24,8},{1,17},{9,25},{17,1},{25,9},{2,18},{10... | collective-permute-start | bytes 393224 | tf_op jit(solution)/shard_map/ppermute | solution.py:430
  45.8 9.3 %collective-permute-start.12 = (bf16[128,512]{1,0:T(8,128)(2,1)S(1)}, bf16[128,512]{1,0:T(8,128)(2,1)S(1)}, u32[]{:S(2)}, u32[]{:S(2)}) collective-permute-start(bf16[128,512]{1,0:T(8,128)(2,1)S(1)} %get-tuple-element.35), channel_id=1, source_target_pairs={{0,24},{8,16},{16,8},{24,0},{1,25},{9,17},{17,9},{25,1},{2,26},{10... | collective-permute-start | bytes 393224 | tf_op jit(solution)/shard_map/ppermute | solution.py:430
  51.5 9.3 %collective-permute-start.16 = (bf16[2,128,512]{2,1,0:T(8,128)(2,1)S(1)}, bf16[2,128,512]{2,1,0:T(8,128)(2,1)S(1)}, u32[]{:S(2)}, u32[]{:S(2)}) collective-permute-start(bf16[2,128,512]{2,1,0:T(8,128)(2,1)S(1)} %get-tuple-element.40), channel_id=1, source_target_pairs={{0,8},{8,0},{16,24},{24,16},{1,9},{9,1},{17,25},{25,17},{2,10},{10... | collective-permute-start | bytes 786440 | tf_op jit(solution)/shard_map/ppermute | solution.py:430
  52.2 13.4 %collective-permute-start.17 = (bf16[2,128,512]{2,1,0:T(8,128)(2,1)S(1)}, bf16[2,128,512]{2,1,0:T(8,128)(2,1)S(1)}, u32[]{:S(2)}, u32[]{:S(2)}) collective-permute-start(bf16[2,128,512]{2,1,0:T(8,128)(2,1)S(1)} %get-tuple-element.41), channel_id=1, source_target_pairs={{0,16},{8,24},{16,0},{24,8},{1,17},{9,25},{17,1},{25,9},{2,18},{10... | collective-permute-start | bytes 786440 | tf_op jit(solution)/shard_map/ppermute | solution.py:430
  52.7 12.9 %collective-permute-start.18 = (bf16[2,128,512]{2,1,0:T(8,128)(2,1)S(1)}, bf16[2,128,512]{2,1,0:T(8,128)(2,1)S(1)}, u32[]{:S(2)}, u32[]{:S(2)}) collective-permute-start(bf16[2,128,512]{2,1,0:T(8,128)(2,1)S(1)} %get-tuple-element.42), channel_id=1, source_target_pairs={{0,24},{8,16},{16,8},{24,0},{1,25},{9,17},{17,9},{25,1},{2,26},{10... | collective-permute-start | bytes 786440 | tf_op jit(solution)/shard_map/ppermute | solution.py:430

commit v7 on v6

--- a/solution.py
+++ b/solution.py
@@ -21,7 +21,9 @@
 UNITS = SPAN // UNIT
 SCALE = HEAD_DIM ** -0.5
 RATE = SCALE * math.log2(math.e)
-VMEM_BYTES = 24 * 1024 * 1024
+VMEM_BYTES = 46 * 1024 * 1024
+QGROUP = 4
+KGROUP = 4
 SMALL_BYTES = 8 * 1024 * 1024
 
 
@@ -131,6 +133,17 @@
     ) * turn_ref[0]
 
 
+def over_heads(heads, scratch, each_head):
+    group = scratch[0].shape[0]
+
+    def each_group(i, _):
+        for member in range(group):
+            each_head(i * group + member, [ref.at[member] for ref in scratch])
+        return 0
+
+    lax.fori_loop(0, heads // group, each_group, 0)
+
+
 def members(refs):
     return [ref.at[i] for ref in refs for i in range(ref.shape[0])]
 
@@ -140,14 +153,15 @@
     qd_ref, refs = refs[0], refs[1:]
     far_refs, near_refs, refs = refs[:groups], refs[groups:2 * groups], refs[2 * groups:]
     dq_refs, refs = refs[:n], refs[n:]
-    stat_ref, part_ref, give_ref, k_ext, v_ext, k_flip, q_all, g_all, dq_all = refs[:9]
-    s_buf, p_buf, w_buf, d_buf, n_buf = refs[9:14]
+    stat_ref, part_ref, give_ref = refs[:3]
     r, width = kv_refs[0].shape[1:]
     rows = n * r
     tiles = rows // TILE
     ahead = ahead_by(turn_ref)
 
-    def each_head(h, _):
+    def each_head(h, scratch):
+        k_ext, v_ext, k_flip, q_all, g_all, dq_all = scratch[:6]
+        s_buf, p_buf, w_buf, d_buf, n_buf = scratch[6:11]
         lanes = rows_at(h * HEAD_DIM, HEAD_DIM)
         for i, (far, near) in enumerate(zip(members(far_refs), members(near_refs))):
             at = halo_ref[i] * r
@@ -162,7 +176,7 @@
             g_all[rows_at(at, r)] = qd_ref[k, 1, :, lanes]
         k_flip[...] = k_ext[...].T
         if tiles > 1:
-            refs[14][...] = jnp.zeros_like(refs[14])
+            scratch[11][...] = jnp.zeros_like(scratch[11])
 
         def each_tile(tile):
             first = tile * TILE
@@ -245,7 +259,7 @@
                 for which, buf, right in ((0, d_buf, query[sub]), (1, w_buf, grad[sub])):
                     if tiles > 1:
                         spot = rows_at(first + sub * SUB, SPAN)
-                        refs[14][which, spot] += dot(
+                        scratch[11][which, spot] += dot(
                             buf[sub * SUB:sub * SUB + SPAN, mine], right, (1, 0)
                         )
                         continue
@@ -275,15 +289,14 @@
 
         if tiles > 1:
             pl.loop(0, tiles)(each_tile)
-            part_ref[:, :, lanes] = refs[14][:, HALF:HALF + rows]
-            give_ref[:, :, lanes] = refs[14][:, HALF + rows:].astype(jnp.bfloat16)
+            part_ref[:, :, lanes] = scratch[11][:, HALF:HALF + rows]
+            give_ref[:, :, lanes] = scratch[11][:, HALF + rows:].astype(jnp.bfloat16)
         else:
             each_tile(0)
         for k in range(n):
             dq_refs[k][:, lanes] = dq_all[rows_at(place_ref[k] * r, r)]
-        return 0
-
-    lax.fori_loop(0, width // HEAD_DIM, each_head, 0)
+
+    over_heads(width // HEAD_DIM, refs[3:], each_head)
 
 
 def query_part(place, halo, turn, kv, qd, far, near):
@@ -308,6 +321,7 @@
     ]
     if rows != TILE:
         scratch.append(pltpu.VMEM((2, ext, HEAD_DIM), jnp.float32))
+    scratch = [pltpu.VMEM((min(QGROUP, heads), *x.shape), x.dtype) for x in scratch]
     outs = pl.pallas_call(
         lambda *refs: query_kernel(n, len(far), *refs),
         in_specs=[scalars] * 3 + [here] * (n + 1 + 2 * len(far)),
@@ -333,13 +347,14 @@
 def key_kernel(n, place_ref, halo_ref, turn_ref, *refs):
     kv_refs, refs = refs[:n], refs[n:]
     far_ref, stat_ref, part_ref, got_ref = refs[:4]
-    out_refs, (k_all, v_all, q_all, g_all, acc, w_buf, d_buf) = refs[4:4 + n], refs[4 + n:]
+    out_refs = refs[4:4 + n]
     r, width = kv_refs[0].shape[1:]
     rows = n * r
     ahead = ahead_by(turn_ref)
     steps = HALF // SUB
 
-    def each_head(h, _):
+    def each_head(h, scratch):
+        k_all, v_all, q_all, g_all, low, w_buf, d_buf = scratch
         lanes = rows_at(h * HEAD_DIM, HEAD_DIM)
         for k in range(n):
             at = rows_at(place_ref[k] * r, r)
@@ -349,11 +364,6 @@
             at = rows_at(halo_ref[i] * r, r)
             q_all[at] = far_ref[i, 0, :, lanes]
             g_all[at] = far_ref[i, 1, :, lanes]
-        acc[...] = part_ref[:, :, lanes]
-        for a in range(steps):
-            at = slice(rows - HALF + a * SUB, rows - HALF + (a + 1) * SUB)
-            there = slice((steps - 1 - a) * SUB, (steps - a) * SUB)
-            acc[:, at] += got_ref[:, there, lanes].astype(jnp.float32)
         for b in range(steps):
             here = slice(b * SUB, (b + 1) * SUB)
             there = slice((steps - 1 - b) * SUB, (steps - b) * SUB)
@@ -369,16 +379,22 @@
                 ds = w * (dot(v_all[at], grad, (1, 1)) - delta)
                 d_buf[at, here] = ds.astype(jnp.bfloat16)
         for which, buf, right in ((0, d_buf, q_all), (1, w_buf, g_all)):
-            for a in range(steps):
+            for a in range(rows // SUB):
                 at = slice(a * SUB, (a + 1) * SUB)
-                acc[which, at] += dot(buf[at, a * SUB:], right[a * SUB:], (1, 0))
+                value = part_ref[which, at, lanes]
+                if a < steps:
+                    value += dot(buf[at, a * SUB:], right[a * SUB:], (1, 0))
+                if a >= rows // SUB - steps:
+                    first = (rows // SUB - 1 - a) * SUB
+                    value += got_ref[which, first:first + SUB, lanes].astype(jnp.float32)
+                if which == 0:
+                    value = value * SCALE
+                low[which, at] = value.astype(jnp.bfloat16)
         for k in range(n):
             at = rows_at(place_ref[k] * r, r)
-            out_refs[k][0, :, lanes] = (acc[0, at] * SCALE).astype(jnp.bfloat16)
-            out_refs[k][1, :, lanes] = acc[1, at].astype(jnp.bfloat16)
-        return 0
-
-    lax.fori_loop(0, width // HEAD_DIM, each_head, 0)
+            out_refs[k][:, :, lanes] = low[:, at]
+
+    over_heads(width // HEAD_DIM, refs[4 + n:], each_head)
 
 
 def key_part(place, halo, turn, kv, far, stat, part, got):
@@ -387,19 +403,20 @@
     rows = n * r
     heads = width // HEAD_DIM
     here, scalars = pl.BlockSpec(memory_space=pltpu.VMEM), pl.BlockSpec(memory_space=pltpu.SMEM)
+    scratch = [
+        pltpu.VMEM((rows, HEAD_DIM), jnp.bfloat16),
+        pltpu.VMEM((rows, HEAD_DIM), jnp.bfloat16),
+        pltpu.VMEM((HALF, HEAD_DIM), jnp.bfloat16),
+        pltpu.VMEM((HALF, HEAD_DIM), jnp.bfloat16),
+        pltpu.VMEM((2, rows, HEAD_DIM), jnp.bfloat16),
+        pltpu.VMEM((HALF, HALF), jnp.bfloat16),
+        pltpu.VMEM((HALF, HALF), jnp.bfloat16),
+    ]
     return pl.pallas_call(
         lambda *refs: key_kernel(n, *refs),
         in_specs=[scalars] * 3 + [here] * (n + 4),
         out_specs=[here] * n,
-        scratch_shapes=[
-            pltpu.VMEM((rows, HEAD_DIM), jnp.bfloat16),
-            pltpu.VMEM((rows, HEAD_DIM), jnp.bfloat16),
-            pltpu.VMEM((HALF, HEAD_DIM), jnp.bfloat16),
-            pltpu.VMEM((HALF, HEAD_DIM), jnp.bfloat16),
-            pltpu.VMEM((2, rows, HEAD_DIM), jnp.float32),
-            pltpu.VMEM((HALF, HALF), jnp.bfloat16),
-            pltpu.VMEM((HALF, HALF), jnp.bfloat16),
-        ],
+        scratch_shapes=[pltpu.VMEM((min(KGROUP, heads), *x.shape), x.dtype) for x in scratch],
         out_shape=[jax.ShapeDtypeStruct((2, r, width), jnp.bfloat16)] * n,
         compiler_params=pltpu.CompilerParams(vmem_limit_bytes=VMEM_BYTES),
         cost_estimate=pl.CostEstimate(

time: 66.9 us -> 66.4 us (level)
  Pallas kernels: 15.3 us -> 14.2 us
  waiting for transfers between devices: 21.6 us -> 22.7 us
  transfers between devices with their start and end apart: 19 -> 19, of which waited for: 7 -> 7; matrix products, arithmetic and copies ran while one was open for 0% -> 0% of each run, Pallas kernels for 21% -> 20%
where the time goes in v7:
time: 66.4 us; the launch traced here: 66.1 us
  starting transfers between devices  24.2 us (36%)
  waiting for transfers between devices  22.7 us (34%)
  Pallas kernels  14.2 us (21%)
  local copies, waits for them, and re-layouts  4.16 us (6%)
  between operations  0.72 us (1%)
    ppermute x12, waiting for transfers between devices, exchanged(): lax.ppermute(pieces[k], 'head', [(i, i ^ k) for i in range(n)])  21.6 us
    ppermute x12, starting transfers between devices, exchanged(): lax.ppermute(pieces[k], 'head', [(i, i ^ k) for i in range(n)])  18.4 us
    pallas_call x1, Pallas kernels, query_part(): pl.pallas_call(lambda *refs: query_kernel(n, len(far), *refs), in_specs=[...  8.86 us
    ppermute x7, starting transfers between devices, swapped(): return lax.ppermute(array, ('head', 'blk'), pairs)  5.78 us
    unnamed x8, local copies, waits for them, and re-layouts  4.16 us
    pallas_call x1, Pallas kernels, key_part(): pl.pallas_call(lambda *refs: key_kernel(n, *refs), in_specs=[scalars] * 3...  2.86 us
    pallas_call x2, Pallas kernels, merged(): pl.pallas_call(lambda *refs: merge_kernel(n, *refs), in_specs=[pl.BlockSp...  1.84 us
  transfers between devices with their start and end apart: 19, of which 7 were waited for; matrix products, arithmetic and copies ran while one was open for 0% of the time, Pallas kernels for 20%

profile of v7, /device:TPU:0, one launch (start us, length us, event | category | flops | bytes accessed | tf_op | source)
XLA Modules:
  0.0 66.1 jit_solution(6952672811401010939)
XLA Ops:
  0.6 0.0 copy-start
  0.6 1.0 %copy-done = bf16[128,2048]{1,0:T(8,128)(2,1)S(1)} copy-done((bf16[128,2048]{1,0:T(8,128)(2,1)S(1)}, bf16[128,2048]{1,0:T(8,128)(2,1)}, u32[]{:S(2)}) %copy-start) | copy-done | bytes 524312
  1.7 0.0 copy-start.1
  1.7 1.0 %copy-done.1 = bf16[128,2048]{1,0:T(8,128)(2,1)S(1)} copy-done((bf16[128,2048]{1,0:T(8,128)(2,1)S(1)}, bf16[128,2048]{1,0:T(8,128)(2,1)}, u32[]{:S(2)}) %copy-start.1) | copy-done | bytes 524312
  2.7 0.2 pack.2
  3.0 3.0 %collective-permute-start = (bf16[2,128,512]{2,1,0:T(8,128)(2,1)S(1)}, bf16[2,128,512]{2,1,0:T(8,128)(2,1)S(1)}, u32[]{:S(2)}, u32[]{:S(2)}) collective-permute-start(bf16[2,128,512]{2,1,0:T(8,128)(2,1)S(1)} %get-tuple-element.25), channel_id=1, source_target_pairs={{0,8},{8,0},{16,24},{24,16},{1,9},{9,1},{17,25},{25,17},{2,10},{10... | collective-permute-start | bytes 786440 | tf_op jit(solution)/shard_map/ppermute | solution.py:447
  6.0 1.5 %collective-permute-start.1 = (bf16[2,128,512]{2,1,0:T(8,128)(2,1)S(1)}, bf16[2,128,512]{2,1,0:T(8,128)(2,1)S(1)}, u32[]{:S(2)}, u32[]{:S(2)}) collective-permute-start(bf16[2,128,512]{2,1,0:T(8,128)(2,1)S(1)} %get-tuple-element.26), channel_id=1, source_target_pairs={{0,16},{8,24},{16,0},{24,8},{1,17},{9,25},{17,1},{25,9},{2,18},{10... | collective-permute-start | bytes 786440 | tf_op jit(solution)/shard_map/ppermute | solution.py:447
  7.5 0.0 copy-start.2
  7.5 1.0 %copy-done.2 = bf16[128,2048]{1,0:T(8,128)(2,1)S(1)} copy-done((bf16[128,2048]{1,0:T(8,128)(2,1)S(1)}, bf16[128,2048]{1,0:T(8,128)(2,1)}, u32[]{:S(2)}) %copy-start.2) | copy-done | bytes 524312
  8.5 0.0 copy-start.3
  8.5 1.0 %copy-done.3 = bf16[128,2048]{1,0:T(8,128)(2,1)S(1)} copy-done((bf16[128,2048]{1,0:T(8,128)(2,1)S(1)}, bf16[128,2048]{1,0:T(8,128)(2,1)}, u32[]{:S(2)}) %copy-start.3) | copy-done | bytes 524312
  9.6 0.2 pack.3
  9.8 0.6 collective-permute-start.3
  10.4 1.4 %collective-permute-start.2 = (bf16[2,128,512]{2,1,0:T(8,128)(2,1)S(1)}, bf16[2,128,512]{2,1,0:T(8,128)(2,1)S(1)}, u32[]{:S(2)}, u32[]{:S(2)}) collective-permute-start(bf16[2,128,512]{2,1,0:T(8,128)(2,1)S(1)} %get-tuple-element.27), channel_id=1, source_target_pairs={{0,24},{8,16},{16,8},{24,0},{1,25},{9,17},{17,9},{25,1},{2,26},{10... | collective-permute-start | bytes 786440 | tf_op jit(solution)/shard_map/ppermute | solution.py:447
  11.8 1.5 %collective-permute-start.4 = (bf16[2,128,512]{2,1,0:T(8,128)(2,1)S(1)}, bf16[2,128,512]{2,1,0:T(8,128)(2,1)S(1)}, u32[]{:S(2)}, u32[]{:S(2)}) collective-permute-start(bf16[2,128,512]{2,1,0:T(8,128)(2,1)S(1)} %get-tuple-element.30), channel_id=1, source_target_pairs={{0,16},{8,24},{16,0},{24,8},{1,17},{9,25},{17,1},{25,9},{2,18},{10... | collective-permute-start | bytes 786440 | tf_op jit(solution)/shard_map/ppermute | solution.py:447
  13.4 0.0 collective-permute-done.refs_1_.refs_4_
  13.4 2.7 %collective-permute-start.5 = (bf16[2,128,512]{2,1,0:T(8,128)(2,1)S(1)}, bf16[2,128,512]{2,1,0:T(8,128)(2,1)S(1)}, u32[]{:S(2)}, u32[]{:S(2)}) collective-permute-start(bf16[2,128,512]{2,1,0:T(8,128)(2,1)S(1)} %get-tuple-element.31), channel_id=1, source_target_pairs={{0,24},{8,16},{16,8},{24,0},{1,25},{9,17},{17,9},{25,1},{2,26},{10... | collective-permute-start | bytes 786440 | tf_op jit(solution)/shard_map/ppermute | solution.py:447
  16.1 0.1 pad_add_fusion.refs_2_
  16.2 0.0 collective-permute-done.1.refs_2_.refs_5_
  16.2 0.1 stack.20
  16.3 0.7 %collective-permute-start.6 = (bf16[3,2,128,512]{3,2,1,0:T(8,128)(2,1)S(1)}, bf16[3,2,128,512]{3,2,1,0:T(8,128)(2,1)S(1)}, u32[]{:S(2)}, u32[]{:S(2)}) collective-permute-start(bf16[3,2,128,512]{3,2,1,0:T(8,128)(2,1)S(1)} %stack.20), channel_id=1, source_target_pairs={{1,2},{2,1},{3,4},{4,3},{5,6},{6,5},{9,10},{10,9},{11,12},{12,11},... | collective-permute-start | bytes 2359304 | tf_op jit(solution)/shard_map/ppermute | solution.py:441
  17.0 2.1 %collective-permute-done.3.refs_1_ = bf16[2,128,512]{2,1,0:T(8,128)(2,1)S(1)} collective-permute-done((bf16[2,128,512]{2,1,0:T(8,128)(2,1)S(1)}, bf16[2,128,512]{2,1,0:T(8,128)(2,1)S(1)}, u32[]{:S(2)}, u32[]{:S(2)}) %collective-permute-start.3) | collective-permute-done | bytes 262176 | tf_op jit(solution)/shard_map/ppermute | solution.py:447
  19.1 0.9 %collective-permute-start.8 = (bf16[3,2,128,512]{3,2,1,0:T(8,128)(2,1)S(1)}, bf16[3,2,128,512]{3,2,1,0:T(8,128)(2,1)S(1)}, u32[]{:S(2)}, u32[]{:S(2)}) collective-permute-start(bf16[3,2,128,512]{3,2,1,0:T(8,128)(2,1)S(1)} %stack.20), channel_id=1, source_target_pairs={{0,1},{1,0},{2,3},{3,2},{4,5},{5,4},{6,7},{7,6},{8,9},{9,8},{10,11... | collective-permute-start | bytes 2359304 | tf_op jit(solution)/shard_map/ppermute | solution.py:441
  20.0 6.0 %collective-permute-done.2.refs_6_ = bf16[2,128,512]{2,1,0:T(8,128)(2,1)S(1)} collective-permute-done((bf16[2,128,512]{2,1,0:T(8,128)(2,1)S(1)}, bf16[2,128,512]{2,1,0:T(8,128)(2,1)S(1)}, u32[]{:S(2)}, u32[]{:S(2)}) %collective-permute-start.2) | collective-permute-done | bytes 262176 | tf_op jit(solution)/shard_map/ppermute | solution.py:447
  26.0 1.4 %collective-permute-start.7 = (bf16[1,2,128,512]{3,2,1,0:T(8,128)(2,1)S(1)}, bf16[1,2,128,512]{3,2,1,0:T(8,128)(2,1)S(1)}, u32[]{:S(2)}, u32[]{:S(2)}) collective-permute-start(bf16[1,2,128,512]{3,2,1,0:T(8,128)(2,1)S(1)} %bitcast.3), channel_id=1, source_target_pairs={{0,8},{1,2},{2,1},{3,4},{4,3},{5,6},{6,5},{7,15},{8,0},{9,10},{10,... | collective-permute-start | bytes 786440 | tf_op jit(solution)/shard_map/ppermute | solution.py:441
  27.3 3.2 %collective-permute-done.4.refs_2_ = bf16[2,128,512]{2,1,0:T(8,128)(2,1)S(1)} collective-permute-done((bf16[2,128,512]{2,1,0:T(8,128)(2,1)S(1)}, bf16[2,128,512]{2,1,0:T(8,128)(2,1)S(1)}, u32[]{:S(2)}, u32[]{:S(2)}) %collective-permute-start.4) | collective-permute-done | bytes 262176 | tf_op jit(solution)/shard_map/ppermute | solution.py:447
  30.6 0.0 collective-permute-start.9
  30.6 0.0 collective-permute-done.5.refs_3_
  30.6 0.1 stack.19.refs_7_
  30.7 1.3 %collective-permute-start.13 = (bf16[4,2,128,512]{3,2,1,0:T(8,128)(2,1)S(1)}, bf16[4,2,128,512]{3,2,1,0:T(8,128)(2,1)S(1)}, u32[]{:S(2)}, u32[]{:S(2)}) collective-permute-start(bf16[4,2,128,512]{3,2,1,0:T(8,128)(2,1)S(1)} %stack.19.refs_7_), channel_id=1, source_target_pairs={{0,8},{1,2},{2,1},{3,4},{4,3},{5,6},{6,5},{7,15},{8,0},{9,10},{10,... | collective-permute-start | bytes 3145736 | tf_op jit(solution)/shard_map/ppermute | solution.py:441
  32.0 0.3 collective-permute-done.7.refs_9_
  32.3 0.0 collective-permute-done.9.refs_11_
  32.3 0.0 collective-permute-done.6.refs_8_
  32.3 0.0 collective-permute-done.8.refs_10_
  32.3 8.9 %query_part.1 = (bf16[128,512]{1,0:T(8,128)(2,1)S(1)}, bf16[128,512]{1,0:T(8,128)(2,1)S(1)}, bf16[128,512]{1,0:T(8,128)(2,1)S(1)}, bf16[128,512]{1,0:T(8,128)(2,...) custom-call(s32[4]{0:T(128)S(1)} %xor_xor_fusion.refs_0_.refs_1_, ...), custom_call_target="tpu_custom_call" | custom-call | flops 3355443200 | bytes 3145728 | tf_op jit(solution)/shard_map/query_part/pallas_call | solution.py:325
  41.2 0.2 collective-permute-start.15
  41.4 1.3 %collective-permute-start.14 = (f32[4,2,512]{2,1,0:T(2,128)S(1)}, f32[4,2,512]{2,1,0:T(2,128)S(1)}, u32[]{:S(2)}, u32[]{:S(2)}) collective-permute-start(f32[4,2,512]{2,1,0:T(2,128)S(1)} %get-tuple-element.36), channel_id=1, source_target_pairs={{0,8},{1,2},{2,1},{3,4},{4,3},{5,6},{6,5},{7,15},{8,0},{9,10},{10,... | collective-permute-start | bytes 49160 | tf_op jit(solution)/shard_map/ppermute | solution.py:441
  42.7 0.7 %collective-permute-start.10 = (bf16[128,512]{1,0:T(8,128)(2,1)S(1)}, bf16[128,512]{1,0:T(8,128)(2,1)S(1)}, u32[]{:S(2)}, u32[]{:S(2)}) collective-permute-start(bf16[128,512]{1,0:T(8,128)(2,1)S(1)} %get-tuple-element.33), channel_id=1, source_target_pairs={{0,8},{8,0},{16,24},{24,16},{1,9},{9,1},{17,25},{25,17},{2,10},{10... | collective-permute-start | bytes 393224 | tf_op jit(solution)/shard_map/ppermute | solution.py:447
  43.4 1.5 %collective-permute-start.11 = (bf16[128,512]{1,0:T(8,128)(2,1)S(1)}, bf16[128,512]{1,0:T(8,128)(2,1)S(1)}, u32[]{:S(2)}, u32[]{:S(2)}) collective-permute-start(bf16[128,512]{1,0:T(8,128)(2,1)S(1)} %get-tuple-element.34), channel_id=1, source_target_pairs={{0,16},{8,24},{16,0},{24,8},{1,17},{9,25},{17,1},{25,9},{2,18},{10... | collective-permute-start | bytes 393224 | tf_op jit(solution)/shard_map/ppermute | solution.py:447
  45.0 0.8 %collective-permute-done.14.refs_8_ = f32[4,2,512]{2,1,0:T(2,128)S(1)} collective-permute-done((f32[4,2,512]{2,1,0:T(2,128)S(1)}, f32[4,2,512]{2,1,0:T(2,128)S(1)}, u32[]{:S(2)}, u32[]{:S(2)}) %collective-permute-start.14) | collective-permute-done | bytes 16416 | tf_op jit(solution)/shard_map/ppermute | solution.py:441
  45.8 1.8 %collective-permute-start.12 = (bf16[128,512]{1,0:T(8,128)(2,1)S(1)}, bf16[128,512]{1,0:T(8,128)(2,1)S(1)}, u32[]{:S(2)}, u32[]{:S(2)}) collective-permute-start(bf16[128,512]{1,0:T(8,128)(2,1)S(1)} %get-tuple-element.35), channel_id=1, source_target_pairs={{0,24},{8,16},{16,8},{24,0},{1,25},{9,17},{17,9},{25,1},{2,26},{10... | collective-permute-start | bytes 393224 | tf_op jit(solution)/shard_map/ppermute | solution.py:447
  47.6 0.0 collective-permute-done.13.refs_7_
  47.6 0.0 collective-permute-done.15.refs_10_
  47.6 2.9 %key_part.1 = (bf16[2,128,512]{2,1,0:T(8,128)(2,1)S(1)}, bf16[2,128,512]{2,1,0:T(8,128)(2,1)S(1)}, bf16[2,128,512]{2,1,0:T(8,128)(2,1)S(1)}, bf16[2,128,512]{2,1,0:T(8,128)(2,1)S(1)}) custom-call(s32[4]{0:T(128)S(1)} %xor_xor_fusion.refs_0_.refs_1_, s32[4]{0:T(128)S(1)} %xor_xor_fusion.refs_0_.refs_1_, s32[2]{0:T(128)S(1)} %pad_add_fusion.refs_2_, ...), custom_call_target="tpu_custom_call" | custom-call | flops 30000001024 | bytes 6291456 | tf_op jit(solution)/shard_map/key_part/pallas_call | solution.py:415
  50.4 1.2 %collective-permute-start.16 = (bf16[2,128,512]{2,1,0:T(8,128)(2,1)S(1)}, bf16[2,128,512]{2,1,0:T(8,128)(2,1)S(1)}, u32[]{:S(2)}, u32[]{:S(2)}) collective-permute-start(bf16[2,128,512]{2,1,0:T(8,128)(2,1)S(1)} %get-tuple-element.40), channel_id=1, source_target_pairs={{0,8},{8,0},{16,24},{24,16},{1,9},{9,1},{17,25},{25,17},{2,10},{10... | collective-permute-start | bytes 786440 | tf_op jit(solution)/shard_map/ppermute | solution.py:447
  51.7 0.5 collective-permute-start.17
  52.2 0.0 collective-permute-done.10.refs_1_
  52.2 1.8 %collective-permute-start.18 = (bf16[2,128,512]{2,1,0:T(8,128)(2,1)S(1)}, bf16[2,128,512]{2,1,0:T(8,128)(2,1)S(1)}, u32[]{:S(2)}, u32[]{:S(2)}) collective-permute-start(bf16[2,128,512]{2,1,0:T(8,128)(2,1)S(1)} %get-tuple-element.42), channel_id=1, source_target_pairs={{0,24},{8,16},{16,8},{24,0},{1,25},{9,17},{17,9},{25,1},{2,26},{10... | collective-permute-start | bytes 786440 | tf_op jit(solution)/shard_map/ppermute | solution.py:447
  54.0 0.0 collective-permute-done.11.refs_2_
  54.0 0.0 collective-permute-done.12.refs_3_
  54.0 0.8 %merge.2 = bf16[128,2048]{1,0:T(8,128)(2,1)} custom-call(bf16[128,512]{1,0:T(8,128)(2,1)S(1)} %get-tuple-element.32.refs_0_, bf16[128,512]{1,0:T(8,128)(2,1)S(1)} %collective-permute-done.10.refs_1_, bf16[128,512]{1,0:T(8,128)(2,1)S(1)} %collective-permute-done.11.refs_2_, bf16[128,512]{1,0:T(8,128)(2,1)S(1)} %collective-permute-done.12.refs_3_), custom_call_target="tpu_custom_call" | custom-call | flops 30000001024 | tf_op jit(solution)/shard_map/merge/pallas_call | solution.py:117
  54.8 4.9 %collective-permute-done.16.refs_1_ = bf16[2,128,512]{2,1,0:T(8,128)(2,1)S(1)} collective-permute-done((bf16[2,128,512]{2,1,0:T(8,128)(2,1)S(1)}, bf16[2,128,512]{2,1,0:T(8,128)(2,1)S(1)}, u32[]{:S(2)}, u32[]{:S(2)}) %collective-permute-start.16) | collective-permute-done | bytes 262176 | tf_op jit(solution)/shard_map/ppermute | solution.py:447
  59.7 5.3 %collective-permute-done.17.refs_2_ = bf16[2,128,512]{2,1,0:T(8,128)(2,1)S(1)} collective-permute-done((bf16[2,128,512]{2,1,0:T(8,128)(2,1)S(1)}, bf16[2,128,512]{2,1,0:T(8,128)(2,1)S(1)}, u32[]{:S(2)}, u32[]{:S(2)}) %collective-permute-start.17) | collective-permute-done | bytes 262176 | tf_op jit(solution)/shard_map/ppermute | solution.py:447
  65.1 0.0 collective-permute-done.18.refs_3_
  65.1 1.0 %merge.3 = (bf16[128,2048]{1,0:T(8,128)(2,1)}, bf16[128,2048]{1,0:T(8,128)(2,1)}) custom-call(bf16[2,128,512]{2,1,0:T(8,128)(2,1)S(1)} %get-tuple-element.39.refs_0_, bf16[2,128,512]{2,1,0:T(8,128)(2,1)S(1)} %collective-permute-done.16.refs_1_, bf16[2,128,512]{2,1,0:T(8,128)(2,1)S(1)} %collective-permute-done.17.refs_2_, ...), custom_call_target="tpu_custom_call" | custom-call | tf_op jit(solution)/shard_map/merge/pallas_call | solution.py:117
  (1 shorter events, 0.0 us)
Async XLA Ops:
  0.6 1.0 %copy-start = (bf16[128,2048]{1,0:T(8,128)(2,1)S(1)}, bf16[128,2048]{1,0:T(8,128)(2,1)}, u32[]{:S(2)}) copy-start(bf16[128,2048]{1,0:T(8,128)(2,1)} %refs_0_.2) | copy-start | bytes 1572868
  1.7 1.0 %copy-start.1 = (bf16[128,2048]{1,0:T(8,128)(2,1)S(1)}, bf16[128,2048]{1,0:T(8,128)(2,1)}, u32[]{:S(2)}) copy-start(bf16[128,2048]{1,0:T(8,128)(2,1)} %refs_1_.2) | copy-start | bytes 1572868
  3.0 10.4 %collective-permute-start = (bf16[2,128,512]{2,1,0:T(8,128)(2,1)S(1)}, bf16[2,128,512]{2,1,0:T(8,128)(2,1)S(1)}, u32[]{:S(2)}, u32[]{:S(2)}) collective-permute-start(bf16[2,128,512]{2,1,0:T(8,128)(2,1)S(1)} %get-tuple-element.25), channel_id=1, source_target_pairs={{0,8},{8,0},{16,24},{24,16},{1,9},{9,1},{17,25},{25,17},{2,10},{10... | collective-permute-start | bytes 786440 | tf_op jit(solution)/shard_map/ppermute | solution.py:447
  6.0 10.2 %collective-permute-start.1 = (bf16[2,128,512]{2,1,0:T(8,128)(2,1)S(1)}, bf16[2,128,512]{2,1,0:T(8,128)(2,1)S(1)}, u32[]{:S(2)}, u32[]{:S(2)}) collective-permute-start(bf16[2,128,512]{2,1,0:T(8,128)(2,1)S(1)} %get-tuple-element.26), channel_id=1, source_target_pairs={{0,16},{8,24},{16,0},{24,8},{1,17},{9,25},{17,1},{25,9},{2,18},{10... | collective-permute-start | bytes 786440 | tf_op jit(solution)/shard_map/ppermute | solution.py:447
  7.5 1.0 %copy-start.2 = (bf16[128,2048]{1,0:T(8,128)(2,1)S(1)}, bf16[128,2048]{1,0:T(8,128)(2,1)}, u32[]{:S(2)}) copy-start(bf16[128,2048]{1,0:T(8,128)(2,1)} %refs_0_.3) | copy-start | bytes 1572868
  8.5 1.0 %copy-start.3 = (bf16[128,2048]{1,0:T(8,128)(2,1)S(1)}, bf16[128,2048]{1,0:T(8,128)(2,1)}, u32[]{:S(2)}) copy-start(bf16[128,2048]{1,0:T(8,128)(2,1)} %refs_1_.3) | copy-start | bytes 1572868
  9.8 9.3 %collective-permute-start.3 = (bf16[2,128,512]{2,1,0:T(8,128)(2,1)S(1)}, bf16[2,128,512]{2,1,0:T(8,128)(2,1)S(1)}, u32[]{:S(2)}, u32[]{:S(2)}) collective-permute-start(bf16[2,128,512]{2,1,0:T(8,128)(2,1)S(1)} %get-tuple-element.29), channel_id=1, source_target_pairs={{0,8},{8,0},{16,24},{24,16},{1,9},{9,1},{17,25},{25,17},{2,10},{10... | collective-permute-start | bytes 786440 | tf_op jit(solution)/shard_map/ppermute | solution.py:447
  10.4 15.5 %collective-permute-start.2 = (bf16[2,128,512]{2,1,0:T(8,128)(2,1)S(1)}, bf16[2,128,512]{2,1,0:T(8,128)(2,1)S(1)}, u32[]{:S(2)}, u32[]{:S(2)}) collective-permute-start(bf16[2,128,512]{2,1,0:T(8,128)(2,1)S(1)} %get-tuple-element.27), channel_id=1, source_target_pairs={{0,24},{8,16},{16,8},{24,0},{1,25},{9,17},{17,9},{25,1},{2,26},{10... | collective-permute-start | bytes 786440 | tf_op jit(solution)/shard_map/ppermute | solution.py:447
  11.8 18.7 %collective-permute-start.4 = (bf16[2,128,512]{2,1,0:T(8,128)(2,1)S(1)}, bf16[2,128,512]{2,1,0:T(8,128)(2,1)S(1)}, u32[]{:S(2)}, u32[]{:S(2)}) collective-permute-start(bf16[2,128,512]{2,1,0:T(8,128)(2,1)S(1)} %get-tuple-element.30), channel_id=1, source_target_pairs={{0,16},{8,24},{16,0},{24,8},{1,17},{9,25},{17,1},{25,9},{2,18},{10... | collective-permute-start | bytes 786440 | tf_op jit(solution)/shard_map/ppermute | solution.py:447
  13.4 17.2 %collective-permute-start.5 = (bf16[2,128,512]{2,1,0:T(8,128)(2,1)S(1)}, bf16[2,128,512]{2,1,0:T(8,128)(2,1)S(1)}, u32[]{:S(2)}, u32[]{:S(2)}) collective-permute-start(bf16[2,128,512]{2,1,0:T(8,128)(2,1)S(1)} %get-tuple-element.31), channel_id=1, source_target_pairs={{0,24},{8,16},{16,8},{24,0},{1,25},{9,17},{17,9},{25,1},{2,26},{10... | collective-permute-start | bytes 786440 | tf_op jit(solution)/shard_map/ppermute | solution.py:447
  16.3 16.0 %collective-permute-start.6 = (bf16[3,2,128,512]{3,2,1,0:T(8,128)(2,1)S(1)}, bf16[3,2,128,512]{3,2,1,0:T(8,128)(2,1)S(1)}, u32[]{:S(2)}, u32[]{:S(2)}) collective-permute-start(bf16[3,2,128,512]{3,2,1,0:T(8,128)(2,1)S(1)} %stack.20), channel_id=1, source_target_pairs={{1,2},{2,1},{3,4},{4,3},{5,6},{6,5},{9,10},{10,9},{11,12},{12,11},... | collective-permute-start | bytes 2359304 | tf_op jit(solution)/shard_map/ppermute | solution.py:441
  19.1 13.2 %collective-permute-start.8 = (bf16[3,2,128,512]{3,2,1,0:T(8,128)(2,1)S(1)}, bf16[3,2,128,512]{3,2,1,0:T(8,128)(2,1)S(1)}, u32[]{:S(2)}, u32[]{:S(2)}) collective-permute-start(bf16[3,2,128,512]{3,2,1,0:T(8,128)(2,1)S(1)} %stack.20), channel_id=1, source_target_pairs={{0,1},{1,0},{2,3},{3,2},{4,5},{5,4},{6,7},{7,6},{8,9},{9,8},{10,11... | collective-permute-start | bytes 2359304 | tf_op jit(solution)/shard_map/ppermute | solution.py:441
  26.0 6.4 %collective-permute-start.7 = (bf16[1,2,128,512]{3,2,1,0:T(8,128)(2,1)S(1)}, bf16[1,2,128,512]{3,2,1,0:T(8,128)(2,1)S(1)}, u32[]{:S(2)}, u32[]{:S(2)}) collective-permute-start(bf16[1,2,128,512]{3,2,1,0:T(8,128)(2,1)S(1)} %bitcast.3), channel_id=1, source_target_pairs={{0,8},{1,2},{2,1},{3,4},{4,3},{5,6},{6,5},{7,15},{8,0},{9,10},{10,... | collective-permute-start | bytes 786440 | tf_op jit(solution)/shard_map/ppermute | solution.py:441
  30.6 1.8 %collective-permute-start.9 = (bf16[1,2,128,512]{3,2,1,0:T(8,128)(2,1)S(1)}, bf16[1,2,128,512]{3,2,1,0:T(8,128)(2,1)S(1)}, u32[]{:S(2)}, u32[]{:S(2)}) collective-permute-start(bf16[1,2,128,512]{3,2,1,0:T(8,128)(2,1)S(1)} %bitcast.4), channel_id=1, source_target_pairs={{0,1},{1,0},{2,3},{3,2},{4,5},{5,4},{6,7},{7,6},{8,9},{9,8},{10,11... | collective-permute-start | bytes 786440 | tf_op jit(solution)/shard_map/ppermute | solution.py:441
  30.7 16.8 %collective-permute-start.13 = (bf16[4,2,128,512]{3,2,1,0:T(8,128)(2,1)S(1)}, bf16[4,2,128,512]{3,2,1,0:T(8,128)(2,1)S(1)}, u32[]{:S(2)}, u32[]{:S(2)}) collective-permute-start(bf16[4,2,128,512]{3,2,1,0:T(8,128)(2,1)S(1)} %stack.19.refs_7_), channel_id=1, source_target_pairs={{0,8},{1,2},{2,1},{3,4},{4,3},{5,6},{6,5},{7,15},{8,0},{9,10},{10,... | collective-permute-start | bytes 3145736 | tf_op jit(solution)/shard_map/ppermute | solution.py:441
  41.2 6.4 %collective-permute-start.15 = (bf16[2,512,512]{2,1,0:T(8,128)(2,1)S(1)}, bf16[2,512,512]{2,1,0:T(8,128)(2,1)S(1)}, u32[]{:S(2)}, u32[]{:S(2)}) collective-permute-start(bf16[2,512,512]{2,1,0:T(8,128)(2,1)S(1)} %get-tuple-element.38), channel_id=1, source_target_pairs={{0,1},{1,0},{2,3},{3,2},{4,5},{5,4},{6,7},{7,6},{8,9},{9,8},{10,11... | collective-permute-start | bytes 3145736 | tf_op jit(solution)/shard_map/ppermute | solution.py:441
  41.4 4.3 %collective-permute-start.14 = (f32[4,2,512]{2,1,0:T(2,128)S(1)}, f32[4,2,512]{2,1,0:T(2,128)S(1)}, u32[]{:S(2)}, u32[]{:S(2)}) collective-permute-start(f32[4,2,512]{2,1,0:T(2,128)S(1)} %get-tuple-element.36), channel_id=1, source_target_pairs={{0,8},{1,2},{2,1},{3,4},{4,3},{5,6},{6,5},{7,15},{8,0},{9,10},{10,... | collective-permute-start | bytes 49160 | tf_op jit(solution)/shard_map/ppermute | solution.py:441
  42.7 9.4 %collective-permute-start.10 = (bf16[128,512]{1,0:T(8,128)(2,1)S(1)}, bf16[128,512]{1,0:T(8,128)(2,1)S(1)}, u32[]{:S(2)}, u32[]{:S(2)}) collective-permute-start(bf16[128,512]{1,0:T(8,128)(2,1)S(1)} %get-tuple-element.33), channel_id=1, source_target_pairs={{0,8},{8,0},{16,24},{24,16},{1,9},{9,1},{17,25},{25,17},{2,10},{10... | collective-permute-start | bytes 393224 | tf_op jit(solution)/shard_map/ppermute | solution.py:447
  43.4 10.5 %collective-permute-start.11 = (bf16[128,512]{1,0:T(8,128)(2,1)S(1)}, bf16[128,512]{1,0:T(8,128)(2,1)S(1)}, u32[]{:S(2)}, u32[]{:S(2)}) collective-permute-start(bf16[128,512]{1,0:T(8,128)(2,1)S(1)} %get-tuple-element.34), channel_id=1, source_target_pairs={{0,16},{8,24},{16,0},{24,8},{1,17},{9,25},{17,1},{25,9},{2,18},{10... | collective-permute-start | bytes 393224 | tf_op jit(solution)/shard_map/ppermute | solution.py:447
  45.8 8.2 %collective-permute-start.12 = (bf16[128,512]{1,0:T(8,128)(2,1)S(1)}, bf16[128,512]{1,0:T(8,128)(2,1)S(1)}, u32[]{:S(2)}, u32[]{:S(2)}) collective-permute-start(bf16[128,512]{1,0:T(8,128)(2,1)S(1)} %get-tuple-element.35), channel_id=1, source_target_pairs={{0,24},{8,16},{16,8},{24,0},{1,25},{9,17},{17,9},{25,1},{2,26},{10... | collective-permute-start | bytes 393224 | tf_op jit(solution)/shard_map/ppermute | solution.py:447
  50.4 9.3 %collective-permute-start.16 = (bf16[2,128,512]{2,1,0:T(8,128)(2,1)S(1)}, bf16[2,128,512]{2,1,0:T(8,128)(2,1)S(1)}, u32[]{:S(2)}, u32[]{:S(2)}) collective-permute-start(bf16[2,128,512]{2,1,0:T(8,128)(2,1)S(1)} %get-tuple-element.40), channel_id=1, source_target_pairs={{0,8},{8,0},{16,24},{24,16},{1,9},{9,1},{17,25},{25,17},{2,10},{10... | collective-permute-start | bytes 786440 | tf_op jit(solution)/shard_map/ppermute | solution.py:447
  51.7 13.4 %collective-permute-start.17 = (bf16[2,128,512]{2,1,0:T(8,128)(2,1)S(1)}, bf16[2,128,512]{2,1,0:T(8,128)(2,1)S(1)}, u32[]{:S(2)}, u32[]{:S(2)}) collective-permute-start(bf16[2,128,512]{2,1,0:T(8,128)(2,1)S(1)} %get-tuple-element.41), channel_id=1, source_target_pairs={{0,16},{8,24},{16,0},{24,8},{1,17},{9,25},{17,1},{25,9},{2,18},{10... | collective-permute-start | bytes 786440 | tf_op jit(solution)/shard_map/ppermute | solution.py:447
  52.2 12.9 %collective-permute-start.18 = (bf16[2,128,512]{2,1,0:T(8,128)(2,1)S(1)}, bf16[2,128,512]{2,1,0:T(8,128)(2,1)S(1)}, u32[]{:S(2)}, u32[]{:S(2)}) collective-permute-start(bf16[2,128,512]{2,1,0:T(8,128)(2,1)S(1)} %get-tuple-element.42), channel_id=1, source_target_pairs={{0,24},{8,16},{16,8},{24,0},{1,25},{9,17},{17,9},{25,1},{2,26},{10... | collective-permute-start | bytes 786440 | tf_op jit(solution)/shard_map/ppermute | solution.py:447

commit v8 on v7

--- a/solution.py
+++ b/solution.py
@@ -23,7 +23,7 @@
 RATE = SCALE * math.log2(math.e)
 VMEM_BYTES = 46 * 1024 * 1024
 QGROUP = 4
-KGROUP = 4
+KGROUP = 2
 SMALL_BYTES = 8 * 1024 * 1024
 
 
@@ -122,6 +122,40 @@
         scratch_shapes=[pltpu.SemaphoreType.DMA((count * n,))],
         compiler_params=pltpu.CompilerParams(vmem_limit_bytes=SMALL_BYTES),
         cost_estimate=pl.CostEstimate(flops=flops, bytes_accessed=0, transcendentals=0),
+        name="merge",
+    )(*pieces)
+
+
+def merge_pair_kernel(n, *refs):
+    outs, sems = refs[-3:-1], refs[-1]
+    batches = len(refs[:-3]) // n
+    width = refs[0].shape[-1]
+    me = lax.axis_index("head")
+    copies = []
+    for b in range(batches):
+        for k in range(n):
+            start = ((me ^ k) * batches + b) * width
+            columns = pl.ds(pl.multiple_of(start, 128), width)
+            for which, out in enumerate(outs):
+                source, sem = refs[b * n + k].at[which], sems.at[2 * (b * n + k) + which]
+                copies.append(pltpu.make_async_copy(source, out.at[:, columns], sem))
+    for copy in copies:
+        copy.start()
+    for copy in copies:
+        copy.wait()
+
+
+def merged_pair(batches):
+    n = len(batches[0])
+    r, width = batches[0][0].shape[-2:]
+    pieces = [piece for batch in batches for piece in batch]
+    return pl.pallas_call(
+        lambda *refs: merge_pair_kernel(n, *refs),
+        in_specs=[pl.BlockSpec(memory_space=pltpu.VMEM)] * len(pieces),
+        out_specs=[pl.BlockSpec(memory_space=pl.ANY)] * 2,
+        out_shape=[jax.ShapeDtypeStruct((r, len(pieces) * width), pieces[0].dtype)] * 2,
+        scratch_shapes=[pltpu.SemaphoreType.DMA((2 * len(pieces),))],
+        compiler_params=pltpu.CompilerParams(vmem_limit_bytes=SMALL_BYTES),
         name="merge",
     )(*pieces)
 
@@ -344,18 +378,19 @@
     return outs[:n], outs[n], outs[n + 1], outs[n + 2]
 
 
-def key_kernel(n, place_ref, halo_ref, turn_ref, *refs):
+def key_kernel(n, begin, place_ref, halo_ref, turn_ref, *refs):
     kv_refs, refs = refs[:n], refs[n:]
     far_ref, stat_ref, part_ref, got_ref = refs[:4]
     out_refs = refs[4:4 + n]
-    r, width = kv_refs[0].shape[1:]
+    r, width = out_refs[0].shape[1:]
     rows = n * r
     ahead = ahead_by(turn_ref)
     steps = HALF // SUB
 
-    def each_head(h, scratch):
+    def each_head(part, scratch):
         k_all, v_all, q_all, g_all, low, w_buf, d_buf = scratch
-        lanes = rows_at(h * HEAD_DIM, HEAD_DIM)
+        h = begin + part
+        lanes, out_lanes = rows_at(h * HEAD_DIM, HEAD_DIM), rows_at(part * HEAD_DIM, HEAD_DIM)
         for k in range(n):
             at = rows_at(place_ref[k] * r, r)
             k_all[at] = kv_refs[k][0, :, lanes]
@@ -392,16 +427,16 @@
                 low[which, at] = value.astype(jnp.bfloat16)
         for k in range(n):
             at = rows_at(place_ref[k] * r, r)
-            out_refs[k][:, :, lanes] = low[:, at]
+            out_refs[k][:, :, out_lanes] = low[:, at]
 
     over_heads(width // HEAD_DIM, refs[4 + n:], each_head)
 
 
-def key_part(place, halo, turn, kv, far, stat, part, got):
+def key_part(place, halo, turn, kv, far, stat, part, got, begin, heads):
     n = len(kv)
     _, r, width = kv[0].shape
     rows = n * r
-    heads = width // HEAD_DIM
+    width = heads * HEAD_DIM
     here, scalars = pl.BlockSpec(memory_space=pltpu.VMEM), pl.BlockSpec(memory_space=pltpu.SMEM)
     scratch = [
         pltpu.VMEM((rows, HEAD_DIM), jnp.bfloat16),
@@ -413,7 +448,7 @@
         pltpu.VMEM((HALF, HALF), jnp.bfloat16),
     ]
     return pl.pallas_call(
-        lambda *refs: key_kernel(n, *refs),
+        lambda *refs: key_kernel(n, begin, *refs),
         in_specs=[scalars] * 3 + [here] * (n + 4),
         out_specs=[here] * n,
         scratch_shapes=[pltpu.VMEM((min(KGROUP, heads), *x.shape), x.dtype) for x in scratch],
@@ -483,8 +518,13 @@
     dq, stat, part, give = query_part(place, halo, turn, kv, qd, kv_far, kv_near)
     stat_far = swapped(stat[:, :, :HALF], 1, True)
     got = swapped(give, 0)
-    dkv = key_part(place, key_halo, turn, kv, qd_far, stat_far, part, got)
-    return *merged(exchanged(dq), HINT), *merged(exchanged(dkv))
+    heads = stat.shape[0]
+    batch = max(1, heads // 2)
+    dkv = [
+        key_part(place, key_halo, turn, kv, qd_far, stat_far, part, got, begin, batch)
+        for begin in range(0, heads, batch)
+    ]
+    return *merged(exchanged(dq), HINT), *merged_pair([exchanged(pieces) for pieces in dkv])
 
 
 def solution(mesh):

time: 66.4 us -> 65.7 us (0.989)
  waiting for transfers between devices: 22.7 us -> 17.7 us
  starting transfers between devices: 24.2 us -> 27.7 us
  Pallas kernels: 14.2 us -> 15 us
    ppermute x12 -> x15, waiting for transfers between devices: 21.6 us -> 16.5 us  [exchanged(): lax.ppermute(pieces[k], 'head', [(i, i ^ k) for i in range(n)])]
    ppermute x12 -> x15, starting transfers between devices: 18.4 us -> 21.9 us  [exchanged(): lax.ppermute(pieces[k], 'head', [(i, i ^ k) for i in range(n)])]
    pallas_call x1 -> x3, Pallas kernels: 2.86 us -> 4.63 us  [the longest x2 3.55 us: key_part(): pl.pallas_call(lambda *refs: key_kernel(n, begin, *refs), in_specs=[scala...]
    pallas_call x2 -> x1, Pallas kernels: 1.84 us -> 0.82 us  [merged(): pl.pallas_call(lambda *refs: merge_kernel(n, *refs), in_specs=[pl.BlockSp...]
  transfers between devices with their start and end apart: 19 -> 22, of which waited for: 7 -> 8; matrix products, arithmetic and copies ran while one was open for 0% -> 0% of each run, Pallas kernels for 20% -> 21%
where the time goes in v8:
time: 65.7 us; the launch traced here: 65.4 us
  starting transfers between devices  27.7 us (42%)
  waiting for transfers between devices  17.7 us (27%)
  Pallas kernels  15 us (23%)
  local copies, waits for them, and re-layouts  4.16 us (6%)
  between operations  0.75 us (1%)
    ppermute x15, starting transfers between devices, exchanged(): lax.ppermute(pieces[k], 'head', [(i, i ^ k) for i in range(n)])  21.9 us
    ppermute x15, waiting for transfers between devices, exchanged(): lax.ppermute(pieces[k], 'head', [(i, i ^ k) for i in range(n)])  16.5 us
    pallas_call x1, Pallas kernels, query_part(): pl.pallas_call(lambda *refs: query_kernel(n, len(far), *refs), in_specs=[...  8.86 us
    ppermute x7, starting transfers between devices, swapped(): return lax.ppermute(array, ('head', 'blk'), pairs)  5.77 us
    unnamed x8, local copies, waits for them, and re-layouts  4.16 us
    pallas_call x2, Pallas kernels, key_part(): pl.pallas_call(lambda *refs: key_kernel(n, begin, *refs), in_specs=[scala...  3.55 us
  transfers between devices with their start and end apart: 22, of which 8 were waited for; matrix products, arithmetic and copies ran while one was open for 0% of the time, Pallas kernels for 21%

profile of v8, /device:TPU:0, one launch (start us, length us, event | category | flops | bytes accessed | tf_op | source)
XLA Modules:
  0.0 65.4 jit_solution(6195493006532260462)
XLA Ops:
  0.6 0.0 copy-start
  0.6 1.0 %copy-done = bf16[128,2048]{1,0:T(8,128)(2,1)S(1)} copy-done((bf16[128,2048]{1,0:T(8,128)(2,1)S(1)}, bf16[128,2048]{1,0:T(8,128)(2,1)}, u32[]{:S(2)}) %copy-start) | copy-done | bytes 524312
  1.7 0.0 copy-start.1
  1.7 1.0 %copy-done.1 = bf16[128,2048]{1,0:T(8,128)(2,1)S(1)} copy-done((bf16[128,2048]{1,0:T(8,128)(2,1)S(1)}, bf16[128,2048]{1,0:T(8,128)(2,1)}, u32[]{:S(2)}) %copy-start.1) | copy-done | bytes 524312
  2.7 0.2 pack.2
  3.0 3.0 %collective-permute-start = (bf16[2,128,512]{2,1,0:T(8,128)(2,1)S(1)}, bf16[2,128,512]{2,1,0:T(8,128)(2,1)S(1)}, u32[]{:S(2)}, u32[]{:S(2)}) collective-permute-start(bf16[2,128,512]{2,1,0:T(8,128)(2,1)S(1)} %get-tuple-element.29), channel_id=1, source_target_pairs={{0,8},{8,0},{16,24},{24,16},{1,9},{9,1},{17,25},{25,17},{2,10},{10... | collective-permute-start | bytes 786440 | tf_op jit(solution)/shard_map/ppermute | solution.py:482
  6.0 1.5 %collective-permute-start.1 = (bf16[2,128,512]{2,1,0:T(8,128)(2,1)S(1)}, bf16[2,128,512]{2,1,0:T(8,128)(2,1)S(1)}, u32[]{:S(2)}, u32[]{:S(2)}) collective-permute-start(bf16[2,128,512]{2,1,0:T(8,128)(2,1)S(1)} %get-tuple-element.30), channel_id=1, source_target_pairs={{0,16},{8,24},{16,0},{24,8},{1,17},{9,25},{17,1},{25,9},{2,18},{10... | collective-permute-start | bytes 786440 | tf_op jit(solution)/shard_map/ppermute | solution.py:482
  7.5 0.0 copy-start.2
  7.5 1.0 %copy-done.2 = bf16[128,2048]{1,0:T(8,128)(2,1)S(1)} copy-done((bf16[128,2048]{1,0:T(8,128)(2,1)S(1)}, bf16[128,2048]{1,0:T(8,128)(2,1)}, u32[]{:S(2)}) %copy-start.2) | copy-done | bytes 524312
  8.5 0.0 copy-start.3
  8.5 1.0 %copy-done.3 = bf16[128,2048]{1,0:T(8,128)(2,1)S(1)} copy-done((bf16[128,2048]{1,0:T(8,128)(2,1)S(1)}, bf16[128,2048]{1,0:T(8,128)(2,1)}, u32[]{:S(2)}) %copy-start.3) | copy-done | bytes 524312
  9.6 0.2 pack.3
  9.8 0.6 collective-permute-start.3
  10.4 1.4 %collective-permute-start.2 = (bf16[2,128,512]{2,1,0:T(8,128)(2,1)S(1)}, bf16[2,128,512]{2,1,0:T(8,128)(2,1)S(1)}, u32[]{:S(2)}, u32[]{:S(2)}) collective-permute-start(bf16[2,128,512]{2,1,0:T(8,128)(2,1)S(1)} %get-tuple-element.31), channel_id=1, source_target_pairs={{0,24},{8,16},{16,8},{24,0},{1,25},{9,17},{17,9},{25,1},{2,26},{10... | collective-permute-start | bytes 786440 | tf_op jit(solution)/shard_map/ppermute | solution.py:482
  11.8 1.5 %collective-permute-start.4 = (bf16[2,128,512]{2,1,0:T(8,128)(2,1)S(1)}, bf16[2,128,512]{2,1,0:T(8,128)(2,1)S(1)}, u32[]{:S(2)}, u32[]{:S(2)}) collective-permute-start(bf16[2,128,512]{2,1,0:T(8,128)(2,1)S(1)} %get-tuple-element.34), channel_id=1, source_target_pairs={{0,16},{8,24},{16,0},{24,8},{1,17},{9,25},{17,1},{25,9},{2,18},{10... | collective-permute-start | bytes 786440 | tf_op jit(solution)/shard_map/ppermute | solution.py:482
  13.4 0.0 collective-permute-done.refs_1_.refs_4_
  13.4 2.7 %collective-permute-start.5 = (bf16[2,128,512]{2,1,0:T(8,128)(2,1)S(1)}, bf16[2,128,512]{2,1,0:T(8,128)(2,1)S(1)}, u32[]{:S(2)}, u32[]{:S(2)}) collective-permute-start(bf16[2,128,512]{2,1,0:T(8,128)(2,1)S(1)} %get-tuple-element.35), channel_id=1, source_target_pairs={{0,24},{8,16},{16,8},{24,0},{1,25},{9,17},{17,9},{25,1},{2,26},{10... | collective-permute-start | bytes 786440 | tf_op jit(solution)/shard_map/ppermute | solution.py:482
  16.1 0.1 pad_add_fusion.refs_2_
  16.2 0.0 collective-permute-done.1.refs_2_.refs_5_
  16.2 0.1 stack.20
  16.3 0.7 %collective-permute-start.6 = (bf16[3,2,128,512]{3,2,1,0:T(8,128)(2,1)S(1)}, bf16[3,2,128,512]{3,2,1,0:T(8,128)(2,1)S(1)}, u32[]{:S(2)}, u32[]{:S(2)}) collective-permute-start(bf16[3,2,128,512]{3,2,1,0:T(8,128)(2,1)S(1)} %stack.20), channel_id=1, source_target_pairs={{1,2},{2,1},{3,4},{4,3},{5,6},{6,5},{9,10},{10,9},{11,12},{12,11},... | collective-permute-start | bytes 2359304 | tf_op jit(solution)/shard_map/ppermute | solution.py:476
  17.0 2.1 %collective-permute-done.3.refs_1_ = bf16[2,128,512]{2,1,0:T(8,128)(2,1)S(1)} collective-permute-done((bf16[2,128,512]{2,1,0:T(8,128)(2,1)S(1)}, bf16[2,128,512]{2,1,0:T(8,128)(2,1)S(1)}, u32[]{:S(2)}, u32[]{:S(2)}) %collective-permute-start.3) | collective-permute-done | bytes 262176 | tf_op jit(solution)/shard_map/ppermute | solution.py:482
  19.1 0.9 %collective-permute-start.8 = (bf16[3,2,128,512]{3,2,1,0:T(8,128)(2,1)S(1)}, bf16[3,2,128,512]{3,2,1,0:T(8,128)(2,1)S(1)}, u32[]{:S(2)}, u32[]{:S(2)}) collective-permute-start(bf16[3,2,128,512]{3,2,1,0:T(8,128)(2,1)S(1)} %stack.20), channel_id=1, source_target_pairs={{0,1},{1,0},{2,3},{3,2},{4,5},{5,4},{6,7},{7,6},{8,9},{9,8},{10,11... | collective-permute-start | bytes 2359304 | tf_op jit(solution)/shard_map/ppermute | solution.py:476
  20.0 6.0 %collective-permute-done.2.refs_6_ = bf16[2,128,512]{2,1,0:T(8,128)(2,1)S(1)} collective-permute-done((bf16[2,128,512]{2,1,0:T(8,128)(2,1)S(1)}, bf16[2,128,512]{2,1,0:T(8,128)(2,1)S(1)}, u32[]{:S(2)}, u32[]{:S(2)}) %collective-permute-start.2) | collective-permute-done | bytes 262176 | tf_op jit(solution)/shard_map/ppermute | solution.py:482
  26.0 1.4 %collective-permute-start.7 = (bf16[1,2,128,512]{3,2,1,0:T(8,128)(2,1)S(1)}, bf16[1,2,128,512]{3,2,1,0:T(8,128)(2,1)S(1)}, u32[]{:S(2)}, u32[]{:S(2)}) collective-permute-start(bf16[1,2,128,512]{3,2,1,0:T(8,128)(2,1)S(1)} %bitcast.3), channel_id=1, source_target_pairs={{0,8},{1,2},{2,1},{3,4},{4,3},{5,6},{6,5},{7,15},{8,0},{9,10},{10,... | collective-permute-start | bytes 786440 | tf_op jit(solution)/shard_map/ppermute | solution.py:476
  27.3 3.2 %collective-permute-done.4.refs_2_ = bf16[2,128,512]{2,1,0:T(8,128)(2,1)S(1)} collective-permute-done((bf16[2,128,512]{2,1,0:T(8,128)(2,1)S(1)}, bf16[2,128,512]{2,1,0:T(8,128)(2,1)S(1)}, u32[]{:S(2)}, u32[]{:S(2)}) %collective-permute-start.4) | collective-permute-done | bytes 262176 | tf_op jit(solution)/shard_map/ppermute | solution.py:482
  30.6 0.0 collective-permute-start.9
  30.6 0.0 collective-permute-done.5.refs_3_
  30.6 0.1 stack.19.refs_7_
  30.7 1.3 %collective-permute-start.13 = (bf16[4,2,128,512]{3,2,1,0:T(8,128)(2,1)S(1)}, bf16[4,2,128,512]{3,2,1,0:T(8,128)(2,1)S(1)}, u32[]{:S(2)}, u32[]{:S(2)}) collective-permute-start(bf16[4,2,128,512]{3,2,1,0:T(8,128)(2,1)S(1)} %stack.19.refs_7_), channel_id=1, source_target_pairs={{0,8},{1,2},{2,1},{3,4},{4,3},{5,6},{6,5},{7,15},{8,0},{9,10},{10,... | collective-permute-start | bytes 3145736 | tf_op jit(solution)/shard_map/ppermute | solution.py:476
  32.0 0.3 collective-permute-done.7.refs_9_
  32.3 0.0 collective-permute-done.9.refs_11_
  32.3 0.0 collective-permute-done.6.refs_8_
  32.3 0.0 collective-permute-done.8.refs_10_
  32.3 8.9 %query_part.1 = (bf16[128,512]{1,0:T(8,128)(2,1)S(1)}, bf16[128,512]{1,0:T(8,128)(2,1)S(1)}, bf16[128,512]{1,0:T(8,128)(2,1)S(1)}, bf16[128,512]{1,0:T(8,128)(2,...) custom-call(s32[4]{0:T(128)S(1)} %xor_xor_fusion.refs_0_.refs_1_, ...), custom_call_target="tpu_custom_call" | custom-call | flops 3355443200 | bytes 3145728 | tf_op jit(solution)/shard_map/query_part/pallas_call | solution.py:359
  41.2 0.2 collective-permute-start.15
  41.4 1.3 %collective-permute-start.14 = (f32[4,2,512]{2,1,0:T(2,128)S(1)}, f32[4,2,512]{2,1,0:T(2,128)S(1)}, u32[]{:S(2)}, u32[]{:S(2)}) collective-permute-start(f32[4,2,512]{2,1,0:T(2,128)S(1)} %get-tuple-element.40), channel_id=1, source_target_pairs={{0,8},{1,2},{2,1},{3,4},{4,3},{5,6},{6,5},{7,15},{8,0},{9,10},{10,... | collective-permute-start | bytes 49160 | tf_op jit(solution)/shard_map/ppermute | solution.py:476
  42.7 0.7 %collective-permute-start.10 = (bf16[128,512]{1,0:T(8,128)(2,1)S(1)}, bf16[128,512]{1,0:T(8,128)(2,1)S(1)}, u32[]{:S(2)}, u32[]{:S(2)}) collective-permute-start(bf16[128,512]{1,0:T(8,128)(2,1)S(1)} %get-tuple-element.37), channel_id=1, source_target_pairs={{0,8},{8,0},{16,24},{24,16},{1,9},{9,1},{17,25},{25,17},{2,10},{10... | collective-permute-start | bytes 393224 | tf_op jit(solution)/shard_map/ppermute | solution.py:482
  43.4 1.5 %collective-permute-start.11 = (bf16[128,512]{1,0:T(8,128)(2,1)S(1)}, bf16[128,512]{1,0:T(8,128)(2,1)S(1)}, u32[]{:S(2)}, u32[]{:S(2)}) collective-permute-start(bf16[128,512]{1,0:T(8,128)(2,1)S(1)} %get-tuple-element.38), channel_id=1, source_target_pairs={{0,16},{8,24},{16,0},{24,8},{1,17},{9,25},{17,1},{25,9},{2,18},{10... | collective-permute-start | bytes 393224 | tf_op jit(solution)/shard_map/ppermute | solution.py:482
  45.0 0.8 %collective-permute-done.14.refs_8_ = f32[4,2,512]{2,1,0:T(2,128)S(1)} collective-permute-done((f32[4,2,512]{2,1,0:T(2,128)S(1)}, f32[4,2,512]{2,1,0:T(2,128)S(1)}, u32[]{:S(2)}, u32[]{:S(2)}) %collective-permute-start.14) | collective-permute-done | bytes 16416 | tf_op jit(solution)/shard_map/ppermute | solution.py:476
  45.8 1.8 %collective-permute-start.12 = (bf16[128,512]{1,0:T(8,128)(2,1)S(1)}, bf16[128,512]{1,0:T(8,128)(2,1)S(1)}, u32[]{:S(2)}, u32[]{:S(2)}) collective-permute-start(bf16[128,512]{1,0:T(8,128)(2,1)S(1)} %get-tuple-element.39), channel_id=1, source_target_pairs={{0,24},{8,16},{16,8},{24,0},{1,25},{9,17},{17,9},{25,1},{2,26},{10... | collective-permute-start | bytes 393224 | tf_op jit(solution)/shard_map/ppermute | solution.py:482
  47.6 0.0 collective-permute-done.13.refs_7_
  47.6 0.0 collective-permute-done.15.refs_10_
  47.6 1.8 %key_part.3 = (bf16[2,128,256]{2,1,0:T(8,128)(2,1)S(1)}, bf16[2,128,256]{2,1,0:T(8,128)(2,1)S(1)}, bf16[2,128,256]{2,1,0:T(8,128)(2,1)S(1)}, bf16[2,128,256]{2,1,0:T(8,128)(2,1)S(1)}) custom-call(s32[4]{0:T(128)S(1)} %xor_xor_fusion.refs_0_.refs_1_, s32[4]{0:T(128)S(1)} %xor_xor_fusion.refs_0_.refs_1_, s32[2]{0:T(128)S(1)} %pad_add_fusion.refs_2_, ...), custom_call_target="tpu_custom_call" | custom-call | flops 30000001024 | bytes 3145728 | tf_op jit(solution)/shard_map/key_part/pallas_call | solution.py:450
  49.3 1.2 %collective-permute-start.19 = (bf16[2,128,256]{2,1,0:T(8,128)(2,1)S(1)}, bf16[2,128,256]{2,1,0:T(8,128)(2,1)S(1)}, u32[]{:S(2)}, u32[]{:S(2)}) collective-permute-start(bf16[2,128,256]{2,1,0:T(8,128)(2,1)S(1)} %get-tuple-element.48), channel_id=1, source_target_pairs={{0,8},{8,0},{16,24},{24,16},{1,9},{9,1},{17,25},{25,17},{2,10},{10... | collective-permute-start | bytes 393224 | tf_op jit(solution)/shard_map/ppermute | solution.py:482
  50.6 0.5 collective-permute-start.20
  51.1 1.8 %key_part.2 = (bf16[2,128,256]{2,1,0:T(8,128)(2,1)S(1)}, bf16[2,128,256]{2,1,0:T(8,128)(2,1)S(1)}, bf16[2,128,256]{2,1,0:T(8,128)(2,1)S(1)}, bf16[2,128,256]{2,1,0:T(8,128)(2,1)S(1)}) custom-call(s32[4]{0:T(128)S(1)} %xor_xor_fusion.refs_0_.refs_1_, s32[4]{0:T(128)S(1)} %xor_xor_fusion.refs_0_.refs_1_, s32[2]{0:T(128)S(1)} %pad_add_fusion.refs_2_, ...), custom_call_target="tpu_custom_call" | custom-call | flops 30000001024 | bytes 3145728 | tf_op jit(solution)/shard_map/key_part/pallas_call | solution.py:450
  52.9 0.0 collective-permute-done.10.refs_1_
  52.9 1.9 %collective-permute-start.21 = (bf16[2,128,256]{2,1,0:T(8,128)(2,1)S(1)}, bf16[2,128,256]{2,1,0:T(8,128)(2,1)S(1)}, u32[]{:S(2)}, u32[]{:S(2)}) collective-permute-start(bf16[2,128,256]{2,1,0:T(8,128)(2,1)S(1)} %get-tuple-element.50), channel_id=1, source_target_pairs={{0,24},{8,16},{16,8},{24,0},{1,25},{9,17},{17,9},{25,1},{2,26},{10... | collective-permute-start | bytes 393224 | tf_op jit(solution)/shard_map/ppermute | solution.py:482
  54.7 0.0 collective-permute-done.11.refs_2_
  54.8 1.2 %collective-permute-start.16 = (bf16[2,128,256]{2,1,0:T(8,128)(2,1)S(1)}, bf16[2,128,256]{2,1,0:T(8,128)(2,1)S(1)}, u32[]{:S(2)}, u32[]{:S(2)}) collective-permute-start(bf16[2,128,256]{2,1,0:T(8,128)(2,1)S(1)} %get-tuple-element.44), channel_id=1, source_target_pairs={{0,8},{8,0},{16,24},{24,16},{1,9},{9,1},{17,25},{25,17},{2,10},{10... | collective-permute-start | bytes 393224 | tf_op jit(solution)/shard_map/ppermute | solution.py:482
  55.9 0.0 collective-permute-done.12.refs_3_
  55.9 0.5 collective-permute-start.17
  56.5 0.0 collective-permute-done.19.refs_5_
  56.5 1.8 %collective-permute-start.18 = (bf16[2,128,256]{2,1,0:T(8,128)(2,1)S(1)}, bf16[2,128,256]{2,1,0:T(8,128)(2,1)S(1)}, u32[]{:S(2)}, u32[]{:S(2)}) collective-permute-start(bf16[2,128,256]{2,1,0:T(8,128)(2,1)S(1)} %get-tuple-element.46), channel_id=1, source_target_pairs={{0,24},{8,16},{16,8},{24,0},{1,25},{9,17},{17,9},{25,1},{2,26},{10... | collective-permute-start | bytes 393224 | tf_op jit(solution)/shard_map/ppermute | solution.py:482
  58.2 0.8 %merge.2 = bf16[128,2048]{1,0:T(8,128)(2,1)} custom-call(bf16[128,512]{1,0:T(8,128)(2,1)S(1)} %get-tuple-element.36.refs_0_, bf16[128,512]{1,0:T(8,128)(2,1)S(1)} %collective-permute-done.10.refs_1_, bf16[128,512]{1,0:T(8,128)(2,1)S(1)} %collective-permute-done.11.refs_2_, bf16[128,512]{1,0:T(8,128)(2,1)S(1)} %collective-permute-done.12.refs_3_), custom_call_target="tpu_custom_call" | custom-call | flops 30000001024 | tf_op jit(solution)/shard_map/merge/pallas_call | solution.py:117
  59.1 0.0 collective-permute-done.20.refs_6_
  59.1 1.3 %collective-permute-done.21.refs_7_ = bf16[2,128,256]{2,1,0:T(8,128)(2,1)S(1)} collective-permute-done((bf16[2,128,256]{2,1,0:T(8,128)(2,1)S(1)}, bf16[2,128,256]{2,1,0:T(8,128)(2,1)S(1)}, u32[]{:S(2)}, u32[]{:S(2)}) %collective-permute-start.21) | collective-permute-done | bytes 131104 | tf_op jit(solution)/shard_map/ppermute | solution.py:482
  60.4 2.4 %collective-permute-done.16.refs_1_ = bf16[2,128,256]{2,1,0:T(8,128)(2,1)S(1)} collective-permute-done((bf16[2,128,256]{2,1,0:T(8,128)(2,1)S(1)}, bf16[2,128,256]{2,1,0:T(8,128)(2,1)S(1)}, u32[]{:S(2)}, u32[]{:S(2)}) %collective-permute-start.16) | collective-permute-done | bytes 131104 | tf_op jit(solution)/shard_map/ppermute | solution.py:482
  62.8 1.5 %collective-permute-done.17.refs_2_ = bf16[2,128,256]{2,1,0:T(8,128)(2,1)S(1)} collective-permute-done((bf16[2,128,256]{2,1,0:T(8,128)(2,1)S(1)}, bf16[2,128,256]{2,1,0:T(8,128)(2,1)S(1)}, u32[]{:S(2)}, u32[]{:S(2)}) %collective-permute-start.17) | collective-permute-done | bytes 131104 | tf_op jit(solution)/shard_map/ppermute | solution.py:482
  64.3 0.0 collective-permute-done.18.refs_3_
  64.3 1.1 %merge.3 = (bf16[128,2048]{1,0:T(8,128)(2,1)}, bf16[128,2048]{1,0:T(8,128)(2,1)}) custom-call(bf16[2,128,256]{2,1,0:T(8,128)(2,1)S(1)} %get-tuple-element.43.refs_0_, bf16[2,128,256]{2,1,0:T(8,128)(2,1)S(1)} %collective-permute-done.16.refs_1_, bf16[2,128,256]{2,1,0:T(8,128)(2,1)S(1)} %collective-permute-done.17.refs_2_, ...), custom_call_target="tpu_custom_call" | custom-call | tf_op jit(solution)/shard_map/merge/pallas_call | solution.py:152
  (1 shorter events, 0.0 us)
Async XLA Ops:
  0.6 1.0 %copy-start = (bf16[128,2048]{1,0:T(8,128)(2,1)S(1)}, bf16[128,2048]{1,0:T(8,128)(2,1)}, u32[]{:S(2)}) copy-start(bf16[128,2048]{1,0:T(8,128)(2,1)} %refs_0_.2) | copy-start | bytes 1572868
  1.7 1.0 %copy-start.1 = (bf16[128,2048]{1,0:T(8,128)(2,1)S(1)}, bf16[128,2048]{1,0:T(8,128)(2,1)}, u32[]{:S(2)}) copy-start(bf16[128,2048]{1,0:T(8,128)(2,1)} %refs_1_.2) | copy-start | bytes 1572868
  3.0 10.4 %collective-permute-start = (bf16[2,128,512]{2,1,0:T(8,128)(2,1)S(1)}, bf16[2,128,512]{2,1,0:T(8,128)(2,1)S(1)}, u32[]{:S(2)}, u32[]{:S(2)}) collective-permute-start(bf16[2,128,512]{2,1,0:T(8,128)(2,1)S(1)} %get-tuple-element.29), channel_id=1, source_target_pairs={{0,8},{8,0},{16,24},{24,16},{1,9},{9,1},{17,25},{25,17},{2,10},{10... | collective-permute-start | bytes 786440 | tf_op jit(solution)/shard_map/ppermute | solution.py:482
  6.0 10.2 %collective-permute-start.1 = (bf16[2,128,512]{2,1,0:T(8,128)(2,1)S(1)}, bf16[2,128,512]{2,1,0:T(8,128)(2,1)S(1)}, u32[]{:S(2)}, u32[]{:S(2)}) collective-permute-start(bf16[2,128,512]{2,1,0:T(8,128)(2,1)S(1)} %get-tuple-element.30), channel_id=1, source_target_pairs={{0,16},{8,24},{16,0},{24,8},{1,17},{9,25},{17,1},{25,9},{2,18},{10... | collective-permute-start | bytes 786440 | tf_op jit(solution)/shard_map/ppermute | solution.py:482
  7.5 1.0 %copy-start.2 = (bf16[128,2048]{1,0:T(8,128)(2,1)S(1)}, bf16[128,2048]{1,0:T(8,128)(2,1)}, u32[]{:S(2)}) copy-start(bf16[128,2048]{1,0:T(8,128)(2,1)} %refs_0_.3) | copy-start | bytes 1572868
  8.5 1.0 %copy-start.3 = (bf16[128,2048]{1,0:T(8,128)(2,1)S(1)}, bf16[128,2048]{1,0:T(8,128)(2,1)}, u32[]{:S(2)}) copy-start(bf16[128,2048]{1,0:T(8,128)(2,1)} %refs_1_.3) | copy-start | bytes 1572868
  9.8 9.3 %collective-permute-start.3 = (bf16[2,128,512]{2,1,0:T(8,128)(2,1)S(1)}, bf16[2,128,512]{2,1,0:T(8,128)(2,1)S(1)}, u32[]{:S(2)}, u32[]{:S(2)}) collective-permute-start(bf16[2,128,512]{2,1,0:T(8,128)(2,1)S(1)} %get-tuple-element.33), channel_id=1, source_target_pairs={{0,8},{8,0},{16,24},{24,16},{1,9},{9,1},{17,25},{25,17},{2,10},{10... | collective-permute-start | bytes 786440 | tf_op jit(solution)/shard_map/ppermute | solution.py:482
  10.4 15.5 %collective-permute-start.2 = (bf16[2,128,512]{2,1,0:T(8,128)(2,1)S(1)}, bf16[2,128,512]{2,1,0:T(8,128)(2,1)S(1)}, u32[]{:S(2)}, u32[]{:S(2)}) collective-permute-start(bf16[2,128,512]{2,1,0:T(8,128)(2,1)S(1)} %get-tuple-element.31), channel_id=1, source_target_pairs={{0,24},{8,16},{16,8},{24,0},{1,25},{9,17},{17,9},{25,1},{2,26},{10... | collective-permute-start | bytes 786440 | tf_op jit(solution)/shard_map/ppermute | solution.py:482
  11.8 18.7 %collective-permute-start.4 = (bf16[2,128,512]{2,1,0:T(8,128)(2,1)S(1)}, bf16[2,128,512]{2,1,0:T(8,128)(2,1)S(1)}, u32[]{:S(2)}, u32[]{:S(2)}) collective-permute-start(bf16[2,128,512]{2,1,0:T(8,128)(2,1)S(1)} %get-tuple-element.34), channel_id=1, source_target_pairs={{0,16},{8,24},{16,0},{24,8},{1,17},{9,25},{17,1},{25,9},{2,18},{10... | collective-permute-start | bytes 786440 | tf_op jit(solution)/shard_map/ppermute | solution.py:482
  13.4 17.2 %collective-permute-start.5 = (bf16[2,128,512]{2,1,0:T(8,128)(2,1)S(1)}, bf16[2,128,512]{2,1,0:T(8,128)(2,1)S(1)}, u32[]{:S(2)}, u32[]{:S(2)}) collective-permute-start(bf16[2,128,512]{2,1,0:T(8,128)(2,1)S(1)} %get-tuple-element.35), channel_id=1, source_target_pairs={{0,24},{8,16},{16,8},{24,0},{1,25},{9,17},{17,9},{25,1},{2,26},{10... | collective-permute-start | bytes 786440 | tf_op jit(solution)/shard_map/ppermute | solution.py:482
  16.3 16.0 %collective-permute-start.6 = (bf16[3,2,128,512]{3,2,1,0:T(8,128)(2,1)S(1)}, bf16[3,2,128,512]{3,2,1,0:T(8,128)(2,1)S(1)}, u32[]{:S(2)}, u32[]{:S(2)}) collective-permute-start(bf16[3,2,128,512]{3,2,1,0:T(8,128)(2,1)S(1)} %stack.20), channel_id=1, source_target_pairs={{1,2},{2,1},{3,4},{4,3},{5,6},{6,5},{9,10},{10,9},{11,12},{12,11},... | collective-permute-start | bytes 2359304 | tf_op jit(solution)/shard_map/ppermute | solution.py:476
  19.1 13.2 %collective-permute-start.8 = (bf16[3,2,128,512]{3,2,1,0:T(8,128)(2,1)S(1)}, bf16[3,2,128,512]{3,2,1,0:T(8,128)(2,1)S(1)}, u32[]{:S(2)}, u32[]{:S(2)}) collective-permute-start(bf16[3,2,128,512]{3,2,1,0:T(8,128)(2,1)S(1)} %stack.20), channel_id=1, source_target_pairs={{0,1},{1,0},{2,3},{3,2},{4,5},{5,4},{6,7},{7,6},{8,9},{9,8},{10,11... | collective-permute-start | bytes 2359304 | tf_op jit(solution)/shard_map/ppermute | solution.py:476
  26.0 6.4 %collective-permute-start.7 = (bf16[1,2,128,512]{3,2,1,0:T(8,128)(2,1)S(1)}, bf16[1,2,128,512]{3,2,1,0:T(8,128)(2,1)S(1)}, u32[]{:S(2)}, u32[]{:S(2)}) collective-permute-start(bf16[1,2,128,512]{3,2,1,0:T(8,128)(2,1)S(1)} %bitcast.3), channel_id=1, source_target_pairs={{0,8},{1,2},{2,1},{3,4},{4,3},{5,6},{6,5},{7,15},{8,0},{9,10},{10,... | collective-permute-start | bytes 786440 | tf_op jit(solution)/shard_map/ppermute | solution.py:476
  30.6 1.8 %collective-permute-start.9 = (bf16[1,2,128,512]{3,2,1,0:T(8,128)(2,1)S(1)}, bf16[1,2,128,512]{3,2,1,0:T(8,128)(2,1)S(1)}, u32[]{:S(2)}, u32[]{:S(2)}) collective-permute-start(bf16[1,2,128,512]{3,2,1,0:T(8,128)(2,1)S(1)} %bitcast.4), channel_id=1, source_target_pairs={{0,1},{1,0},{2,3},{3,2},{4,5},{5,4},{6,7},{7,6},{8,9},{9,8},{10,11... | collective-permute-start | bytes 786440 | tf_op jit(solution)/shard_map/ppermute | solution.py:476
  30.7 16.8 %collective-permute-start.13 = (bf16[4,2,128,512]{3,2,1,0:T(8,128)(2,1)S(1)}, bf16[4,2,128,512]{3,2,1,0:T(8,128)(2,1)S(1)}, u32[]{:S(2)}, u32[]{:S(2)}) collective-permute-start(bf16[4,2,128,512]{3,2,1,0:T(8,128)(2,1)S(1)} %stack.19.refs_7_), channel_id=1, source_target_pairs={{0,8},{1,2},{2,1},{3,4},{4,3},{5,6},{6,5},{7,15},{8,0},{9,10},{10,... | collective-permute-start | bytes 3145736 | tf_op jit(solution)/shard_map/ppermute | solution.py:476
  41.2 6.4 %collective-permute-start.15 = (bf16[2,512,512]{2,1,0:T(8,128)(2,1)S(1)}, bf16[2,512,512]{2,1,0:T(8,128)(2,1)S(1)}, u32[]{:S(2)}, u32[]{:S(2)}) collective-permute-start(bf16[2,512,512]{2,1,0:T(8,128)(2,1)S(1)} %get-tuple-element.42), channel_id=1, source_target_pairs={{0,1},{1,0},{2,3},{3,2},{4,5},{5,4},{6,7},{7,6},{8,9},{9,8},{10,11... | collective-permute-start | bytes 3145736 | tf_op jit(solution)/shard_map/ppermute | solution.py:476
  41.4 4.3 %collective-permute-start.14 = (f32[4,2,512]{2,1,0:T(2,128)S(1)}, f32[4,2,512]{2,1,0:T(2,128)S(1)}, u32[]{:S(2)}, u32[]{:S(2)}) collective-permute-start(f32[4,2,512]{2,1,0:T(2,128)S(1)} %get-tuple-element.40), channel_id=1, source_target_pairs={{0,8},{1,2},{2,1},{3,4},{4,3},{5,6},{6,5},{7,15},{8,0},{9,10},{10,... | collective-permute-start | bytes 49160 | tf_op jit(solution)/shard_map/ppermute | solution.py:476
  42.7 10.2 %collective-permute-start.10 = (bf16[128,512]{1,0:T(8,128)(2,1)S(1)}, bf16[128,512]{1,0:T(8,128)(2,1)S(1)}, u32[]{:S(2)}, u32[]{:S(2)}) collective-permute-start(bf16[128,512]{1,0:T(8,128)(2,1)S(1)} %get-tuple-element.37), channel_id=1, source_target_pairs={{0,8},{8,0},{16,24},{24,16},{1,9},{9,1},{17,25},{25,17},{2,10},{10... | collective-permute-start | bytes 393224 | tf_op jit(solution)/shard_map/ppermute | solution.py:482
  43.4 11.3 %collective-permute-start.11 = (bf16[128,512]{1,0:T(8,128)(2,1)S(1)}, bf16[128,512]{1,0:T(8,128)(2,1)S(1)}, u32[]{:S(2)}, u32[]{:S(2)}) collective-permute-start(bf16[128,512]{1,0:T(8,128)(2,1)S(1)} %get-tuple-element.38), channel_id=1, source_target_pairs={{0,16},{8,24},{16,0},{24,8},{1,17},{9,25},{17,1},{25,9},{2,18},{10... | collective-permute-start | bytes 393224 | tf_op jit(solution)/shard_map/ppermute | solution.py:482
  45.8 10.2 %collective-permute-start.12 = (bf16[128,512]{1,0:T(8,128)(2,1)S(1)}, bf16[128,512]{1,0:T(8,128)(2,1)S(1)}, u32[]{:S(2)}, u32[]{:S(2)}) collective-permute-start(bf16[128,512]{1,0:T(8,128)(2,1)S(1)} %get-tuple-element.39), channel_id=1, source_target_pairs={{0,24},{8,16},{16,8},{24,0},{1,25},{9,17},{17,9},{25,1},{2,26},{10... | collective-permute-start | bytes 393224 | tf_op jit(solution)/shard_map/ppermute | solution.py:482
  49.3 7.1 %collective-permute-start.19 = (bf16[2,128,256]{2,1,0:T(8,128)(2,1)S(1)}, bf16[2,128,256]{2,1,0:T(8,128)(2,1)S(1)}, u32[]{:S(2)}, u32[]{:S(2)}) collective-permute-start(bf16[2,128,256]{2,1,0:T(8,128)(2,1)S(1)} %get-tuple-element.48), channel_id=1, source_target_pairs={{0,8},{8,0},{16,24},{24,16},{1,9},{9,1},{17,25},{25,17},{2,10},{10... | collective-permute-start | bytes 393224 | tf_op jit(solution)/shard_map/ppermute | solution.py:482
  50.6 8.5 %collective-permute-start.20 = (bf16[2,128,256]{2,1,0:T(8,128)(2,1)S(1)}, bf16[2,128,256]{2,1,0:T(8,128)(2,1)S(1)}, u32[]{:S(2)}, u32[]{:S(2)}) collective-permute-start(bf16[2,128,256]{2,1,0:T(8,128)(2,1)S(1)} %get-tuple-element.49), channel_id=1, source_target_pairs={{0,16},{8,24},{16,0},{24,8},{1,17},{9,25},{17,1},{25,9},{2,18},{10... | collective-permute-start | bytes 393224 | tf_op jit(solution)/shard_map/ppermute | solution.py:482
  52.9 7.5 %collective-permute-start.21 = (bf16[2,128,256]{2,1,0:T(8,128)(2,1)S(1)}, bf16[2,128,256]{2,1,0:T(8,128)(2,1)S(1)}, u32[]{:S(2)}, u32[]{:S(2)}) collective-permute-start(bf16[2,128,256]{2,1,0:T(8,128)(2,1)S(1)} %get-tuple-element.50), channel_id=1, source_target_pairs={{0,24},{8,16},{16,8},{24,0},{1,25},{9,17},{17,9},{25,1},{2,26},{10... | collective-permute-start | bytes 393224 | tf_op jit(solution)/shard_map/ppermute | solution.py:482
  54.8 8.0 %collective-permute-start.16 = (bf16[2,128,256]{2,1,0:T(8,128)(2,1)S(1)}, bf16[2,128,256]{2,1,0:T(8,128)(2,1)S(1)}, u32[]{:S(2)}, u32[]{:S(2)}) collective-permute-start(bf16[2,128,256]{2,1,0:T(8,128)(2,1)S(1)} %get-tuple-element.44), channel_id=1, source_target_pairs={{0,8},{8,0},{16,24},{24,16},{1,9},{9,1},{17,25},{25,17},{2,10},{10... | collective-permute-start | bytes 393224 | tf_op jit(solution)/shard_map/ppermute | solution.py:482
  55.9 8.3 %collective-permute-start.17 = (bf16[2,128,256]{2,1,0:T(8,128)(2,1)S(1)}, bf16[2,128,256]{2,1,0:T(8,128)(2,1)S(1)}, u32[]{:S(2)}, u32[]{:S(2)}) collective-permute-start(bf16[2,128,256]{2,1,0:T(8,128)(2,1)S(1)} %get-tuple-element.45), channel_id=1, source_target_pairs={{0,16},{8,24},{16,0},{24,8},{1,17},{9,25},{17,1},{25,9},{2,18},{10... | collective-permute-start | bytes 393224 | tf_op jit(solution)/shard_map/ppermute | solution.py:482
  56.5 7.8 %collective-permute-start.18 = (bf16[2,128,256]{2,1,0:T(8,128)(2,1)S(1)}, bf16[2,128,256]{2,1,0:T(8,128)(2,1)S(1)}, u32[]{:S(2)}, u32[]{:S(2)}) collective-permute-start(bf16[2,128,256]{2,1,0:T(8,128)(2,1)S(1)} %get-tuple-element.46), channel_id=1, source_target_pairs={{0,24},{8,16},{16,8},{24,0},{1,25},{9,17},{17,9},{25,1},{2,26},{10... | collective-permute-start | bytes 393224 | tf_op jit(solution)/shard_map/ppermute | solution.py:482
